TPU v7x, 256 devices: a whole 4x4x8 slice. The times are simulated.
256 devices in a mesh: prow: 8 (over z), pcol: 8 (over y_hi, x), orb: 4 (over y_lo, core).
Axes of the slice: x: 4, y: 4 (y_hi: 2, y_lo: 2; y = y_hi * 2 + y_lo), z: 8, core: 2. Of those that a mesh axis runs over, the one named last changes fastest.
Arguments:
- panel_orbitals: bfloat16 [20000, 512], P('orb', ('prow', 'pcol')), may hold values from -8 to 8
- orbitals: bfloat16 [20000, 65536], P('orb', ('prow', 'pcol')), may hold values from -6 to 6
Outputs:
- coupling: float32 [512, 65536], P(None, ('prow', 'pcol', 'orb'))
All inputs are finite; a program needn't handle non-finite values.
Results may differ from a plain program's by a relative error of at most 0.00035.
Values may be sent and summed in bfloat16 or wider, within the bound.
No kernel may reach another device: no remote copies, remote signals or barrier semaphores. Data moves between devices by JAX's collectives and lax.ppermute only.
A program may use at most 128 MiB of HBM per device.

v0:
```python
import jax
import jax.numpy as jnp
from jax import lax
from jax.sharding import PartitionSpec as P


def on_device(panel_orbitals, orbitals):
    contract = (((0,), (0,)), ((), ()))
    panel_full = lax.all_gather(panel_orbitals, ("prow", "pcol"), axis=1, tiled=True)
    panel_gram = lax.dot_general(
        panel_full, panel_full, contract, preferred_element_type=jnp.float32
    )
    panel_gram = lax.psum(panel_gram, "orb")
    pair_panel = panel_gram * panel_gram
    factor = jnp.linalg.cholesky(pair_panel)
    share_cols = orbitals.shape[1] // lax.axis_size("orb")
    partial_rows = lax.dot_general(
        orbitals, panel_full, contract, preferred_element_type=jnp.float32
    )
    summed_rows = lax.psum(partial_rows, "orb")
    gram_rows = lax.dynamic_slice_in_dim(
        summed_rows, lax.axis_index("orb") * share_cols, share_cols, 0
    )
    pair_rows = gram_rows * gram_rows
    return jax.scipy.linalg.solve_triangular(factor, pair_rows.T, lower=True)


def solution(mesh):
    return jax.shard_map(
        on_device,
        mesh=mesh,
        in_specs=(P("orb", ("prow", "pcol")), P("orb", ("prow", "pcol"))),
        out_specs=P(None, ("prow", "pcol", "orb")),
        check_vma=False,
    )
```

profile of v0, /device:TPU:1, one launch (start us, length us, event | category | flops | bytes accessed | tf_op | source)
XLA Modules:
  0.0 386.6 jit_solution(18246137927982304088)
XLA Ops:
  6.5 0.0 all-gather.2.cloned.1.call-start
  6.5 0.7 all-gather.2.cloned.1.call-update
  7.3 0.0 all-reduce.4.cloned.1.call-start
  7.3 136.0 %all-gather.2.cloned.1.call-done = bf16[5000,512]{0,1:T(8,128)(2,1)} async-done(((bf16[5000,8]{0,1:T(8,128)(2,1)}), bf16[5000,512]{0,1:T(8,128)(2,1)}) %all-gather.2.cloned.1.call-update) | async-done | bytes 5120016 | tf_op jit(solution)/shard_map/all_gather | solution.py:9
  143.3 0.0 copy-start.1
  143.3 8.1 %fusion.31 = f32[512,512]{0,1:T(8,128)} fusion(bf16[5000,512]{0,1:T(8,128)(2,1)} %all-gather.2.cloned.1.call-done), kind=kOutput, calls=%fused_computation.68 | convolution fusion | flops 2621440000 | bytes 6168576 | tf_op jit(solution)/shard_map/dot_general | solution.py:10
  151.4 0.0 copy-done.1
  151.4 9.7 %fusion.32 = f32[1024,512]{1,0:T(8,128)} fusion(bf16[5000,1024]{1,0:T(8,128)(2,1)} %param.3, bf16[5000,512]{0,1:T(8,128)(2,1)S(1)} %copy-done.1), kind=kOutput, calls=%fused_computation.69 | convolution fusion | flops 5242880000 | bytes 17457152 | tf_op jit(solution)/shard_map/dot_general | solution.py:17
  161.2 0.0 all-reduce.4.cloned.1.call-update
  161.2 80.4 %all-reduce.4.cloned.1.call-done = (f32[1024,512]{1,0:T(8,128)}, f32[512,512]{0,1:T(8,128)}) async-done(((f32[1024,512]{1,0:T(8,128)}, f32[512,512]{0,1:T(8,128)}), (f32[1024,512]{1,0:T(8,128)}, f32[512,512]{0,1:T(8,128)})) %all-reduce.4.cloned.1.call-update) | async-done | bytes 3145744 | tf_op jit(solution)/shard_map/psum | solution.py:20
  241.7 0.0 copy-start
  241.7 1.8 mul.9
  243.5 0.3 copy.4
  243.8 0.0 copy-done
  243.8 0.2 fusion
  244.1 11.7 %cholesky.104 = f32[128,128]{1,0:T(8,128)S(1)} custom-call(f32[128,128]{1,0:T(8,128)S(1)} %cholesky.266), custom_call_target="Cholesky" | custom-call | tf_op jit(solution)/shard_map/jit(cholesky)/cholesky | solution.py:15
  255.9 9.8 %custom-call.31 = f32[1,128,128]{1,2,0:T(8,128)S(1)} custom-call(f32[1,128,128]{2,1,0:T(8,128)S(1)} %get-tuple-element.34), custom_call_target="InvertDiagBlocksLowerTriangular" | custom-call | tf_op jit(solution)/shard_map/jit(cholesky)/cholesky | solution.py:15
  265.7 0.1 cholesky.224
  265.8 0.3 constant_dynamic-update-slice_fusion.3
  266.1 0.3 convolution_subtract_fusion
  266.5 11.7 %cholesky.217 = f32[128,128]{1,0:T(8,128)S(1)} custom-call(f32[128,128]{1,0:T(8,128)S(1)} %cholesky.270), custom_call_target="Cholesky" | custom-call | tf_op jit(solution)/shard_map/jit(cholesky)/cholesky | solution.py:15
  278.2 10.0 %custom-call.32 = f32[1,128,128]{1,2,0:T(8,128)S(1)} custom-call(f32[1,128,128]{2,1,0:T(8,128)S(1)} %get-tuple-element.31), custom_call_target="InvertDiagBlocksLowerTriangular" | custom-call | tf_op jit(solution)/shard_map/jit(cholesky)/cholesky | solution.py:15
  288.2 0.3 convolution_dynamic-update-slice_fusion
  288.5 0.4 convolution_subtract_fusion.3
  288.9 11.7 %cholesky.238 = f32[128,128]{1,0:T(8,128)S(1)} custom-call(f32[128,128]{1,0:T(8,128)S(1)} %cholesky.275), custom_call_target="Cholesky" | custom-call | tf_op jit(solution)/shard_map/jit(cholesky)/cholesky | solution.py:15
  300.6 0.7 compare_reduce_fusion.1
  301.3 9.8 %custom-call.33 = f32[1,128,128]{1,2,0:T(8,128)S(1)} custom-call(f32[1,128,128]{2,1,0:T(8,128)S(1)} %get-tuple-element.28), custom_call_target="InvertDiagBlocksLowerTriangular" | custom-call | tf_op jit(solution)/shard_map/jit(cholesky)/cholesky | solution.py:15
  311.1 0.2 convolution_dynamic-update-slice_fusion.1
  311.3 0.4 convolution_subtract_fusion.5
  311.7 11.7 %cholesky.255 = f32[128,128]{1,0:T(8,128)S(1)} custom-call(f32[128,128]{1,0:T(8,128)S(1)} %convolution_subtract_fusion.5), custom_call_target="Cholesky" | custom-call | tf_op jit(solution)/shard_map/jit(cholesky)/cholesky | solution.py:15
  323.4 0.3 select_reduce_fusion
  323.7 0.7 compare_reduce_fusion
  324.4 0.6 compare_reduce_fusion.2
  327.4 0.1 select_select_fusion
  327.5 7.8 %while.1 = (s32[]{:T(128)}, f32[512,512]{1,0:T(8,128)S(1)}, s32[4,2]{0,1:T(2,128)S(1)}, f32[4,128,128]{2,1,0:T(8,128)S(1)}, s32[]{:T(128)}) while((s32[]{:T(128)}, f32[512,512]{1,0:T(8,128)S(1)}, s32[4,2]{0,1:T(2,128)S(1)}, f32[4,128,128]{2,1,0:T(8,128)S(1)}, s32[]{:T(128)}) %tuple.27), condition=%wide.while_cond, body=%wide.while_body.sunk | while | flops 2 | bytes 131181 | solution.py:25
  327.6 0.1 constant_dynamic-slice_fusion.2
  327.6 0.5 fusion.43
  328.2 1.3 bitcast_dynamic-update-slice_fusion.2
  329.5 0.1 constant_dynamic-slice_fusion.2
  329.6 0.5 fusion.43
  330.1 1.3 bitcast_dynamic-update-slice_fusion.2
  331.5 0.1 constant_dynamic-slice_fusion.2
  331.5 0.5 fusion.43
  332.1 1.3 bitcast_dynamic-update-slice_fusion.2
  333.4 0.1 constant_dynamic-slice_fusion.2
  333.5 0.5 fusion.43
  334.1 1.3 bitcast_dynamic-update-slice_fusion.2
  335.4 39.3 %custom-call.34 = f32[4,128,128]{1,2,0:T(8,128)S(1)} custom-call(f32[4,128,128]{2,1,0:T(8,128)S(1)} %get-tuple-element.12), custom_call_target="InvertDiagBlocksLowerTriangular" | custom-call | tf_op jit(solution)/shard_map/jit(_solve_triangular)/triangular_solve | solution.py:25
  374.7 1.1 multiply_bitcast_fusion
  375.8 0.3 fusion.15
  376.1 0.4 convolution_subtract_fusion.4
  376.5 0.3 fusion.22
  376.8 0.6 convolution_subtract_fusion.2
  377.4 0.3 fusion.20
  377.7 0.8 convolution_subtract_fusion.1
  378.6 0.3 fusion.19
  378.9 0.8 pad_maximum_fusion
  (9 shorter events, 0.1 us)
Async XLA Ops:
  6.5 136.8 %all-gather.2.cloned.1.call-start = ((), (), s32[]{:S(2)}) async-start(), calls=%async_computation | async-start | bytes 5324800 | tf_op jit(solution)/shard_map/all_gather | solution.py:9
  7.3 234.4 %all-reduce.4.cloned.1.call-start = ((), (), s32[]{:S(2)}) async-start(), calls=%async_computation.1 | async-start | bytes 6291456 | tf_op jit(solution)/shard_map/psum | solution.py:20
  143.3 8.1 %copy-start.1 = (bf16[5000,512]{0,1:T(8,128)(2,1)S(1)}, bf16[5000,512]{0,1:T(8,128)(2,1)}, u32[]{:S(2)}) copy-start(bf16[5000,512]{0,1:T(8,128)(2,1)} %all-gather.2.cloned.1.call-done) | copy-start | bytes 15360004
  241.7 2.2 copy-start
Sparse Core Ops, SparseCore 0:
  10.9 132.3 all-gather.1
  161.3 80.2 all-reduce.3
where the time goes:
time: 387 us
  waiting for transfers between devices  217 us (56%)
  other arithmetic  122 us (32%)
  matrix products  22.7 us (6%)
  between operations  16 us (4%)
  local copies, waits for them, and re-layouts  8.22 us (2%)
    all_gather x1, waiting for transfers between devices, on_device(): lax.all_gather(panel_orbitals, ('prow', 'pcol'), axis=1, tiled=True)  136 us
    psum x1, waiting for transfers between devices, on_device(): summed_rows = lax.psum(partial_rows, 'orb')  80.4 us
    another operation x14, other arithmetic, on_device(): factor = jnp.linalg.cholesky(pair_panel)  78.8 us
    another operation x4, other arithmetic, on_device(): return jax.scipy.linalg.solve_triangular(factor, pair_rows.T, lower=True)  40.3 us
    dot_general x1, matrix products, on_device(): lax.dot_general(orbitals, panel_full, contract, preferred_element_type=jn...  9.73 us
    dot_general x1, matrix products, on_device(): lax.dot_general(panel_full, panel_full, contract, preferred_element_type=...  8.11 us
    another operation x12, local copies, waits for them, and re-layouts  7.74 us
  transfers between devices with their start and end apart: 2, of which 2 were waited for; matrix products, arithmetic and copies ran while one was open for 0% of the time, Pallas kernels for 0%

commit v1 on v0

v1 whole, which is shorter than its diff:
```python
import jax
import jax.numpy as jnp
from jax import lax
from jax.experimental import pallas as pl
from jax.experimental.pallas import tpu as pltpu
from jax.sharding import PartitionSpec as P

F32 = jnp.float32
HI = lax.Precision.HIGHEST
ROW0 = (((0,), (0,)), ((), ()))
NB = 128

CORE_SWAP = [(0, 1), (1, 0), (2, 3), (3, 2)]
CHIP_SWAP = [(0, 2), (2, 0), (1, 3), (3, 1)]


def x_shift(k):
    return [(h * 4 + x, h * 4 + (x + k) % 4) for h in range(2) for x in range(4)]


Y_SWAP = [(c, (c + 4) % 8) for c in range(8)]


def spread(v):
    return jnp.broadcast_to(v, (8, NB))


def reciprocal(v):
    r = pl.reciprocal(v, approx=True)
    r = r * (2.0 - v * r)
    return r * (2.0 - v * r)


def inverse_factor(rows):
    rows = list(rows)
    lane = lax.broadcasted_iota(jnp.int32, (8, NB), 1)
    sub = lax.broadcasted_iota(jnp.int32, (8, NB), 0)
    at = [sub == s for s in range(8)]
    groups, out = len(rows), []
    for q in range(groups):
        b = 8 * q
        w = rows[q]
        cols = [spread(w[:, b + t : b + t + 1]) for t in range(8)]
        a = {(s, t): spread(cols[t][s : s + 1, :]) for t in range(8) for s in range(t, 8)}
        here = (lane >= b) & (lane < b + 8)
        w = jnp.where(here, jnp.where(lane - b == sub, 1.0, 0.0), w)
        below = {}
        for g in range(q + 1, groups):
            for t in range(8):
                below[g, t] = spread(rows[g][:, b + t : b + t + 1])
            rows[g] = jnp.where(here, 0.0, rows[g])
        scale = jnp.zeros((8, NB), F32)
        for t in range(8):
            d = a[t, t]
            r = reciprocal(d)
            root = lax.rsqrt(d)
            root = root * (1.5 - (0.5 * d * root) * root)
            scale = jnp.where(at[t], root, scale)
            m = {s: a[s, t] * r for s in range(t + 1, 8)}
            for u in range(t + 1, 8):
                for s in range(u, 8):
                    a[s, u] = a[s, u] - m[s] * a[u, t]
            pivot_row = spread(w[t : t + 1, :])
            if t < 7:
                m_col = jnp.zeros((8, NB), F32)
                for s in range(t + 1, 8):
                    m_col = jnp.where(at[s], m[s], m_col)
                w = w - m_col * pivot_row
            for g in range(q + 1, groups):
                mg = below[g, t] * r
                for u in range(t + 1, 8):
                    below[g, u] = below[g, u] - mg * a[u, t]
                rows[g] = rows[g] - mg * pivot_row
        out.append(jnp.where(lane <= sub + b, w * scale, 0.0))
    return out


def factor_kernel(gram_ref, inv_ref, upper_ref, pair_ref):
    pair_ref[...] = gram_ref[...] * gram_ref[...]

    def step(j, carry):
        o = pl.multiple_of(j * NB, NB)
        rows = [pair_ref[pl.ds(o + 8 * q, 8), pl.ds(o, NB)] for q in range(NB // 8)]
        inv = jnp.concatenate(inverse_factor(rows), 0)
        inv_ref[j] = inv
        upper = jnp.dot(inv, pair_ref[pl.ds(o, NB), :], precision=HI, preferred_element_type=F32)
        upper_ref[j] = upper
        pair_ref[...] -= lax.dot_general(
            upper, upper, ROW0, precision=HI, preferred_element_type=F32
        )
        return carry

    lax.fori_loop(0, gram_ref.shape[0] // NB, step, 0)


def solve_kernel(inv_ref, upper_ref, mine_ref, other_ref, out_ref):
    blocks = inv_ref.shape[0]
    solved = []
    for j in range(blocks):
        cut = slice(j * NB, (j + 1) * NB)
        gram = mine_ref[cut, :] + other_ref[cut, :]
        rest = gram * gram
        for i in range(j):
            rest -= lax.dot_general(
                upper_ref[i, :, cut], solved[i], ROW0, precision=HI, preferred_element_type=F32
            )
        x = jnp.dot(inv_ref[j], rest, precision=HI, preferred_element_type=F32)
        solved.append(x)
        out_ref[cut, :] = x


def factorise(gram):
    n = gram.shape[0]
    blocks = n // NB
    return pl.pallas_call(
        factor_kernel,
        out_shape=(
            jax.ShapeDtypeStruct((blocks, NB, NB), F32),
            jax.ShapeDtypeStruct((blocks, NB, n), F32),
        ),
        scratch_shapes=[pltpu.VMEM((n, n), F32)],
        compiler_params=pltpu.CompilerParams(vmem_limit_bytes=40 << 20),
        cost_estimate=pl.CostEstimate(flops=30_000_000_000, bytes_accessed=3 << 20, transcendentals=0),
        name="factor",
    )(gram)


def solve(inv, upper, mine, other):
    return pl.pallas_call(
        solve_kernel,
        out_shape=jax.ShapeDtypeStruct(mine.shape, F32),
        compiler_params=pltpu.CompilerParams(vmem_limit_bytes=40 << 20),
        name="solve",
    )(inv, upper, mine, other)


def gather_panel(panel):
    own = panel.T
    y_hi = lax.axis_index("pcol") // 4
    x = lax.axis_index("pcol") % 4
    far = lax.ppermute(own, "pcol", Y_SWAP)
    first = y_hi == 0
    pair = jnp.stack([jnp.where(first, own, far), jnp.where(first, far, own)])
    turn = [pair] + [lax.ppermute(pair, "pcol", x_shift(k)) for k in (1, 2, 3)]
    ring = jnp.stack(turn[::-1] + turn[::-1])
    ring = lax.dynamic_slice_in_dim(ring, 3 - x, 4, 0)
    plane = ring.transpose(1, 0, 2, 3).reshape(64, -1)
    return lax.all_gather(plane, "prow", axis=0, tiled=True)


def on_device(panel_orbitals, orbitals):
    core = lax.axis_index("orb") % 2
    chip = lax.axis_index("orb") // 2
    full = gather_panel(panel_orbitals)
    panel = lax.dot_general(full, full, (((1,), (1,)), ((), ())), preferred_element_type=F32)
    half = panel.shape[0] // 2

    def rows_of(v, which):
        return lax.dynamic_slice_in_dim(v, which * half, half, 0)

    summed = rows_of(panel, core) + lax.ppermute(rows_of(panel, 1 - core), "orb", CORE_SWAP)
    summed = summed + lax.ppermute(summed, "orb", CHIP_SWAP)
    other = lax.ppermute(summed, "orb", CORE_SWAP)
    first = core == 0
    gram = jnp.concatenate([jnp.where(first, summed, other), jnp.where(first, other, summed)], 0)
    inv, upper = factorise(gram)

    rows = lax.dot_general(full, orbitals, (((1,), (0,)), ((), ())), preferred_element_type=F32)
    quarter = rows.shape[1] // 4

    def share(v, which):
        return lax.dynamic_slice_in_dim(v, which * quarter, quarter, 1)

    give = jnp.concatenate([share(rows, 1 - core), share(rows, 3 - core)], 1)
    keep = jnp.concatenate([share(rows, core), share(rows, 2 + core)], 1)
    on_chip = keep + lax.ppermute(give, "orb", CORE_SWAP)
    mine = share(on_chip, chip)
    arrived = lax.ppermute(share(on_chip, 1 - chip), "orb", CHIP_SWAP)
    return solve(inv, upper, mine, arrived)


def solution(mesh):
    return jax.shard_map(
        on_device,
        mesh=mesh,
        in_specs=(P("orb", ("prow", "pcol")), P("orb", ("prow", "pcol"))),
        out_specs=P(None, ("prow", "pcol", "orb")),
        check_vma=False,
    )
```

time: 387 us -> 167 us (0.43)
  waiting for transfers between devices: 217 us -> 88.3 us
  other arithmetic: 122 us -> 3.62 us
  Pallas kernels: 0 us -> 30.9 us
  starting transfers between devices: 0.04 us -> 13 us
  matrix products: 22.7 us -> 15.4 us
  local copies, waits for them, and re-layouts: 8.22 us -> 2.2 us
    another operation x18 -> x3, other arithmetic: 119 us -> 0.94 us  [the longest x2 0.92 us: gather_panel(): pair = jnp.stack([jnp.where(first, own, far), jnp.where(first, far, own)])]
    psum x1 -> x0, waiting for transfers between devices: 80.4 us -> none  [on_device(): summed_rows = lax.psum(partial_rows, 'orb')]
    all_gather x1, waiting for transfers between devices: 136 us -> 68.4 us  [gather_panel(): return lax.all_gather(plane, 'prow', axis=0, tiled=True)]
    pallas_call x0 -> x2, Pallas kernels: none -> 30.9 us  [the longest x1 27.8 us: factorise(): pl.pallas_call(factor_kernel, out_shape=(jax.ShapeDtypeStruct((blocks, NB...]
    ppermute x0 -> x9, waiting for transfers between devices: none -> 19.9 us  [the longest x1 11.8 us: on_device(): summed = summed + lax.ppermute(summed, 'orb', CHIP_SWAP)]
    ppermute x0 -> x9, starting transfers between devices: none -> 13 us  [the longest x3 4.34 us: gather_panel(): turn = [pair] + [lax.ppermute(pair, 'pcol', x_shift(k)) for k in (1, 2, 3)]]
    another operation x17 -> x0, local copies, waits for them, and re-layouts: 7.88 us -> none
    another operation x13 -> x0, matrix products: 4.91 us -> none  [the longest x7 3.04 us: on_device(): return jax.scipy.linalg.solve_triangular(factor, pair_rows.T, lower=True)]
  transfers between devices with their start and end apart: 2 -> 10, of which waited for: 2 -> 6; matrix products, arithmetic and copies ran while one was open for 0% -> 7% of each run, Pallas kernels for 0% -> 17%
where the time goes in v1:
time: 167 us
  waiting for transfers between devices  88.3 us (53%)
  Pallas kernels  30.9 us (19%)
  matrix products  15.4 us (9%)
  between operations  13.6 us (8%)
  starting transfers between devices  13 us (8%)
  other arithmetic  3.62 us (2%)
  local copies, waits for them, and re-layouts  2.2 us (1%)
    all_gather x1, waiting for transfers between devices, gather_panel(): return lax.all_gather(plane, 'prow', axis=0, tiled=True)  68.4 us
    pallas_call x1, Pallas kernels, factorise(): pl.pallas_call(factor_kernel, out_shape=(jax.ShapeDtypeStruct((blocks, NB...  27.8 us
    ppermute x1, waiting for transfers between devices, on_device(): summed = summed + lax.ppermute(summed, 'orb', CHIP_SWAP)  11.8 us
    dot_general x1, matrix products, on_device(): lax.dot_general(full, orbitals, (((1,), (0,)), ((), ())), preferred_eleme...  8.41 us
    dot_general x1, matrix products, on_device(): lax.dot_general(full, full, (((1,), (1,)), ((), ())), preferred_element_t...  7.02 us
    ppermute x3, waiting for transfers between devices, gather_panel(): turn = [pair] + [lax.ppermute(pair, 'pcol', x_shift(k)) for k in (1, 2, 3)]  6.11 us
    ppermute x3, starting transfers between devices, gather_panel(): turn = [pair] + [lax.ppermute(pair, 'pcol', x_shift(k)) for k in (1, 2, 3)]  4.34 us
    ppermute x1, starting transfers between devices, gather_panel(): far = lax.ppermute(own, 'pcol', Y_SWAP)  3.74 us
  transfers between devices with their start and end apart: 10, of which 6 were waited for; matrix products, arithmetic and copies ran while one was open for 7% of the time, Pallas kernels for 17%

profile of v1, /device:TPU:1, one launch (start us, length us, event | category | flops | bytes accessed | tf_op | source)
XLA Modules:
  0.0 167.0 jit_solution(709474174882973538)
XLA Ops:
  6.5 0.0 all-gather.2.cloned.1.call-start
  6.5 3.7 %collective-permute-start = (bf16[8,5000]{1,0:T(8,128)(2,1)}, bf16[8,5000]{1,0:T(8,128)(2,1)S(1)}, u32[]{:S(2)}, u32[]{:S(2)}) collective-permute-start(bf16[8,5000]{1,0:T(8,128)(2,1)} %bitcast.36), channel_id=1, source_target_pairs={{0,16},{4,20},{8,24},{12,28},{16,0},{20,4},{24,8},{28,12},{1,17},{... | collective-permute-start | bytes 240008 | tf_op jit(solution)/shard_map/ppermute | solution.py:141
  10.3 2.0 %collective-permute-done = bf16[8,5000]{1,0:T(8,128)(2,1)S(1)} collective-permute-done((bf16[8,5000]{1,0:T(8,128)(2,1)}, bf16[8,5000]{1,0:T(8,128)(2,1)S(1)}, u32[]{:S(2)}, u32[]{:S(2)}) %collective-permute-start) | collective-permute-done | bytes 80032 | tf_op jit(solution)/shard_map/ppermute | solution.py:141
  12.3 0.9 select_bitcast_fusion.1
  13.3 2.6 %collective-permute-start.1 = (bf16[2,8,5000]{2,1,0:T(8,128)(2,1)S(1)}, bf16[2,8,5000]{2,1,0:T(8,128)(2,1)S(1)}, u32[]{:S(2)}, u32[]{:S(2)}) collective-permute-start(bf16[2,8,5000]{2,1,0:T(8,128)(2,1)S(1)} %pad_maximum_fusion.2), channel_id=1, source_target_pairs={{0,12},{4,0},{8,4},{12,8},{16,28},{20,16},{24,20},{28,24},{1,13},{... | collective-permute-start | bytes 480008 | tf_op jit(solution)/shard_map/ppermute | solution.py:144
  15.9 0.0 collective-permute-start.3
  15.9 1.7 %collective-permute-start.2 = (bf16[2,8,5000]{2,1,0:T(8,128)(2,1)S(1)}, bf16[2,8,5000]{2,1,0:T(8,128)(2,1)S(1)}, u32[]{:S(2)}, u32[]{:S(2)}) collective-permute-start(bf16[2,8,5000]{2,1,0:T(8,128)(2,1)S(1)} %pad_maximum_fusion.2), channel_id=1, source_target_pairs={{0,8},{4,12},{8,0},{12,4},{16,24},{20,28},{24,16},{28,20},{1,9},{5... | collective-permute-start | bytes 480008 | tf_op jit(solution)/shard_map/ppermute | solution.py:144
  17.6 0.5 collective-permute-done.1
  18.1 4.8 %collective-permute-done.2 = bf16[2,8,5000]{2,1,0:T(8,128)(2,1)S(1)} collective-permute-done((bf16[2,8,5000]{2,1,0:T(8,128)(2,1)S(1)}, bf16[2,8,5000]{2,1,0:T(8,128)(2,1)S(1)}, u32[]{:S(2)}, u32[]{:S(2)}) %collective-permute-start.2) | collective-permute-done | bytes 160032 | tf_op jit(solution)/shard_map/ppermute | solution.py:144
  22.9 0.8 collective-permute-done.3
  23.9 0.9 constant_dynamic-slice_fusion.7
  24.8 0.0 all-gather.2.cloned.1.call-update
  24.8 68.4 %all-gather.2.cloned.1.call-done = bf16[512,5000]{1,0:T(8,128)(2,1)} async-done(((bf16[64,5000]{1,0:T(8,128)(2,1)}), bf16[512,5000]{1,0:T(8,128)(2,1)}) %all-gather.2.cloned.1.call-update) | async-done | bytes 5120016 | tf_op jit(solution)/shard_map/all_gather | solution.py:148
  93.2 0.0 copy-start
  93.2 7.0 %fusion = f32[512,512]{1,0:T(8,128)S(1)} fusion(bf16[512,5000]{1,0:T(8,128)(2,1)} %all-gather.2.cloned.1.call-done), kind=kOutput, calls=%fused_computation.25 | convolution fusion | flops 2621440000 | bytes 6168576 | tf_op jit(solution)/shard_map/dot_general | solution.py:155
  100.2 0.8 constant_dynamic-slice_fusion.6
  101.1 0.7 collective-permute-start.4
  101.7 0.0 copy-done
  101.8 8.4 %fusion.1 = f32[512,1024]{1,0:T(8,128)S(1)} fusion(bf16[512,5000]{1,0:T(8,128)(2,1)S(1)} %copy-done, bf16[5000,1024]{1,0:T(8,128)(2,1)} %param.3), kind=kOutput, calls=%fused_computation.26 | convolution fusion | flops 5242880000 | bytes 17457152 | tf_op jit(solution)/shard_map/dot_general | solution.py:168
  110.2 0.2 constant_dynamic-slice_fusion.5
  110.4 1.1 pad_maximum_fusion.1
  111.6 0.0 collective-permute-start.7
  111.6 0.0 collective-permute-done.4
  111.6 1.1 dynamic-slice_add_fusion
  112.7 1.3 collective-permute-start.5
  114.0 11.8 %collective-permute-done.5 = f32[256,512]{1,0:T(8,128)S(1)} collective-permute-done((f32[256,512]{1,0:T(8,128)S(1)}, f32[256,512]{1,0:T(8,128)S(1)}, u32[]{:S(2)}, u32[]{:S(2)}) %collective-permute-start.5) | collective-permute-done | bytes 524320 | tf_op jit(solution)/shard_map/ppermute | solution.py:162
  125.8 0.1 add.55
  125.8 1.4 collective-permute-start.6
  127.3 0.0 collective-permute-done.7
  127.3 0.2 maximum_add_fusion
  127.5 0.1 constant_dynamic-slice_fusion
  127.6 1.5 collective-permute-start.8
  129.1 0.0 collective-permute-done.6
  129.1 0.1 broadcast_select_fusion.1
  129.2 0.1 pad_maximum_fusion.gram_ref
  129.2 27.8 %factor.1 = (f32[4,128,128]{2,1,0:T(8,128)S(1)}, f32[4,128,512]{2,1,0:T(8,128)S(1)}) custom-call(f32[512,512]{1,0:T(8,128)S(1)} %pad_maximum_fusion.gram_ref), custom_call_target="tpu_custom_call" | custom-call | flops 30000001024 | bytes 3145728 | tf_op jit(solution)/shard_map/factor/pallas_call | solution.py:115
  157.1 0.0 collective-permute-done.8.other_ref
  157.1 3.1 %solve.1 = f32[512,256]{1,0:T(8,128)} custom-call(f32[4,128,128]{2,1,0:T(8,128)S(1)} %get-tuple-element.7.inv_ref, f32[4,128,512]{2,1,0:T(8,128)S(1)} %get-tuple-element.8.upper_ref, f32[512,256]{1,0:T(8,128)S(1)} %get-tuple-element.14.mine_ref, f32[512,256]{1,0:T(8,128)S(1)} %collective-permute-done.8.other_ref), custom_call_target="tpu_custom_call" | custom-call | tf_op jit(solution)/shard_map/solve/pallas_call | solution.py:129
  (9 shorter events, 0.1 us)
Async XLA Ops:
  6.5 86.7 %all-gather.2.cloned.1.call-start = ((), (), s32[]{:S(2)}) async-start(), calls=%async_computation | async-start | bytes 5898240 | tf_op jit(solution)/shard_map/all_gather | solution.py:148
  6.5 5.8 %collective-permute-start = (bf16[8,5000]{1,0:T(8,128)(2,1)}, bf16[8,5000]{1,0:T(8,128)(2,1)S(1)}, u32[]{:S(2)}, u32[]{:S(2)}) collective-permute-start(bf16[8,5000]{1,0:T(8,128)(2,1)} %bitcast.36), channel_id=1, source_target_pairs={{0,16},{4,20},{8,24},{12,28},{16,0},{20,4},{24,8},{28,12},{1,17},{... | collective-permute-start | bytes 240008 | tf_op jit(solution)/shard_map/ppermute | solution.py:141
  13.3 4.9 %collective-permute-start.1 = (bf16[2,8,5000]{2,1,0:T(8,128)(2,1)S(1)}, bf16[2,8,5000]{2,1,0:T(8,128)(2,1)S(1)}, u32[]{:S(2)}, u32[]{:S(2)}) collective-permute-start(bf16[2,8,5000]{2,1,0:T(8,128)(2,1)S(1)} %pad_maximum_fusion.2), channel_id=1, source_target_pairs={{0,12},{4,0},{8,4},{12,8},{16,28},{20,16},{24,20},{28,24},{1,13},{... | collective-permute-start | bytes 480008 | tf_op jit(solution)/shard_map/ppermute | solution.py:144
  15.9 7.9 %collective-permute-start.3 = (bf16[2,8,5000]{2,1,0:T(8,128)(2,1)S(1)}, bf16[2,8,5000]{2,1,0:T(8,128)(2,1)S(1)}, u32[]{:S(2)}, u32[]{:S(2)}) collective-permute-start(bf16[2,8,5000]{2,1,0:T(8,128)(2,1)S(1)} %pad_maximum_fusion.2), channel_id=1, source_target_pairs={{0,4},{4,8},{8,12},{12,0},{16,20},{20,24},{24,28},{28,16},{1,5},{5... | collective-permute-start | bytes 480008 | tf_op jit(solution)/shard_map/ppermute | solution.py:144
  15.9 7.1 %collective-permute-start.2 = (bf16[2,8,5000]{2,1,0:T(8,128)(2,1)S(1)}, bf16[2,8,5000]{2,1,0:T(8,128)(2,1)S(1)}, u32[]{:S(2)}, u32[]{:S(2)}) collective-permute-start(bf16[2,8,5000]{2,1,0:T(8,128)(2,1)S(1)} %pad_maximum_fusion.2), channel_id=1, source_target_pairs={{0,8},{4,12},{8,0},{12,4},{16,24},{20,28},{24,16},{28,20},{1,9},{5... | collective-permute-start | bytes 480008 | tf_op jit(solution)/shard_map/ppermute | solution.py:144
  93.2 8.5 %copy-start = (bf16[512,5000]{1,0:T(8,128)(2,1)S(1)}, bf16[512,5000]{1,0:T(8,128)(2,1)}, u32[]{:S(2)}) copy-start(bf16[512,5000]{1,0:T(8,128)(2,1)} %all-gather.2.cloned.1.call-done) | copy-start | bytes 15360004
  101.1 10.5 %collective-permute-start.4 = (f32[256,512]{1,0:T(8,128)}, f32[256,512]{1,0:T(8,128)}, u32[]{:S(2)}, u32[]{:S(2)}) collective-permute-start(f32[256,512]{1,0:T(8,128)} %constant_dynamic-slice_fusion.6), channel_id=1, source_target_pairs={{0,1},{1,0},{2,3},{3,2},{4,5},{5,4},{6,7},{7,6},{8,9},{9,8},{10,11... | collective-permute-start | bytes 1572872 | tf_op jit(solution)/shard_map/ppermute | solution.py:161
  111.6 15.7 %collective-permute-start.7 = (f32[512,512]{1,0:T(8,128)}, f32[512,512]{1,0:T(8,128)S(1)}, u32[]{:S(2)}, u32[]{:S(2)}) collective-permute-start(f32[512,512]{1,0:T(8,128)} %pad_maximum_fusion.1), channel_id=1, source_target_pairs={{0,1},{1,0},{2,3},{3,2},{4,5},{5,4},{6,7},{7,6},{8,9},{9,8},{10,11... | collective-permute-start | bytes 3145736 | tf_op jit(solution)/shard_map/ppermute | solution.py:176
  112.7 13.1 %collective-permute-start.5 = (f32[256,512]{1,0:T(8,128)S(1)}, f32[256,512]{1,0:T(8,128)S(1)}, u32[]{:S(2)}, u32[]{:S(2)}) collective-permute-start(f32[256,512]{1,0:T(8,128)S(1)} %dynamic-slice_add_fusion), channel_id=1, source_target_pairs={{0,2},{2,0},{1,3},{3,1},{4,6},{6,4},{5,7},{7,5},{8,10},{10,8},{9,1... | collective-permute-start | bytes 1572872 | tf_op jit(solution)/shard_map/ppermute | solution.py:162
  125.8 3.2 %collective-permute-start.6 = (f32[256,512]{1,0:T(8,128)S(1)}, f32[256,512]{1,0:T(8,128)S(1)}, u32[]{:S(2)}, u32[]{:S(2)}) collective-permute-start(f32[256,512]{1,0:T(8,128)S(1)} %add.55), channel_id=1, source_target_pairs={{0,1},{1,0},{2,3},{3,2},{4,5},{5,4},{6,7},{7,6},{8,9},{9,8},{10,11... | collective-permute-start | bytes 1572872 | tf_op jit(solution)/shard_map/ppermute | solution.py:163
  127.6 29.5 %collective-permute-start.8 = (f32[512,256]{1,0:T(8,128)S(1)}, f32[512,256]{1,0:T(8,128)S(1)}, u32[]{:S(2)}, u32[]{:S(2)}) collective-permute-start(f32[512,256]{1,0:T(8,128)S(1)} %get-tuple-element.13), channel_id=1, source_target_pairs={{0,2},{2,0},{1,3},{3,1},{4,6},{6,4},{5,7},{7,5},{8,10},{10,8},{9,1... | collective-permute-start | bytes 1572872 | tf_op jit(solution)/shard_map/ppermute | solution.py:178
Sparse Core Ops, SparseCore 0:
  24.9 68.2 all-gather.1

commit v2 on v1

v2 whole, which is shorter than its diff:
```python
import jax
import jax.numpy as jnp
from jax import lax
from jax.experimental import pallas as pl
from jax.experimental.pallas import tpu as pltpu
from jax.sharding import PartitionSpec as P

F32 = jnp.float32
HI = lax.Precision.HIGHEST
ROW0 = (((0,), (0,)), ((), ()))
NB = 128
PANEL = 512
HALF_K = 2560
CHUNK_K = 512
HALVES = (((0, 0), (0, 1), (0, 2), (0, 3), (3, 3)), ((1, 1), (1, 2), (1, 3), (2, 2), (2, 3)))

CORE_SWAP = [(0, 1), (1, 0), (2, 3), (3, 2)]
CHIP_SWAP = [(0, 2), (2, 0), (1, 3), (3, 1)]


def x_shift(k):
    return [(h * 4 + x, h * 4 + (x + k) % 4) for h in range(2) for x in range(4)]


Y_SWAP = [(c, (c + 4) % 8) for c in range(8)]


def spread(v):
    return jnp.broadcast_to(v, (8, NB))


def reciprocal(v):
    return pl.reciprocal(v, approx=True)


def held_group(q):
    z, rest = divmod(q, 8)
    y, x = divmod(rest, 4)
    return z * 8 + x * 2 + y


def three_way(v):
    high = v.astype(jnp.bfloat16).astype(F32)
    v = v - high
    mid = v.astype(jnp.bfloat16).astype(F32)
    return high, mid, v - mid


def inverse_factor(rows):
    rows = list(rows)
    groups, near_by, out = len(rows), 3, []
    lane = lax.broadcasted_iota(jnp.int32, (8, NB), 1)
    sub = lax.broadcasted_iota(jnp.int32, (8, NB), 0)
    at = [sub == s for s in range(8)]
    true_lane = (lane // 64) * 64 + ((lane // 8) % 2) * 32 + ((lane // 16) % 4) * 8 + lane % 8

    def lanes(v, b):
        return [spread(v[:, b + t : b + t + 1]) for t in range(8)]

    def row(v, s):
        return spread(v[s : s + 1, :])

    diag = lanes(rows[0], 8 * held_group(0))
    for q in range(groups):
        b = 8 * held_group(q)
        a = {(s, t): row(diag[t], s) for t in range(8) for s in range(t, 8)}
        here = (lane >= b) & (lane < b + 8)
        w = jnp.where(here, jnp.where(lane - b == sub, 1.0, 0.0), rows[q])
        near = range(q + 1, min(q + 1 + near_by, groups))
        far = range(q + 1 + near_by, groups)
        if q + 1 < groups:
            diag = lanes(rows[q + 1], 8 * held_group(q + 1))
        below = {g: lanes(rows[g], b) for g in near}
        for g in range(q + 1, groups):
            rows[g] = jnp.where(here, 0.0, rows[g])
        pivots = jnp.ones((8, NB), F32)
        for t in range(8):
            d = a[t, t]
            if t < 7:
                square = a[t + 1, t] * a[t + 1, t]
            r = reciprocal(d)
            pivots = jnp.where(at[t], d, pivots)
            m = {s: a[s, t] * r for s in range(t + 1, 8)}
            for u in range(t + 1, 8):
                for s in range(u, 8):
                    step = square * r if s == t + 1 else m[s] * a[u, t]
                    a[s, u] = a[s, u] - step
            if q + 1 < groups:
                mg = below[q + 1][t] * r
                for u in range(8):
                    diag[u] = diag[u] - mg * row(below[q + 1][t], u)
            pivot_row = row(w, t)
            if t < 7:
                m_col = jnp.zeros((8, NB), F32)
                for s in range(t + 1, 8):
                    m_col = jnp.where(at[s], m[s], m_col)
                w = w - m_col * pivot_row
            for g in near:
                mg = below[g][t] * r
                for u in range(t + 1, 8):
                    below[g][u] = below[g][u] - mg * a[u, t]
                rows[g] = rows[g] - mg * pivot_row
        if len(far):
            ah, am, al = three_way(w * reciprocal(pivots))
            bh, bm, bl = three_way(w)
            product = lax.dot_general(
                jnp.concatenate([ah, ah, am, ah, am, al], 0).astype(jnp.bfloat16),
                jnp.concatenate([bh, bm, bh, bl, bm, bh], 0).astype(jnp.bfloat16),
                ROW0,
                preferred_element_type=F32,
            )
            for g in far:
                h = 8 * held_group(g)
                rows[g] = rows[g] - product[h : h + 8]
        root = lax.rsqrt(pivots)
        root = root * (1.5 - (0.5 * pivots * root) * root)
        out.append(jnp.where(true_lane <= sub + 8 * q, w * root, 0.0))
    return out


def factor_kernel(mine_ref, other_ref, inv_ref, upper_ref, pair_ref):
    core = lax.axis_index("orb") % 2

    def place(ref, half):
        for k, (i, j) in enumerate(HALVES[half]):
            gram = ref[k]
            pair_ref[i * NB : (i + 1) * NB, j * NB : (j + 1) * NB] = gram * gram

    @pl.when(core == 0)
    def _():
        place(mine_ref, 0)
        place(other_ref, 1)

    @pl.when(core == 1)
    def _():
        place(other_ref, 0)
        place(mine_ref, 1)

    def step(j, carry):
        o = pl.multiple_of(j * NB, NB)
        rows = [
            pair_ref[pl.ds(o + 8 * held_group(q), 8), pl.ds(o, NB)] for q in range(NB // 8)
        ]
        inv = jnp.concatenate(inverse_factor(rows), 0)
        inv_ref[j] = inv
        for k in range(PANEL // NB - 1):

            @pl.when(j == k)
            def _():
                rest = (k + 1) * NB
                upper = jnp.dot(
                    inv,
                    pair_ref[k * NB : rest, rest:],
                    precision=HI,
                    preferred_element_type=F32,
                )
                upper_ref[k, :, rest:] = upper
                for i in range(rest, PANEL, NB):
                    pair_ref[i : i + NB, i:] -= lax.dot_general(
                        upper[:, i - rest : i - rest + NB],
                        upper[:, i - rest :],
                        ROW0,
                        precision=HI,
                        preferred_element_type=F32,
                    )

        return carry

    lax.fori_loop(0, PANEL // NB, step, 0)


def solve_kernel(inv_ref, upper_ref, keep_ref, arrived_ref, other_ref, out_ref, gram_ref, sems):
    chip = lax.axis_index("orb") // 2
    copies = [
        pltpu.make_async_copy(ref.at[chip], gram_ref.at[k], sems.at[k])
        for k, ref in enumerate((keep_ref, arrived_ref))
    ]
    for copy in copies:
        copy.start()
    for copy in copies:
        copy.wait()
    solved = []
    for j in range(PANEL // NB):
        cut = slice(j * NB, (j + 1) * NB)
        gram = gram_ref[0, cut, :] + gram_ref[1, cut, :] + other_ref[cut, :]
        rest = gram * gram
        for i in range(j):
            rest -= lax.dot_general(
                upper_ref[i, :, cut], solved[i], ROW0, precision=HI, preferred_element_type=F32
            )
        x = jnp.dot(inv_ref[j], rest, precision=HI, preferred_element_type=F32)
        solved.append(x)
        out_ref[cut, :] = x


def factorise(mine, other):
    blocks = PANEL // NB
    return pl.pallas_call(
        factor_kernel,
        out_shape=(
            jax.ShapeDtypeStruct((blocks, NB, NB), F32),
            jax.ShapeDtypeStruct((blocks - 1, NB, PANEL), F32),
        ),
        scratch_shapes=[pltpu.VMEM((PANEL, PANEL), F32)],
        compiler_params=pltpu.CompilerParams(vmem_limit_bytes=40 << 20),
        cost_estimate=pl.CostEstimate(flops=30_000_000_000, bytes_accessed=3 << 20, transcendentals=0),
        name="factor",
    )(mine, other)


def solve(inv, upper, keep, arrived, other):
    vmem, hbm = pl.BlockSpec(memory_space=pltpu.VMEM), pl.BlockSpec(memory_space=pl.ANY)
    return pl.pallas_call(
        solve_kernel,
        in_specs=[vmem, vmem, hbm, hbm, vmem],
        out_shape=jax.ShapeDtypeStruct(other.shape, F32),
        scratch_shapes=[pltpu.VMEM((2,) + other.shape, F32), pltpu.SemaphoreType.DMA((2,))],
        compiler_params=pltpu.CompilerParams(vmem_limit_bytes=40 << 20),
        name="solve",
    )(inv, upper, keep, arrived, other)


def z_shift(k):
    return [(z, (z + k) % 8) for z in range(8)]


def along_z(k, v):
    return lax.ppermute(v, "prow", z_shift(k))


def along_x(k, v):
    return lax.ppermute(v, "pcol", x_shift(k))


def gather_panel(panel):
    own = jnp.pad(panel.T, ((0, 0), (0, 2 * HALF_K - panel.shape[0])))
    far = lax.ppermute(own, "pcol", Y_SWAP)
    first = lax.axis_index("pcol") < 4
    pair = jnp.where(first, jnp.concatenate([own, far], 0), jnp.concatenate([far, own], 0))
    left, right = pair[:, :HALF_K], pair[:, HALF_K:]

    x_steps = (0, -1, 1, 2)
    plane = jnp.concatenate([left, along_x(1, left), along_x(-1, left), along_x(2, left)], 0)
    pieces, places = [plane], [(0, 16 * k, 0, 0, s) for k, s in enumerate(x_steps)]
    up = down = plane
    for s in range(1, 5):
        up = along_z(1, up)
        places += [(len(pieces), 16 * k, 0, -s, t) for k, t in enumerate(x_steps)]
        pieces.append(up)
        if s < 4:
            down = along_z(-1, down)
            places += [(len(pieces), 16 * k, 0, s, t) for k, t in enumerate(x_steps)]
            pieces.append(down)

    z_steps, column = [0], [right]
    up = down = right
    for s in range(1, 5):
        up = along_z(1, up)
        z_steps.append(-s)
        column.append(up)
        if s < 4:
            down = along_z(-1, down)
            z_steps.append(s)
            column.append(down)
    column = jnp.concatenate(column, 0)
    half = column.shape[0] // 2
    up, down = along_x(1, column), along_x(-1, column)
    for piece, t, r in (
        (column, 0, range(8)),
        (up, -1, range(8)),
        (down, 1, range(8)),
        (along_x(1, up[:half]), 2, range(4)),
        (along_x(-1, down[half:]), 2, range(4, 8)),
    ):
        places += [(len(pieces), 16 * k, 1, z_steps[m], t) for k, m in enumerate(r)]
        pieces.append(piece)
    return pieces, places


def load_panel(places, piece_refs, panel_ref, sems):
    z = lax.axis_index("prow")
    x = lax.axis_index("pcol") % 4
    for piece, row, half, dz, dx in places:
        to = lax.rem(z + dz + 8, 8) * 64 + lax.rem(x + dx + 4, 4) * 16
        pltpu.make_async_copy(
            piece_refs[piece].at[pl.ds(row, 16), :],
            panel_ref.at[half, pl.ds(pl.multiple_of(to, 16), 16), :],
            sems.at[half],
        ).start()


def wait_panel(panel_ref, sems, half):
    pltpu.make_async_copy(panel_ref.at[half], panel_ref.at[half], sems.at[half]).wait()


def panel_gram_kernel(places, pieces, *refs):
    piece_refs, (out_ref, panel_ref, sems) = refs[:pieces], refs[pieces:]
    load_panel(places, piece_refs, panel_ref, sems)
    strips = [None, None]
    for half in range(2):
        wait_panel(panel_ref, sems, half)
        for s in range(2):
            part = lax.dot_general(
                panel_ref[half, s * 256 : (s + 1) * 256, :],
                panel_ref[half, s * 256 :, :],
                (((1,), (1,)), ((), ())),
                preferred_element_type=F32,
            )
            strips[s] = part if half == 0 else strips[s] + part
    for h, blocks in enumerate(HALVES):
        for k, (i, j) in enumerate(blocks):
            s = i // 2
            out_ref[h, k] = strips[s][
                (i - 2 * s) * NB : (i - 2 * s + 1) * NB, (j - 2 * s) * NB : (j - 2 * s + 1) * NB
            ]


def panel_gram(pieces, places):
    return pl.pallas_call(
        lambda *refs: panel_gram_kernel(places, len(pieces), *refs),
        in_specs=[pl.BlockSpec(memory_space=pl.ANY)] * len(pieces),
        out_shape=jax.ShapeDtypeStruct((2, 5, NB, NB), F32),
        scratch_shapes=[pltpu.VMEM((2, PANEL, HALF_K), jnp.bfloat16), pltpu.SemaphoreType.DMA((2,))],
        compiler_params=pltpu.CompilerParams(vmem_limit_bytes=60 << 20),
        cost_estimate=pl.CostEstimate(flops=3_000_000_000, bytes_accessed=8 << 20, transcendentals=0),
        name="panel_gram",
    )(*pieces)


def row_gram_kernel(places, pieces, *refs):
    piece_refs = refs[:pieces]
    orbitals_ref, give_ref, keep_ref, panel_ref, window_ref, total_ref, sems, window_sems = refs[pieces:]
    core = lax.axis_index("orb") % 2
    load_panel(places, piece_refs, panel_ref, sems)
    rows = orbitals_ref.shape[0]
    window_ref[rows:, :] = jnp.zeros((2 * HALF_K - rows, orbitals_ref.shape[1]), jnp.bfloat16)
    copies = []
    for k in range(0, rows, CHUNK_K):
        part = pl.ds(k, min(CHUNK_K, rows - k))
        copies.append(
            pltpu.make_async_copy(
                orbitals_ref.at[part, :], window_ref.at[part, :], window_sems.at[len(copies)]
            )
        )
        copies[-1].start()
    for k, copy in enumerate(copies):
        half, at = divmod(k * CHUNK_K, HALF_K)
        if at == 0:
            wait_panel(panel_ref, sems, half)
        copy.wait()
        part = jnp.dot(
            panel_ref[half, :, at : at + CHUNK_K],
            window_ref[k * CHUNK_K : (k + 1) * CHUNK_K, :],
            preferred_element_type=F32,
        )
        quarter = part.shape[1] // 4
        for n in range(4):
            value = part[:, n * quarter : (n + 1) * quarter]
            total_ref[n] = value if k == 0 else total_ref[n] + value
    sends = []
    for c in range(2):
        for ref, which in ((give_ref, 1 - core), (keep_ref, core)):
            sends.append(
                pltpu.make_async_copy(total_ref.at[2 * c + which], ref.at[c], window_sems.at[len(sends)])
            )
            sends[-1].start()
    for send in sends:
        send.wait()


def row_gram(pieces, places, orbitals):
    rows, columns = orbitals.shape
    out = jax.ShapeDtypeStruct((2, PANEL, columns // 4), F32)
    return pl.pallas_call(
        lambda *refs: row_gram_kernel(places, len(pieces), *refs),
        in_specs=[pl.BlockSpec(memory_space=pl.ANY)] * (len(pieces) + 1),
        out_specs=[pl.BlockSpec(memory_space=pl.ANY)] * 2,
        out_shape=(out, out),
        scratch_shapes=[
            pltpu.VMEM((2, PANEL, HALF_K), jnp.bfloat16),
            pltpu.VMEM((2 * HALF_K, columns), jnp.bfloat16),
            pltpu.VMEM((4, PANEL, columns // 4), F32),
            pltpu.SemaphoreType.DMA((2,)),
            pltpu.SemaphoreType.DMA((2 * HALF_K // CHUNK_K,)),
        ],
        compiler_params=pltpu.CompilerParams(vmem_limit_bytes=60 << 20),
        cost_estimate=pl.CostEstimate(flops=6_000_000_000, bytes_accessed=17 << 20, transcendentals=0),
        name="row_gram",
    )(*pieces, orbitals)


def swap_cores(v):
    return lax.ppermute(v, "orb", CORE_SWAP)


def swap_chips(v):
    return lax.ppermute(v, "orb", CHIP_SWAP)


def pick(v, which):
    return lax.dynamic_index_in_dim(v, which, 0, keepdims=False)


def on_device(panel_orbitals, orbitals):
    core = lax.axis_index("orb") % 2
    chip = lax.axis_index("orb") // 2
    pieces, places = gather_panel(panel_orbitals)

    panel = panel_gram(pieces, places)
    half = pick(panel, core) + swap_cores(pick(panel, 1 - core))
    half, pieces = lax.optimization_barrier((half, pieces))
    half = half + swap_chips(half)
    give, keep = row_gram(pieces, places, orbitals)
    half, give = lax.optimization_barrier((half, give))
    arrived = swap_cores(give)
    other = swap_chips(pick(keep, 1 - chip) + pick(arrived, 1 - chip))
    inv, upper = factorise(half, swap_cores(half))
    return solve(inv, upper, keep, arrived, other)


def solution(mesh):
    return jax.shard_map(
        on_device,
        mesh=mesh,
        in_specs=(P("orb", ("prow", "pcol")), P("orb", ("prow", "pcol"))),
        out_specs=P(None, ("prow", "pcol", "orb")),
        check_vma=False,
    )
```

time: 167 us -> 123 us (0.74)
  waiting for transfers between devices: 88.3 us -> 39 us
  starting transfers between devices: 13 us -> 46.3 us
  matrix products: 15.4 us -> 0 us
  between operations: 13.6 us -> 0.44 us
  Pallas kernels: 30.9 us -> 32.8 us
    all_gather x1 -> x0, waiting for transfers between devices: 68.4 us -> none  [gather_panel(): return lax.all_gather(plane, 'prow', axis=0, tiled=True)]
    ppermute x8 -> x26, starting transfers between devices: 9.23 us -> 42.5 us  [the longest x14 21.6 us: along_z(): return lax.ppermute(v, 'prow', z_shift(k))]
    ppermute x8 -> x26, waiting for transfers between devices: 17.9 us -> 37.2 us  [the longest x14 29.8 us: along_z(): return lax.ppermute(v, 'prow', z_shift(k))]
    pallas_call x1 -> x3, Pallas kernels: 3.07 us -> 19.1 us  [the longest x1 10.3 us: row_gram(): pl.pallas_call(lambda *refs: row_gram_kernel(places, len(pieces), *refs),...]
    dot_general x2 -> x0, matrix products: 15.4 us -> none  [the longest x1 8.41 us: on_device(): lax.dot_general(full, orbitals, (((1,), (0,)), ((), ())), preferred_eleme...]
    pallas_call x1, Pallas kernels: 27.8 us -> 13.7 us  [factorise(): pl.pallas_call(factor_kernel, out_shape=(jax.ShapeDtypeStruct((blocks, NB...]
    dynamic_slice x4 -> x0, local copies, waits for them, and re-layouts: 2.12 us -> none  [the longest x1 0.92 us: gather_panel(): ring = lax.dynamic_slice_in_dim(ring, 3 - x, 4, 0)]
  transfers between devices with their start and end apart: 10 -> 27, of which waited for: 6 -> 11; matrix products, arithmetic and copies ran while one was open for 7% -> 1% of each run, Pallas kernels for 17% -> 20%
where the time goes in v2:
time: 123 us
  starting transfers between devices  46.3 us (38%)
  waiting for transfers between devices  39 us (32%)
  Pallas kernels  32.8 us (27%)
  other arithmetic  2.21 us (2%)
  local copies, waits for them, and re-layouts  2.04 us (2%)
    ppermute x14, waiting for transfers between devices, along_z(): return lax.ppermute(v, 'prow', z_shift(k))  29.8 us
    ppermute x14, starting transfers between devices, along_z(): return lax.ppermute(v, 'prow', z_shift(k))  21.6 us
    pallas_call x1, Pallas kernels, factorise(): pl.pallas_call(factor_kernel, out_shape=(jax.ShapeDtypeStruct((blocks, NB...  13.7 us
    ppermute x3, starting transfers between devices, swap_cores(): return lax.ppermute(v, 'orb', CORE_SWAP)  10.3 us
    pallas_call x1, Pallas kernels, row_gram(): pl.pallas_call(lambda *refs: row_gram_kernel(places, len(pieces), *refs),...  10.3 us
    ppermute x7, starting transfers between devices, along_x(): return lax.ppermute(v, 'pcol', x_shift(k))  8.98 us
    pallas_call x1, Pallas kernels, panel_gram(): pl.pallas_call(lambda *refs: panel_gram_kernel(places, len(pieces), *refs...  5.67 us
    ppermute x3, waiting for transfers between devices, swap_cores(): return lax.ppermute(v, 'orb', CORE_SWAP)  4.12 us
  transfers between devices with their start and end apart: 27, of which 11 were waited for; matrix products, arithmetic and copies ran while one was open for 1% of the time, Pallas kernels for 20%

profile of v2, /device:TPU:1, one launch (start us, length us, event | category | flops | bytes accessed | tf_op | source)
XLA Modules:
  0.0 122.8 jit_solution(17434337078331992753)
XLA Ops:
  0.0 0.9 pad.4
  0.9 3.7 %collective-permute-start = (bf16[8,5120]{1,0:T(8,128)(2,1)S(1)}, bf16[8,5120]{1,0:T(8,128)(2,1)S(1)}, u32[]{:S(2)}, u32[]{:S(2)}) collective-permute-start(bf16[8,5120]{1,0:T(8,128)(2,1)S(1)} %pad.4), channel_id=1, source_target_pairs={{0,16},{4,20},{8,24},{12,28},{16,0},{20,4},{24,8},{28,12},{1,17},{... | collective-permute-start | bytes 245768 | tf_op jit(solution)/shard_map/ppermute | solution.py:237
  4.6 1.8 %collective-permute-done = bf16[8,5120]{1,0:T(8,128)(2,1)S(1)} collective-permute-done((bf16[8,5120]{1,0:T(8,128)(2,1)S(1)}, bf16[8,5120]{1,0:T(8,128)(2,1)S(1)}, u32[]{:S(2)}, u32[]{:S(2)}) %collective-permute-start) | collective-permute-done | bytes 81952 | tf_op jit(solution)/shard_map/ppermute | solution.py:237
  6.5 2.9 %collective-permute-start.3 = (bf16[16,2560]{1,0:T(8,128)(2,1)S(1)}, bf16[16,2560]{1,0:T(8,128)(2,1)S(1)}, u32[]{:S(2)}, u32[]{:S(2)}) collective-permute-start(bf16[16,2560]{1,0:T(8,128)(2,1)S(1)} %get-tuple-element.47), channel_id=1, source_target_pairs={{0,8},{4,12},{8,0},{12,4},{16,24},{20,28},{24,16},{28,20},{1,9},{5... | collective-permute-start | bytes 245768 | tf_op jit(solution)/shard_map/ppermute | solution.py:232
  9.4 0.9 collective-permute-start.2
  10.3 0.6 collective-permute-start.1
  10.9 5.6 %collective-permute-start.12 = (bf16[16,2560]{1,0:T(8,128)(2,1)S(1)}, bf16[16,2560]{1,0:T(8,128)(2,1)S(1)}, u32[]{:S(2)}, u32[]{:S(2)}) collective-permute-start(bf16[16,2560]{1,0:T(8,128)(2,1)S(1)} %get-tuple-element.45), channel_id=1, source_target_pairs={{0,224},{32,0},{64,32},{96,64},{128,96},{160,128},{192,160},{224,1... | collective-permute-start | bytes 245768 | tf_op jit(solution)/shard_map/ppermute | solution.py:228
  16.5 0.0 collective-permute-start.11
  16.5 0.0 collective-permute-done.3
  16.5 0.0 collective-permute-done.2
  16.5 0.0 collective-permute-done.1
  16.5 0.0 copy-start.1
  16.5 4.3 %collective-permute-start.5 = (bf16[64,2560]{1,0:T(8,128)(2,1)S(1)}, bf16[64,2560]{1,0:T(8,128)(2,1)S(1)}, u32[]{:S(2)}, u32[]{:S(2)}) collective-permute-start(bf16[64,2560]{1,0:T(8,128)(2,1)S(1)} %pad_maximum_fusion.refs_0_), channel_id=1, source_target_pairs={{0,224},{32,0},{64,32},{96,64},{128,96},{160,128},{192,160},{224,1... | collective-permute-start | bytes 983048 | tf_op jit(solution)/shard_map/ppermute | solution.py:228
  20.8 0.0 collective-permute-start.4
  20.8 0.0 collective-permute-done.12
  20.8 2.7 %collective-permute-start.14 = (bf16[16,2560]{1,0:T(8,128)(2,1)S(1)}, bf16[16,2560]{1,0:T(8,128)(2,1)S(1)}, u32[]{:S(2)}, u32[]{:S(2)}) collective-permute-start(bf16[16,2560]{1,0:T(8,128)(2,1)S(1)} %collective-permute-done.12), channel_id=1, source_target_pairs={{0,224},{32,0},{64,32},{96,64},{128,96},{160,128},{192,160},{224,1... | collective-permute-start | bytes 245768 | tf_op jit(solution)/shard_map/ppermute | solution.py:228
  23.5 0.0 collective-permute-done.11
  23.5 0.0 collective-permute-start.13
  23.5 2.8 %collective-permute-done.14 = bf16[16,2560]{1,0:T(8,128)(2,1)S(1)} collective-permute-done((bf16[16,2560]{1,0:T(8,128)(2,1)S(1)}, bf16[16,2560]{1,0:T(8,128)(2,1)S(1)}, u32[]{:S(2)}, u32[]{:S(2)}) %collective-permute-start.14) | collective-permute-done | bytes 81952 | tf_op jit(solution)/shard_map/ppermute | solution.py:228
  26.3 3.4 %collective-permute-start.16 = (bf16[16,2560]{1,0:T(8,128)(2,1)S(1)}, bf16[16,2560]{1,0:T(8,128)(2,1)S(1)}, u32[]{:S(2)}, u32[]{:S(2)}) collective-permute-start(bf16[16,2560]{1,0:T(8,128)(2,1)S(1)} %collective-permute-done.14), channel_id=1, source_target_pairs={{0,224},{32,0},{64,32},{96,64},{128,96},{160,128},{192,160},{224,1... | collective-permute-start | bytes 245768 | tf_op jit(solution)/shard_map/ppermute | solution.py:228
  29.7 0.0 collective-permute-done.13
  29.7 0.0 collective-permute-start.15
  29.8 4.5 %collective-permute-done.15 = bf16[16,2560]{1,0:T(8,128)(2,1)S(1)} collective-permute-done((bf16[16,2560]{1,0:T(8,128)(2,1)S(1)}, bf16[16,2560]{1,0:T(8,128)(2,1)S(1)}, u32[]{:S(2)}, u32[]{:S(2)}) %collective-permute-start.15) | collective-permute-done | bytes 81952 | tf_op jit(solution)/shard_map/ppermute | solution.py:228
  34.2 0.0 collective-permute-start.17
  34.3 0.0 collective-permute-done.16
  34.3 5.3 %collective-permute-done.17 = bf16[16,2560]{1,0:T(8,128)(2,1)S(1)} collective-permute-done((bf16[16,2560]{1,0:T(8,128)(2,1)S(1)}, bf16[16,2560]{1,0:T(8,128)(2,1)S(1)}, u32[]{:S(2)}, u32[]{:S(2)}) %collective-permute-start.17) | collective-permute-done | bytes 81952 | tf_op jit(solution)/shard_map/ppermute | solution.py:228
  39.6 1.9 %collective-permute-start.19 = (bf16[128,2560]{1,0:T(8,128)(2,1)S(1)}, bf16[128,2560]{1,0:T(8,128)(2,1)S(1)}, u32[]{:S(2)}, u32[]{:S(2)}) collective-permute-start(bf16[128,2560]{1,0:T(8,128)(2,1)S(1)} %constant_dynamic-update-slice_fusion.refs_8_), channel_id=1, source_target_pairs={{0,12},{4,0},{8,4},{12,8},{16,28},{20,16},{24,20},{28,24},{1,13},{... | collective-permute-start | bytes 1966088 | tf_op jit(solution)/shard_map/ppermute | solution.py:232
  41.5 0.0 collective-permute-start.18
  41.5 0.0 collective-permute-done.4.refs_1_
  41.5 0.1 collective-permute-start.6
  41.6 0.0 collective-permute-done.5.refs_2_
  41.6 2.6 %collective-permute-start.7 = (bf16[64,2560]{1,0:T(8,128)(2,1)S(1)}, bf16[64,2560]{1,0:T(8,128)(2,1)}, u32[]{:S(2)}, u32[]{:S(2)}) collective-permute-start(bf16[64,2560]{1,0:T(8,128)(2,1)S(1)} %collective-permute-done.5.refs_2_), channel_id=1, source_target_pairs={{0,224},{32,0},{64,32},{96,64},{128,96},{160,128},{192,160},{224,1... | collective-permute-start | bytes 983048 | tf_op jit(solution)/shard_map/ppermute | solution.py:228
  44.3 4.5 %collective-permute-done.6.refs_3_ = bf16[64,2560]{1,0:T(8,128)(2,1)S(1)} collective-permute-done((bf16[64,2560]{1,0:T(8,128)(2,1)S(1)}, bf16[64,2560]{1,0:T(8,128)(2,1)S(1)}, u32[]{:S(2)}, u32[]{:S(2)}) %collective-permute-start.6) | collective-permute-done | bytes 327712 | tf_op jit(solution)/shard_map/ppermute | solution.py:228
  48.8 0.0 collective-permute-start.8
  48.8 0.0 collective-permute-done.7.refs_4_
  48.8 2.9 %collective-permute-start.9 = (bf16[64,2560]{1,0:T(8,128)(2,1)}, bf16[64,2560]{1,0:T(8,128)(2,1)}, u32[]{:S(2)}, u32[]{:S(2)}) collective-permute-start(bf16[64,2560]{1,0:T(8,128)(2,1)} %collective-permute-done.7.refs_4_), channel_id=1, source_target_pairs={{0,224},{32,0},{64,32},{96,64},{128,96},{160,128},{192,160},{224,1... | collective-permute-start | bytes 983048 | tf_op jit(solution)/shard_map/ppermute | solution.py:228
  51.7 0.0 collective-permute-done.19.refs_10_
  51.8 2.7 %collective-permute-start.21 = (bf16[64,2560]{1,0:T(8,128)(2,1)S(1)}, bf16[64,2560]{1,0:T(8,128)(2,1)}, u32[]{:S(2)}, u32[]{:S(2)}) collective-permute-start(bf16[64,2560]{1,0:T(8,128)(2,1)S(1)} %slice.19), channel_id=1, source_target_pairs={{0,12},{4,0},{8,4},{12,8},{16,28},{20,16},{24,20},{28,24},{1,13},{... | collective-permute-start | bytes 983048 | tf_op jit(solution)/shard_map/ppermute | solution.py:232
  54.4 0.0 copy-done.6
  54.4 0.0 collective-permute-done.18.refs_9_
  54.5 0.1 collective-permute-start.20
  54.6 5.0 %collective-permute-done.8.refs_5_ = bf16[64,2560]{1,0:T(8,128)(2,1)} collective-permute-done((bf16[64,2560]{1,0:T(8,128)(2,1)S(1)}, bf16[64,2560]{1,0:T(8,128)(2,1)}, u32[]{:S(2)}, u32[]{:S(2)}) %collective-permute-start.8) | collective-permute-done | bytes 327712 | tf_op jit(solution)/shard_map/ppermute | solution.py:228
  59.6 0.0 collective-permute-start.10
  59.6 0.0 collective-permute-done.9.refs_6_
  59.6 0.4 collective-permute-done.21.refs_12_
  60.0 2.8 %collective-permute-done.20.refs_11_ = bf16[64,2560]{1,0:T(8,128)(2,1)} collective-permute-done((bf16[64,2560]{1,0:T(8,128)(2,1)S(1)}, bf16[64,2560]{1,0:T(8,128)(2,1)}, u32[]{:S(2)}, u32[]{:S(2)}) %collective-permute-start.20) | collective-permute-done | bytes 327712 | tf_op jit(solution)/shard_map/ppermute | solution.py:232
  62.8 7.6 %collective-permute-done.10.refs_7_ = bf16[64,2560]{1,0:T(8,128)(2,1)} collective-permute-done((bf16[64,2560]{1,0:T(8,128)(2,1)}, bf16[64,2560]{1,0:T(8,128)(2,1)}, u32[]{:S(2)}, u32[]{:S(2)}) %collective-permute-start.10) | collective-permute-done | bytes 327712 | tf_op jit(solution)/shard_map/ppermute | solution.py:228
  70.5 5.7 %panel_gram.1 = f32[2,5,128,128]{3,2,1,0:T(8,128)} custom-call(bf16[64,2560]{1,0:T(8,128)(2,1)} %copy-done.1, bf16[64,2560]{1,0:T(8,128)(2,1)} %copy-done.6, bf16[64,2560]{1,0:T(8,128)(2,1)} %copy-done.5, bf16[64,2560]{1,0:T(8,128)(2,1)} %copy-done.7, bf16[64,2560]{1,0:T(8,128)(2,1)} %collective-permute-done.7.refs_4_, ...), custom_call_target="tpu_custom_call" | custom-call | flops 3000000000 | bytes 8388608 | tf_op jit(solution)/shard_map/panel_gram/pallas_call | solution.py:319
  76.1 1.0 dynamic-slice_bitcast_fusion
  77.1 9.5 %collective-permute-start.22 = (f32[5,128,128]{2,1,0:T(8,128)S(1)}, f32[5,128,128]{2,1,0:T(8,128)S(1)}, u32[]{:S(2)}, u32[]{:S(2)}) collective-permute-start(f32[5,128,128]{2,1,0:T(8,128)S(1)} %dynamic-slice_bitcast_fusion), channel_id=1, source_target_pairs={{0,1},{1,0},{2,3},{3,2},{4,5},{5,4},{6,7},{7,6},{8,9},{9,8},{10,11... | collective-permute-start | bytes 983048 | tf_op jit(solution)/shard_map/ppermute | solution.py:393
  86.6 1.3 %collective-permute-done.22 = f32[5,128,128]{2,1,0:T(8,128)S(1)} collective-permute-done((f32[5,128,128]{2,1,0:T(8,128)S(1)}, f32[5,128,128]{2,1,0:T(8,128)S(1)}, u32[]{:S(2)}, u32[]{:S(2)}) %collective-permute-start.22) | collective-permute-done | bytes 327712 | tf_op jit(solution)/shard_map/ppermute | solution.py:393
  87.9 1.0 bitcast_add_fusion
  88.9 1.4 %collective-permute-start.23 = (f32[5,128,128]{2,1,0:T(8,128)S(1)}, f32[5,128,128]{2,1,0:T(8,128)S(1)}, u32[]{:S(2)}, u32[]{:S(2)}) collective-permute-start(f32[5,128,128]{2,1,0:T(8,128)S(1)} %bitcast_add_fusion), channel_id=1, source_target_pairs={{0,2},{2,0},{1,3},{3,1},{4,6},{6,4},{5,7},{7,5},{8,10},{10,8},{9,1... | collective-permute-start | bytes 983048 | tf_op jit(solution)/shard_map/ppermute | solution.py:397
  90.3 10.3 %row_gram.1 = (f32[2,512,256]{2,1,0:T(8,128)}, f32[2,512,256]{2,1,0:T(8,128)}) custom-call(bf16[64,2560]{1,0:T(8,128)(2,1)} %copy-done.1, bf16[64,2560]{1,0:T(8,128)(2,1)} %copy-done.6, bf16[64,2560]{1,0:T(8,128)(2,1)} %copy-done.5, bf16[64,2560]{1,0:T(8,128)(2,1)} %copy-done.7, bf16[64,2560]{1,0:T(8,128)(2,1)} %collective-permute-done.7.refs_4_, ...), custom_call_target="tpu_custom_call" | custom-call | flops 6000000000 | bytes 17825792 | tf_op jit(solution)/shard_map/row_gram/pallas_call | solution.py:374
  100.6 0.0 collective-permute-done.23
  100.6 0.7 collective-permute-start.25
  101.4 0.1 collective-permute-start.24
  101.5 2.9 %collective-permute-done.25.arrived_ref = f32[2,512,256]{2,1,0:T(8,128)S(1)} collective-permute-done((f32[2,512,256]{2,1,0:T(8,128)}, f32[2,512,256]{2,1,0:T(8,128)S(1)}, u32[]{:S(2)}, u32[]{:S(2)}) %collective-permute-start.25) | collective-permute-done | bytes 1048608 | tf_op jit(solution)/shard_map/ppermute | solution.py:393
  104.3 1.1 add_bitcast_fusion
  105.5 0.3 collective-permute-start.26
  105.7 0.0 collective-permute-done.24.other_ref
  105.7 13.7 %factor.1 = (f32[4,128,128]{2,1,0:T(8,128)S(1)}, f32[3,128,512]{2,1,0:T(8,128)S(1)}) custom-call(f32[5,128,128]{2,1,0:T(8,128)S(1)} %add.37.mine_ref, f32[5,128,128]{2,1,0:T(8,128)S(1)} %collective-permute-done.24.other_ref), custom_call_target="tpu_custom_call" | custom-call | flops 30000001024 | bytes 3145728 | tf_op jit(solution)/shard_map/factor/pallas_call | solution.py:198
  119.4 0.0 collective-permute-done.26.other_ref
  119.4 3.2 %solve.1 = f32[512,256]{1,0:T(8,128)} custom-call(f32[4,128,128]{2,1,0:T(8,128)S(1)} %get-tuple-element.41.inv_ref, f32[3,128,512]{2,1,0:T(8,128)S(1)} %get-tuple-element.42.upper_ref, f32[2,512,256]{2,1,0:T(8,128)S(1)} %copy-done, f32[2,512,256]{2,1,0:T(8,128)S(1)} %collective-permute-done.25.arrived_ref, f32[512,256]{1,0:T(8,128)S(1)} %collective-permute-done.26.other_ref), custom_call_target="tpu_custom_call" | custom-call | tf_op jit(solution)/shard_map/solve/pallas_call | solution.py:213
  (27 shorter events, 0.2 us)
Async XLA Ops:
  0.9 5.6 %collective-permute-start = (bf16[8,5120]{1,0:T(8,128)(2,1)S(1)}, bf16[8,5120]{1,0:T(8,128)(2,1)S(1)}, u32[]{:S(2)}, u32[]{:S(2)}) collective-permute-start(bf16[8,5120]{1,0:T(8,128)(2,1)S(1)} %pad.4), channel_id=1, source_target_pairs={{0,16},{4,20},{8,24},{12,28},{16,0},{20,4},{24,8},{28,12},{1,17},{... | collective-permute-start | bytes 245768 | tf_op jit(solution)/shard_map/ppermute | solution.py:237
  6.5 9.9 %collective-permute-start.3 = (bf16[16,2560]{1,0:T(8,128)(2,1)S(1)}, bf16[16,2560]{1,0:T(8,128)(2,1)S(1)}, u32[]{:S(2)}, u32[]{:S(2)}) collective-permute-start(bf16[16,2560]{1,0:T(8,128)(2,1)S(1)} %get-tuple-element.47), channel_id=1, source_target_pairs={{0,8},{4,12},{8,0},{12,4},{16,24},{20,28},{24,16},{28,20},{1,9},{5... | collective-permute-start | bytes 245768 | tf_op jit(solution)/shard_map/ppermute | solution.py:232
  9.4 7.1 %collective-permute-start.2 = (bf16[16,2560]{1,0:T(8,128)(2,1)S(1)}, bf16[16,2560]{1,0:T(8,128)(2,1)S(1)}, u32[]{:S(2)}, u32[]{:S(2)}) collective-permute-start(bf16[16,2560]{1,0:T(8,128)(2,1)S(1)} %get-tuple-element.47), channel_id=1, source_target_pairs={{0,12},{4,0},{8,4},{12,8},{16,28},{20,16},{24,20},{28,24},{1,13},{... | collective-permute-start | bytes 245768 | tf_op jit(solution)/shard_map/ppermute | solution.py:232
  10.3 6.2 %collective-permute-start.1 = (bf16[16,2560]{1,0:T(8,128)(2,1)S(1)}, bf16[16,2560]{1,0:T(8,128)(2,1)S(1)}, u32[]{:S(2)}, u32[]{:S(2)}) collective-permute-start(bf16[16,2560]{1,0:T(8,128)(2,1)S(1)} %get-tuple-element.47), channel_id=1, source_target_pairs={{0,4},{4,8},{8,12},{12,0},{16,20},{20,24},{24,28},{28,16},{1,5},{5... | collective-permute-start | bytes 245768 | tf_op jit(solution)/shard_map/ppermute | solution.py:232
  10.9 9.9 %collective-permute-start.12 = (bf16[16,2560]{1,0:T(8,128)(2,1)S(1)}, bf16[16,2560]{1,0:T(8,128)(2,1)S(1)}, u32[]{:S(2)}, u32[]{:S(2)}) collective-permute-start(bf16[16,2560]{1,0:T(8,128)(2,1)S(1)} %get-tuple-element.45), channel_id=1, source_target_pairs={{0,224},{32,0},{64,32},{96,64},{128,96},{160,128},{192,160},{224,1... | collective-permute-start | bytes 245768 | tf_op jit(solution)/shard_map/ppermute | solution.py:228
  16.5 7.0 %collective-permute-start.11 = (bf16[16,2560]{1,0:T(8,128)(2,1)S(1)}, bf16[16,2560]{1,0:T(8,128)(2,1)S(1)}, u32[]{:S(2)}, u32[]{:S(2)}) collective-permute-start(bf16[16,2560]{1,0:T(8,128)(2,1)S(1)} %get-tuple-element.45), channel_id=1, source_target_pairs={{0,32},{32,64},{64,96},{96,128},{128,160},{160,192},{192,224},{224... | collective-permute-start | bytes 245768 | tf_op jit(solution)/shard_map/ppermute | solution.py:228
  16.5 53.9 %copy-start.1 = (bf16[64,2560]{1,0:T(8,128)(2,1)}, bf16[64,2560]{1,0:T(8,128)(2,1)S(1)}, u32[]{:S(2)}) copy-start(bf16[64,2560]{1,0:T(8,128)(2,1)S(1)} %pad_maximum_fusion.refs_0_) | copy-start | bytes 983044
  16.5 25.1 %collective-permute-start.5 = (bf16[64,2560]{1,0:T(8,128)(2,1)S(1)}, bf16[64,2560]{1,0:T(8,128)(2,1)S(1)}, u32[]{:S(2)}, u32[]{:S(2)}) collective-permute-start(bf16[64,2560]{1,0:T(8,128)(2,1)S(1)} %pad_maximum_fusion.refs_0_), channel_id=1, source_target_pairs={{0,224},{32,0},{64,32},{96,64},{128,96},{160,128},{192,160},{224,1... | collective-permute-start | bytes 983048 | tf_op jit(solution)/shard_map/ppermute | solution.py:228
  20.8 20.7 %collective-permute-start.4 = (bf16[64,2560]{1,0:T(8,128)(2,1)S(1)}, bf16[64,2560]{1,0:T(8,128)(2,1)S(1)}, u32[]{:S(2)}, u32[]{:S(2)}) collective-permute-start(bf16[64,2560]{1,0:T(8,128)(2,1)S(1)} %pad_maximum_fusion.refs_0_), channel_id=1, source_target_pairs={{0,32},{32,64},{64,96},{96,128},{128,160},{160,192},{192,224},{224... | collective-permute-start | bytes 983048 | tf_op jit(solution)/shard_map/ppermute | solution.py:228
  20.8 5.5 %collective-permute-start.14 = (bf16[16,2560]{1,0:T(8,128)(2,1)S(1)}, bf16[16,2560]{1,0:T(8,128)(2,1)S(1)}, u32[]{:S(2)}, u32[]{:S(2)}) collective-permute-start(bf16[16,2560]{1,0:T(8,128)(2,1)S(1)} %collective-permute-done.12), channel_id=1, source_target_pairs={{0,224},{32,0},{64,32},{96,64},{128,96},{160,128},{192,160},{224,1... | collective-permute-start | bytes 245768 | tf_op jit(solution)/shard_map/ppermute | solution.py:228
  23.5 6.3 %collective-permute-start.13 = (bf16[16,2560]{1,0:T(8,128)(2,1)S(1)}, bf16[16,2560]{1,0:T(8,128)(2,1)S(1)}, u32[]{:S(2)}, u32[]{:S(2)}) collective-permute-start(bf16[16,2560]{1,0:T(8,128)(2,1)S(1)} %collective-permute-done.11), channel_id=1, source_target_pairs={{0,32},{32,64},{64,96},{96,128},{128,160},{160,192},{192,224},{224... | collective-permute-start | bytes 245768 | tf_op jit(solution)/shard_map/ppermute | solution.py:228
  26.3 7.9 %collective-permute-start.16 = (bf16[16,2560]{1,0:T(8,128)(2,1)S(1)}, bf16[16,2560]{1,0:T(8,128)(2,1)S(1)}, u32[]{:S(2)}, u32[]{:S(2)}) collective-permute-start(bf16[16,2560]{1,0:T(8,128)(2,1)S(1)} %collective-permute-done.14), channel_id=1, source_target_pairs={{0,224},{32,0},{64,32},{96,64},{128,96},{160,128},{192,160},{224,1... | collective-permute-start | bytes 245768 | tf_op jit(solution)/shard_map/ppermute | solution.py:228
  29.7 4.5 %collective-permute-start.15 = (bf16[16,2560]{1,0:T(8,128)(2,1)S(1)}, bf16[16,2560]{1,0:T(8,128)(2,1)S(1)}, u32[]{:S(2)}, u32[]{:S(2)}) collective-permute-start(bf16[16,2560]{1,0:T(8,128)(2,1)S(1)} %collective-permute-done.13), channel_id=1, source_target_pairs={{0,32},{32,64},{64,96},{96,128},{128,160},{160,192},{192,224},{224... | collective-permute-start | bytes 245768 | tf_op jit(solution)/shard_map/ppermute | solution.py:228
  34.2 5.4 %collective-permute-start.17 = (bf16[16,2560]{1,0:T(8,128)(2,1)S(1)}, bf16[16,2560]{1,0:T(8,128)(2,1)S(1)}, u32[]{:S(2)}, u32[]{:S(2)}) collective-permute-start(bf16[16,2560]{1,0:T(8,128)(2,1)S(1)} %collective-permute-done.15), channel_id=1, source_target_pairs={{0,32},{32,64},{64,96},{96,128},{128,160},{160,192},{192,224},{224... | collective-permute-start | bytes 245768 | tf_op jit(solution)/shard_map/ppermute | solution.py:228
  39.6 30.8 %copy-start.4 = (bf16[128,2560]{1,0:T(8,128)(2,1)}, bf16[128,2560]{1,0:T(8,128)(2,1)S(1)}, u32[]{:S(2)}) copy-start(bf16[128,2560]{1,0:T(8,128)(2,1)S(1)} %constant_dynamic-update-slice_fusion.refs_8_) | copy-start | bytes 1966084
  39.6 12.1 %collective-permute-start.19 = (bf16[128,2560]{1,0:T(8,128)(2,1)S(1)}, bf16[128,2560]{1,0:T(8,128)(2,1)S(1)}, u32[]{:S(2)}, u32[]{:S(2)}) collective-permute-start(bf16[128,2560]{1,0:T(8,128)(2,1)S(1)} %constant_dynamic-update-slice_fusion.refs_8_), channel_id=1, source_target_pairs={{0,12},{4,0},{8,4},{12,8},{16,28},{20,16},{24,20},{28,24},{1,13},{... | collective-permute-start | bytes 1966088 | tf_op jit(solution)/shard_map/ppermute | solution.py:232
  41.5 12.9 %collective-permute-start.18 = (bf16[128,2560]{1,0:T(8,128)(2,1)S(1)}, bf16[128,2560]{1,0:T(8,128)(2,1)S(1)}, u32[]{:S(2)}, u32[]{:S(2)}) collective-permute-start(bf16[128,2560]{1,0:T(8,128)(2,1)S(1)} %constant_dynamic-update-slice_fusion.refs_8_), channel_id=1, source_target_pairs={{0,4},{4,8},{8,12},{12,0},{16,20},{20,24},{24,28},{28,16},{1,5},{5... | collective-permute-start | bytes 1966088 | tf_op jit(solution)/shard_map/ppermute | solution.py:232
  41.5 12.9 %copy-start.6 = (bf16[64,2560]{1,0:T(8,128)(2,1)}, bf16[64,2560]{1,0:T(8,128)(2,1)S(1)}, u32[]{:S(2)}) copy-start(bf16[64,2560]{1,0:T(8,128)(2,1)S(1)} %collective-permute-done.4.refs_1_) | copy-start | bytes 983044
  41.5 7.3 %collective-permute-start.6 = (bf16[64,2560]{1,0:T(8,128)(2,1)S(1)}, bf16[64,2560]{1,0:T(8,128)(2,1)S(1)}, u32[]{:S(2)}, u32[]{:S(2)}) collective-permute-start(bf16[64,2560]{1,0:T(8,128)(2,1)S(1)} %collective-permute-done.4.refs_1_), channel_id=1, source_target_pairs={{0,32},{32,64},{64,96},{96,128},{128,160},{160,192},{192,224},{224... | collective-permute-start | bytes 983048 | tf_op jit(solution)/shard_map/ppermute | solution.py:228
  41.6 28.8 %copy-start.5 = (bf16[64,2560]{1,0:T(8,128)(2,1)}, bf16[64,2560]{1,0:T(8,128)(2,1)S(1)}, u32[]{:S(2)}) copy-start(bf16[64,2560]{1,0:T(8,128)(2,1)S(1)} %collective-permute-done.5.refs_2_) | copy-start | bytes 983044
  41.6 7.2 %collective-permute-start.7 = (bf16[64,2560]{1,0:T(8,128)(2,1)S(1)}, bf16[64,2560]{1,0:T(8,128)(2,1)}, u32[]{:S(2)}, u32[]{:S(2)}) collective-permute-start(bf16[64,2560]{1,0:T(8,128)(2,1)S(1)} %collective-permute-done.5.refs_2_), channel_id=1, source_target_pairs={{0,224},{32,0},{64,32},{96,64},{128,96},{160,128},{192,160},{224,1... | collective-permute-start | bytes 983048 | tf_op jit(solution)/shard_map/ppermute | solution.py:228
  48.8 5.8 %copy-start.7 = (bf16[64,2560]{1,0:T(8,128)(2,1)}, bf16[64,2560]{1,0:T(8,128)(2,1)S(1)}, u32[]{:S(2)}) copy-start(bf16[64,2560]{1,0:T(8,128)(2,1)S(1)} %collective-permute-done.6.refs_3_) | copy-start | bytes 983044
  48.8 10.8 %collective-permute-start.8 = (bf16[64,2560]{1,0:T(8,128)(2,1)S(1)}, bf16[64,2560]{1,0:T(8,128)(2,1)}, u32[]{:S(2)}, u32[]{:S(2)}) collective-permute-start(bf16[64,2560]{1,0:T(8,128)(2,1)S(1)} %collective-permute-done.6.refs_3_), channel_id=1, source_target_pairs={{0,32},{32,64},{64,96},{96,128},{128,160},{160,192},{192,224},{224... | collective-permute-start | bytes 983048 | tf_op jit(solution)/shard_map/ppermute | solution.py:228
  48.8 10.8 %collective-permute-start.9 = (bf16[64,2560]{1,0:T(8,128)(2,1)}, bf16[64,2560]{1,0:T(8,128)(2,1)}, u32[]{:S(2)}, u32[]{:S(2)}) collective-permute-start(bf16[64,2560]{1,0:T(8,128)(2,1)} %collective-permute-done.7.refs_4_), channel_id=1, source_target_pairs={{0,224},{32,0},{64,32},{96,64},{128,96},{160,128},{192,160},{224,1... | collective-permute-start | bytes 983048 | tf_op jit(solution)/shard_map/ppermute | solution.py:228
  51.7 18.7 %copy-start.2 = (bf16[128,2560]{1,0:T(8,128)(2,1)}, bf16[128,2560]{1,0:T(8,128)(2,1)S(1)}, u32[]{:S(2)}) copy-start(bf16[128,2560]{1,0:T(8,128)(2,1)S(1)} %collective-permute-done.19.refs_10_) | copy-start | bytes 1966084
  51.8 8.2 %collective-permute-start.21 = (bf16[64,2560]{1,0:T(8,128)(2,1)S(1)}, bf16[64,2560]{1,0:T(8,128)(2,1)}, u32[]{:S(2)}, u32[]{:S(2)}) collective-permute-start(bf16[64,2560]{1,0:T(8,128)(2,1)S(1)} %slice.19), channel_id=1, source_target_pairs={{0,12},{4,0},{8,4},{12,8},{16,28},{20,16},{24,20},{28,24},{1,13},{... | collective-permute-start | bytes 983048 | tf_op jit(solution)/shard_map/ppermute | solution.py:232
  54.4 16.0 %copy-start.3 = (bf16[128,2560]{1,0:T(8,128)(2,1)}, bf16[128,2560]{1,0:T(8,128)(2,1)S(1)}, u32[]{:S(2)}) copy-start(bf16[128,2560]{1,0:T(8,128)(2,1)S(1)} %collective-permute-done.18.refs_9_) | copy-start | bytes 1966084
  54.5 8.3 %collective-permute-start.20 = (bf16[64,2560]{1,0:T(8,128)(2,1)S(1)}, bf16[64,2560]{1,0:T(8,128)(2,1)}, u32[]{:S(2)}, u32[]{:S(2)}) collective-permute-start(bf16[64,2560]{1,0:T(8,128)(2,1)S(1)} %slice.18), channel_id=1, source_target_pairs={{0,4},{4,8},{8,12},{12,0},{16,20},{20,24},{24,28},{28,16},{1,5},{5... | collective-permute-start | bytes 983048 | tf_op jit(solution)/shard_map/ppermute | solution.py:232
  59.6 10.9 %collective-permute-start.10 = (bf16[64,2560]{1,0:T(8,128)(2,1)}, bf16[64,2560]{1,0:T(8,128)(2,1)}, u32[]{:S(2)}, u32[]{:S(2)}) collective-permute-start(bf16[64,2560]{1,0:T(8,128)(2,1)} %collective-permute-done.8.refs_5_), channel_id=1, source_target_pairs={{0,32},{32,64},{64,96},{96,128},{128,160},{160,192},{192,224},{224... | collective-permute-start | bytes 983048 | tf_op jit(solution)/shard_map/ppermute | solution.py:228
  77.1 10.7 %collective-permute-start.22 = (f32[5,128,128]{2,1,0:T(8,128)S(1)}, f32[5,128,128]{2,1,0:T(8,128)S(1)}, u32[]{:S(2)}, u32[]{:S(2)}) collective-permute-start(f32[5,128,128]{2,1,0:T(8,128)S(1)} %dynamic-slice_bitcast_fusion), channel_id=1, source_target_pairs={{0,1},{1,0},{2,3},{3,2},{4,5},{5,4},{6,7},{7,6},{8,9},{9,8},{10,11... | collective-permute-start | bytes 983048 | tf_op jit(solution)/shard_map/ppermute | solution.py:393
  88.9 11.7 %collective-permute-start.23 = (f32[5,128,128]{2,1,0:T(8,128)S(1)}, f32[5,128,128]{2,1,0:T(8,128)S(1)}, u32[]{:S(2)}, u32[]{:S(2)}) collective-permute-start(f32[5,128,128]{2,1,0:T(8,128)S(1)} %bitcast_add_fusion), channel_id=1, source_target_pairs={{0,2},{2,0},{1,3},{3,1},{4,6},{6,4},{5,7},{7,5},{8,10},{10,8},{9,1... | collective-permute-start | bytes 983048 | tf_op jit(solution)/shard_map/ppermute | solution.py:397
  100.6 3.7 %collective-permute-start.25 = (f32[2,512,256]{2,1,0:T(8,128)}, f32[2,512,256]{2,1,0:T(8,128)S(1)}, u32[]{:S(2)}, u32[]{:S(2)}) collective-permute-start(f32[2,512,256]{2,1,0:T(8,128)} %get-tuple-element.44), channel_id=1, source_target_pairs={{0,1},{1,0},{2,3},{3,2},{4,5},{5,4},{6,7},{7,6},{8,9},{9,8},{10,11... | collective-permute-start | bytes 3145736 | tf_op jit(solution)/shard_map/ppermute | solution.py:393
  101.4 4.3 %collective-permute-start.24 = (f32[5,128,128]{2,1,0:T(8,128)S(1)}, f32[5,128,128]{2,1,0:T(8,128)S(1)}, u32[]{:S(2)}, u32[]{:S(2)}) collective-permute-start(f32[5,128,128]{2,1,0:T(8,128)S(1)} %add.37.mine_ref), channel_id=1, source_target_pairs={{0,1},{1,0},{2,3},{3,2},{4,5},{5,4},{6,7},{7,6},{8,9},{9,8},{10,11... | collective-permute-start | bytes 983048 | tf_op jit(solution)/shard_map/ppermute | solution.py:393
  105.4 14.0 %copy-start = (f32[2,512,256]{2,1,0:T(8,128)S(1)}, f32[2,512,256]{2,1,0:T(8,128)}, u32[]{:S(2)}) copy-start(f32[2,512,256]{2,1,0:T(8,128)} %get-tuple-element.43.keep_ref) | copy-start | bytes 3145732
  105.5 13.9 %collective-permute-start.26 = (f32[512,256]{1,0:T(8,128)S(1)}, f32[512,256]{1,0:T(8,128)S(1)}, u32[]{:S(2)}, u32[]{:S(2)}) collective-permute-start(f32[512,256]{1,0:T(8,128)S(1)} %add_bitcast_fusion), channel_id=1, source_target_pairs={{0,2},{2,0},{1,3},{3,1},{4,6},{6,4},{5,7},{7,5},{8,10},{10,8},{9,1... | collective-permute-start | bytes 1572872 | tf_op jit(solution)/shard_map/ppermute | solution.py:397

commit v3 on v2

--- a/solution.py
+++ b/solution.py
@@ -10,8 +10,9 @@
 ROW0 = (((0,), (0,)), ((), ()))
 NB = 128
 PANEL = 512
-HALF_K = 2560
-CHUNK_K = 512
+FIRST_K = 2432
+SECOND_K = 2688
+CHUNK_K = 1024
 HALVES = (((0, 0), (0, 1), (0, 2), (0, 3), (3, 3)), ((1, 1), (1, 2), (1, 3), (2, 2), (2, 3)))
 
 CORE_SWAP = [(0, 1), (1, 0), (2, 3), (3, 2)]
@@ -232,161 +233,282 @@
     return lax.ppermute(v, "pcol", x_shift(k))
 
 
+def after(v, *others):
+    return lax.optimization_barrier((v,) + others)[0]
+
+
 def gather_panel(panel):
-    own = jnp.pad(panel.T, ((0, 0), (0, 2 * HALF_K - panel.shape[0])))
+    own = panel.T
     far = lax.ppermute(own, "pcol", Y_SWAP)
     first = lax.axis_index("pcol") < 4
     pair = jnp.where(first, jnp.concatenate([own, far], 0), jnp.concatenate([far, own], 0))
-    left, right = pair[:, :HALF_K], pair[:, HALF_K:]
+    left = pair[:, :FIRST_K]
+    right = jnp.pad(pair[:, FIRST_K:], ((0, 0), (0, FIRST_K + SECOND_K - panel.shape[0])))
 
     x_steps = (0, -1, 1, 2)
     plane = jnp.concatenate([left, along_x(1, left), along_x(-1, left), along_x(2, left)], 0)
-    pieces, places = [plane], [(0, 16 * k, 0, 0, s) for k, s in enumerate(x_steps)]
-    up = down = plane
-    for s in range(1, 5):
-        up = along_z(1, up)
-        places += [(len(pieces), 16 * k, 0, -s, t) for k, t in enumerate(x_steps)]
-        pieces.append(up)
-        if s < 4:
-            down = along_z(-1, down)
-            places += [(len(pieces), 16 * k, 0, s, t) for k, t in enumerate(x_steps)]
-            pieces.append(down)
-
-    z_steps, column = [0], [right]
-    up = down = right
-    for s in range(1, 5):
-        up = along_z(1, up)
-        z_steps.append(-s)
-        column.append(up)
-        if s < 4:
-            down = along_z(-1, down)
-            z_steps.append(s)
-            column.append(down)
+    planes, plane_z = [plane], [0]
+    column, column_z = [right], [0]
+
+    def turn(pieces, steps, s, *ties):
+        up, down = pieces[-2:] if s > 1 else pieces * 2
+        pieces += [along_z(1, after(up, *ties)), along_z(-1, after(down, *ties))]
+        steps += [-s, s]
+
+    turn(column, column_z, 1)
+    turn(planes, plane_z, 1)
+    turn(column, column_z, 2)
+    turn(column, column_z, 3, *planes[1:3])
+    column_z.append(4)
+    column.append(along_z(1, column[-2]))
+    turn(planes, plane_z, 2)
     column = jnp.concatenate(column, 0)
     half = column.shape[0] // 2
-    up, down = along_x(1, column), along_x(-1, column)
-    for piece, t, r in (
+    column = after(column, *planes[3:5])
+    x_up, x_down = along_x(1, column), along_x(-1, column)
+    turn(planes, plane_z, 3)
+    x_far = (
+        along_x(1, after(x_up[:half], *planes[5:7])),
+        along_x(-1, after(x_down[half:], *planes[5:7])),
+    )
+    planes.append(along_z(1, planes[-2]))
+    plane_z.append(4)
+
+    plane_places = [
+        (n, 16 * k, dz, dx) for n, dz in enumerate(plane_z) for k, dx in enumerate(x_steps)
+    ]
+    columns, column_places = [], []
+    for piece, dx, units in (
         (column, 0, range(8)),
-        (up, -1, range(8)),
-        (down, 1, range(8)),
-        (along_x(1, up[:half]), 2, range(4)),
-        (along_x(-1, down[half:]), 2, range(4, 8)),
+        (x_up, -1, range(8)),
+        (x_down, 1, range(8)),
+        (x_far[0], 2, range(4)),
+        (x_far[1], 2, range(4, 8)),
     ):
-        places += [(len(pieces), 16 * k, 1, z_steps[m], t) for k, m in enumerate(r)]
-        pieces.append(piece)
-    return pieces, places
-
-
-def load_panel(places, piece_refs, panel_ref, sems):
+        column_places += [(len(columns), 16 * k, column_z[m], dx) for k, m in enumerate(units)]
+        columns.append(piece)
+    return (planes, plane_places), (columns, column_places)
+
+
+def chunks(depth):
+    return [slice(k, min(k + CHUNK_K, depth)) for k in range(0, depth, CHUNK_K)]
+
+
+def stream(places, piece_refs, panel_ref, sems, window=None):
     z = lax.axis_index("prow")
     x = lax.axis_index("pcol") % 4
-    for piece, row, half, dz, dx in places:
-        to = lax.rem(z + dz + 8, 8) * 64 + lax.rem(x + dx + 4, 4) * 16
-        pltpu.make_async_copy(
-            piece_refs[piece].at[pl.ds(row, 16), :],
-            panel_ref.at[half, pl.ds(pl.multiple_of(to, 16), 16), :],
-            sems.at[half],
-        ).start()
-
-
-def wait_panel(panel_ref, sems, half):
-    pltpu.make_async_copy(panel_ref.at[half], panel_ref.at[half], sems.at[half]).wait()
-
-
-def panel_gram_kernel(places, pieces, *refs):
-    piece_refs, (out_ref, panel_ref, sems) = refs[:pieces], refs[pieces:]
-    load_panel(places, piece_refs, panel_ref, sems)
-    strips = [None, None]
-    for half in range(2):
-        wait_panel(panel_ref, sems, half)
-        for s in range(2):
-            part = lax.dot_general(
-                panel_ref[half, s * 256 : (s + 1) * 256, :],
-                panel_ref[half, s * 256 :, :],
-                (((1,), (1,)), ((), ())),
-                preferred_element_type=F32,
-            )
-            strips[s] = part if half == 0 else strips[s] + part
+    units = [
+        (piece, row, pl.multiple_of(lax.rem(z + dz + 8, 8) * 64 + lax.rem(x + dx + 4, 4) * 16, 16))
+        for piece, row, dz, dx in places
+    ]
+    parts = chunks(panel_ref.shape[1])
+
+    def window_copy(c):
+        orbitals_ref, start, window_ref, window_sems = window
+        first = parts[c].start
+        size = min(parts[c].stop, orbitals_ref.shape[0] - start) - first
+        return pltpu.make_async_copy(
+            orbitals_ref.at[pl.ds(start + first, size), :],
+            window_ref.at[pl.ds(first, size), :],
+            window_sems.at[c],
+        )
+
+    def start_chunk(c):
+        for piece, row, to in units:
+            pltpu.make_async_copy(
+                piece_refs[piece].at[pl.ds(row, 16), parts[c]],
+                panel_ref.at[pl.ds(to, 16), parts[c]],
+                sems.at[c],
+            ).start()
+        if window is not None:
+            window_copy(c).start()
+
+    for c in range(min(2, len(parts))):
+        start_chunk(c)
+    for c, part in enumerate(parts):
+        here = panel_ref.at[:, part]
+        pltpu.make_async_copy(here, here, sems.at[c]).wait()
+        if window is not None:
+            window_copy(c).wait()
+        if c + 2 < len(parts):
+            start_chunk(c + 2)
+        yield c, part
+
+
+def add_rows(panel_ref, window_ref, part, total_ref, started):
+    quarter = total_ref.shape[2]
+    gram = jnp.dot(panel_ref[:, part], window_ref[part, :], preferred_element_type=F32)
+    for n in range(4):
+        value = gram[:, n * quarter : (n + 1) * quarter]
+        total_ref[n] = total_ref[n] + value if started else value
+
+
+def panel_strips(panel_ref, part, before):
+    strips = []
+    for s in range(2):
+        strip = lax.dot_general(
+            panel_ref[s * 256 : (s + 1) * 256, part],
+            panel_ref[s * 256 :, part],
+            (((1,), (1,)), ((), ())),
+            preferred_element_type=F32,
+        )
+        strips.append(strip if before is None else before[s] + strip)
+    return strips
+
+
+def put_blocks(strips, out_ref, before_ref=None):
     for h, blocks in enumerate(HALVES):
         for k, (i, j) in enumerate(blocks):
             s = i // 2
-            out_ref[h, k] = strips[s][
-                (i - 2 * s) * NB : (i - 2 * s + 1) * NB, (j - 2 * s) * NB : (j - 2 * s + 1) * NB
-            ]
-
-
-def panel_gram(pieces, places):
-    return pl.pallas_call(
-        lambda *refs: panel_gram_kernel(places, len(pieces), *refs),
-        in_specs=[pl.BlockSpec(memory_space=pl.ANY)] * len(pieces),
-        out_shape=jax.ShapeDtypeStruct((2, 5, NB, NB), F32),
-        scratch_shapes=[pltpu.VMEM((2, PANEL, HALF_K), jnp.bfloat16), pltpu.SemaphoreType.DMA((2,))],
-        compiler_params=pltpu.CompilerParams(vmem_limit_bytes=60 << 20),
-        cost_estimate=pl.CostEstimate(flops=3_000_000_000, bytes_accessed=8 << 20, transcendentals=0),
-        name="panel_gram",
-    )(*pieces)
-
-
-def row_gram_kernel(places, pieces, *refs):
-    piece_refs = refs[:pieces]
-    orbitals_ref, give_ref, keep_ref, panel_ref, window_ref, total_ref, sems, window_sems = refs[pieces:]
+            i, j = i - 2 * s, j - 2 * s
+            value = strips[s][i * NB : (i + 1) * NB, j * NB : (j + 1) * NB]
+            out_ref[h, k] = value if before_ref is None else before_ref[h, k] + value
+
+
+def first_kernel(places, pieces, *refs):
+    orbitals_ref, panel_out, rows_out = refs[pieces : pieces + 3]
+    panel_ref, window_ref, total_ref, block_ref, sems, window_sems, out_sems = refs[pieces + 3 :]
+    window = (orbitals_ref, 0, window_ref, window_sems)
+    strips = None
+    for c, part in stream(places, refs[:pieces], panel_ref, sems, window):
+        add_rows(panel_ref, window_ref, part, total_ref, c > 0)
+        if part.stop == FIRST_K:
+            send_rows = pltpu.make_async_copy(total_ref, rows_out, out_sems.at[0])
+            send_rows.start()
+        strips = panel_strips(panel_ref, part, strips)
+    put_blocks(strips, block_ref)
+    send_panel = pltpu.make_async_copy(block_ref, panel_out, out_sems.at[1])
+    send_panel.start()
+    send_rows.wait()
+    send_panel.wait()
+
+
+def panel_kernel(places, pieces, *refs):
+    before_ref, give_ref, keep_ref = refs[pieces : pieces + 3]
+    panel_ref, total_ref, start_ref, sems, out_sems = refs[pieces + 3 :]
     core = lax.axis_index("orb") % 2
-    load_panel(places, piece_refs, panel_ref, sems)
-    rows = orbitals_ref.shape[0]
-    window_ref[rows:, :] = jnp.zeros((2 * HALF_K - rows, orbitals_ref.shape[1]), jnp.bfloat16)
-    copies = []
-    for k in range(0, rows, CHUNK_K):
-        part = pl.ds(k, min(CHUNK_K, rows - k))
-        copies.append(
-            pltpu.make_async_copy(
-                orbitals_ref.at[part, :], window_ref.at[part, :], window_sems.at[len(copies)]
-            )
-        )
-        copies[-1].start()
-    for k, copy in enumerate(copies):
-        half, at = divmod(k * CHUNK_K, HALF_K)
-        if at == 0:
-            wait_panel(panel_ref, sems, half)
-        copy.wait()
-        part = jnp.dot(
-            panel_ref[half, :, at : at + CHUNK_K],
-            window_ref[k * CHUNK_K : (k + 1) * CHUNK_K, :],
+    strips = None
+    for c, part in stream(places, refs[:pieces], panel_ref, sems):
+        if c == 0:
+            before = pltpu.make_async_copy(before_ref, start_ref, out_sems.at[2])
+            before.start()
+        strips = panel_strips(panel_ref, part, strips)
+    before.wait()
+    put_blocks(strips, total_ref, start_ref)
+    sends = [
+        pltpu.make_async_copy(total_ref.at[1 - core], give_ref, out_sems.at[0]),
+        pltpu.make_async_copy(total_ref.at[core], keep_ref, out_sems.at[1]),
+    ]
+    for send in sends:
+        send.start()
+    for send in sends:
+        send.wait()
+
+
+def rows_kernel(places, pieces, *refs):
+    orbitals_ref, before_ref, give_ref, keep_ref = refs[pieces : pieces + 4]
+    panel_ref, window_ref, total_ref, start_ref, sems, window_sems, out_sems = refs[pieces + 4 :]
+    core = lax.axis_index("orb") % 2
+    quarter = total_ref.shape[2]
+    rows = orbitals_ref.shape[0] - FIRST_K
+    window_ref[rows:, :] = jnp.zeros((SECOND_K - rows, orbitals_ref.shape[1]), jnp.bfloat16)
+    window = (orbitals_ref, FIRST_K, window_ref, window_sems)
+    for c, part in stream(places, refs[:pieces], panel_ref, sems, window):
+        if c == 0:
+            before = pltpu.make_async_copy(before_ref, start_ref, out_sems.at[4])
+            before.start()
+        if part.stop < SECOND_K:
+            add_rows(panel_ref, window_ref, part, total_ref, c > 0)
+    before.wait()
+    for n in range(4):
+        gram = jnp.dot(
+            panel_ref[:, part],
+            window_ref[part, n * quarter : (n + 1) * quarter],
             preferred_element_type=F32,
         )
-        quarter = part.shape[1] // 4
-        for n in range(4):
-            value = part[:, n * quarter : (n + 1) * quarter]
-            total_ref[n] = value if k == 0 else total_ref[n] + value
-    sends = []
-    for c in range(2):
-        for ref, which in ((give_ref, 1 - core), (keep_ref, core)):
-            sends.append(
-                pltpu.make_async_copy(total_ref.at[2 * c + which], ref.at[c], window_sems.at[len(sends)])
-            )
-            sends[-1].start()
+        total_ref[n] = total_ref[n] + (start_ref[n] + gram)
+        if n % 2:
+            sends = sends if n > 1 else []
+            for ref, which in ((give_ref, 1 - core), (keep_ref, core)):
+                sends.append(
+                    pltpu.make_async_copy(
+                        total_ref.at[n - 1 + which], ref.at[n // 2], out_sems.at[len(sends)]
+                    )
+                )
+                sends[-1].start()
     for send in sends:
         send.wait()
 
 
-def row_gram(pieces, places, orbitals):
-    rows, columns = orbitals.shape
+HBM = pl.BlockSpec(memory_space=pl.ANY)
+DMA = pltpu.SemaphoreType.DMA
+ROOMY = pltpu.CompilerParams(vmem_limit_bytes=60 << 20)
+
+
+def first_grams(pieces, places, orbitals):
+    columns, count = orbitals.shape[1], len(chunks(FIRST_K))
+    blocks, totals = (2, 5, NB, NB), (4, PANEL, columns // 4)
+    return pl.pallas_call(
+        lambda *refs: first_kernel(places, len(pieces), *refs),
+        in_specs=[HBM] * (len(pieces) + 1),
+        out_specs=[HBM] * 2,
+        out_shape=(jax.ShapeDtypeStruct(blocks, F32), jax.ShapeDtypeStruct(totals, F32)),
+        scratch_shapes=[
+            pltpu.VMEM((PANEL, FIRST_K), jnp.bfloat16),
+            pltpu.VMEM((FIRST_K, columns), jnp.bfloat16),
+            pltpu.VMEM(totals, F32),
+            pltpu.VMEM(blocks, F32),
+            DMA((count,)),
+            DMA((count,)),
+            DMA((2,)),
+        ],
+        compiler_params=ROOMY,
+        cost_estimate=pl.CostEstimate(flops=5_000_000_000, bytes_accessed=12 << 20, transcendentals=0),
+        name="first_grams",
+    )(*pieces, orbitals)
+
+
+def panel_gram(pieces, places, before):
+    out = jax.ShapeDtypeStruct((5, NB, NB), F32)
+    return pl.pallas_call(
+        lambda *refs: panel_kernel(places, len(pieces), *refs),
+        in_specs=[HBM] * (len(pieces) + 1),
+        out_specs=[HBM] * 2,
+        out_shape=(out, out),
+        scratch_shapes=[
+            pltpu.VMEM((PANEL, SECOND_K), jnp.bfloat16),
+            pltpu.VMEM((2, 5, NB, NB), F32),
+            pltpu.VMEM((2, 5, NB, NB), F32),
+            DMA((len(chunks(SECOND_K)),)),
+            DMA((3,)),
+        ],
+        compiler_params=ROOMY,
+        cost_estimate=pl.CostEstimate(flops=1_500_000_000, bytes_accessed=4 << 20, transcendentals=0),
+        name="panel_gram",
+    )(*pieces, before)
+
+
+def row_gram(pieces, places, orbitals, before):
+    columns, count = orbitals.shape[1], len(chunks(SECOND_K))
     out = jax.ShapeDtypeStruct((2, PANEL, columns // 4), F32)
     return pl.pallas_call(
-        lambda *refs: row_gram_kernel(places, len(pieces), *refs),
-        in_specs=[pl.BlockSpec(memory_space=pl.ANY)] * (len(pieces) + 1),
-        out_specs=[pl.BlockSpec(memory_space=pl.ANY)] * 2,
+        lambda *refs: rows_kernel(places, len(pieces), *refs),
+        in_specs=[HBM] * (len(pieces) + 2),
+        out_specs=[HBM] * 2,
         out_shape=(out, out),
         scratch_shapes=[
-            pltpu.VMEM((2, PANEL, HALF_K), jnp.bfloat16),
-            pltpu.VMEM((2 * HALF_K, columns), jnp.bfloat16),
+            pltpu.VMEM((PANEL, SECOND_K), jnp.bfloat16),
+            pltpu.VMEM((SECOND_K, columns), jnp.bfloat16),
             pltpu.VMEM((4, PANEL, columns // 4), F32),
-            pltpu.SemaphoreType.DMA((2,)),
-            pltpu.SemaphoreType.DMA((2 * HALF_K // CHUNK_K,)),
+            pltpu.VMEM((4, PANEL, columns // 4), F32),
+            DMA((count,)),
+            DMA((count,)),
+            DMA((5,)),
         ],
-        compiler_params=pltpu.CompilerParams(vmem_limit_bytes=60 << 20),
-        cost_estimate=pl.CostEstimate(flops=6_000_000_000, bytes_accessed=17 << 20, transcendentals=0),
+        compiler_params=ROOMY,
+        cost_estimate=pl.CostEstimate(flops=4_000_000_000, bytes_accessed=12 << 20, transcendentals=0),
         name="row_gram",
-    )(*pieces, orbitals)
+    )(*pieces, orbitals, before)
 
 
 def swap_cores(v):
@@ -402,15 +524,14 @@
 
 
 def on_device(panel_orbitals, orbitals):
-    core = lax.axis_index("orb") % 2
     chip = lax.axis_index("orb") // 2
-    pieces, places = gather_panel(panel_orbitals)
-
-    panel = panel_gram(pieces, places)
-    half = pick(panel, core) + swap_cores(pick(panel, 1 - core))
-    half, pieces = lax.optimization_barrier((half, pieces))
+    (first, first_places), (second, second_places) = gather_panel(panel_orbitals)
+    panel, rows = first_grams(first, first_places, orbitals)
+    give, keep = panel_gram(second, second_places, panel)
+    half = keep + swap_cores(give)
+    half, second = lax.optimization_barrier((half, second))
     half = half + swap_chips(half)
-    give, keep = row_gram(pieces, places, orbitals)
+    give, keep = row_gram(second, second_places, orbitals, rows)
     half, give = lax.optimization_barrier((half, give))
     arrived = swap_cores(give)
     other = swap_chips(pick(keep, 1 - chip) + pick(arrived, 1 - chip))

time: 123 us -> 114 us (0.927)
  waiting for transfers between devices: 39 us -> 29.4 us
  Pallas kernels: 32.8 us -> 36 us
  starting transfers between devices: 46.3 us -> 43.3 us
    ppermute x14, waiting for transfers between devices: 29.8 us -> 19.3 us  [along_z(): return lax.ppermute(v, 'prow', z_shift(k))]
    pallas_call x2 -> x3, Pallas kernels: 15.9 us -> 19.2 us  [the longest x1 8.39 us: first_grams(): pl.pallas_call(lambda *refs: first_kernel(places, len(pieces), *refs), in...]
    ppermute x14, starting transfers between devices: 21.6 us -> 19.3 us  [along_z(): return lax.ppermute(v, 'prow', z_shift(k))]
    ppermute x7, starting transfers between devices: 8.98 us -> 7.5 us  [along_x(): return lax.ppermute(v, 'pcol', x_shift(k))]
  transfers between devices with their start and end apart: 27 -> 27, of which waited for: 11 -> 11; matrix products, arithmetic and copies ran while one was open for 1% -> 1% of each run, Pallas kernels for 20% -> 25%
where the time goes in v3:
time: 114 us; the launch traced here: 113 us
  starting transfers between devices  43.3 us (38%)
  Pallas kernels  36 us (32%)
  waiting for transfers between devices  29.4 us (26%)
  other arithmetic  3.2 us (3%)
    ppermute x14, starting transfers between devices, along_z(): return lax.ppermute(v, 'prow', z_shift(k))  19.3 us
    ppermute x14, waiting for transfers between devices, along_z(): return lax.ppermute(v, 'prow', z_shift(k))  19.3 us
    pallas_call x1, Pallas kernels, factorise(): pl.pallas_call(factor_kernel, out_shape=(jax.ShapeDtypeStruct((blocks, NB...  13.6 us
    ppermute x3, starting transfers between devices, swap_cores(): return lax.ppermute(v, 'orb', CORE_SWAP)  9.96 us
    pallas_call x1, Pallas kernels, first_grams(): pl.pallas_call(lambda *refs: first_kernel(places, len(pieces), *refs), in...  8.39 us
    ppermute x7, starting transfers between devices, along_x(): return lax.ppermute(v, 'pcol', x_shift(k))  7.5 us
    pallas_call x1, Pallas kernels, row_gram(): pl.pallas_call(lambda *refs: rows_kernel(places, len(pieces), *refs), in_...  6.84 us
    ppermute x3, waiting for transfers between devices, swap_cores(): return lax.ppermute(v, 'orb', CORE_SWAP)  4.33 us
  transfers between devices with their start and end apart: 27, of which 11 were waited for; matrix products, arithmetic and copies ran while one was open for 1% of the time, Pallas kernels for 25%

profile of v3, /device:TPU:1, one launch (start us, length us, event | category | flops | bytes accessed | tf_op | source)
XLA Modules:
  0.0 113.4 jit_solution(8658648683983241269)
XLA Ops:
  0.0 3.7 %collective-permute-start = (bf16[8,5000]{1,0:T(8,128)(2,1)}, bf16[8,5000]{1,0:T(8,128)(2,1)S(1)}, u32[]{:S(2)}, u32[]{:S(2)}) collective-permute-start(bf16[8,5000]{1,0:T(8,128)(2,1)} %bitcast.3), channel_id=1, source_target_pairs={{0,16},{4,20},{8,24},{12,28},{16,0},{20,4},{24,8},{28,12},{1,17},{... | collective-permute-start | bytes 240008 | tf_op jit(solution)/shard_map/ppermute | solution.py:242
  3.7 2.0 %collective-permute-done = bf16[8,5000]{1,0:T(8,128)(2,1)S(1)} collective-permute-done((bf16[8,5000]{1,0:T(8,128)(2,1)}, bf16[8,5000]{1,0:T(8,128)(2,1)S(1)}, u32[]{:S(2)}, u32[]{:S(2)}) %collective-permute-start) | collective-permute-done | bytes 80032 | tf_op jit(solution)/shard_map/ppermute | solution.py:242
  5.8 1.0 maximum_select_fusion
  6.8 1.3 %collective-permute-start.5 = (bf16[16,2432]{1,0:T(8,128)(2,1)S(1)}, bf16[16,2432]{1,0:T(8,128)(2,1)S(1)}, u32[]{:S(2)}, u32[]{:S(2)}) collective-permute-start(bf16[16,2432]{1,0:T(8,128)(2,1)S(1)} %slice.17), channel_id=1, source_target_pairs={{0,4},{4,8},{8,12},{12,0},{16,20},{20,24},{24,28},{28,16},{1,5},{5... | collective-permute-start | bytes 233480 | tf_op jit(solution)/shard_map/ppermute | solution.py:233
  8.1 1.4 %collective-permute-start.6 = (bf16[16,2432]{1,0:T(8,128)(2,1)S(1)}, bf16[16,2432]{1,0:T(8,128)(2,1)S(1)}, u32[]{:S(2)}, u32[]{:S(2)}) collective-permute-start(bf16[16,2432]{1,0:T(8,128)(2,1)S(1)} %slice.17), channel_id=1, source_target_pairs={{0,12},{4,0},{8,4},{12,8},{16,28},{20,16},{24,20},{28,24},{1,13},{... | collective-permute-start | bytes 233480 | tf_op jit(solution)/shard_map/ppermute | solution.py:233
  9.6 1.6 %collective-permute-start.7 = (bf16[16,2432]{1,0:T(8,128)(2,1)S(1)}, bf16[16,2432]{1,0:T(8,128)(2,1)S(1)}, u32[]{:S(2)}, u32[]{:S(2)}) collective-permute-start(bf16[16,2432]{1,0:T(8,128)(2,1)S(1)} %slice.17), channel_id=1, source_target_pairs={{0,8},{4,12},{8,0},{12,4},{16,24},{20,28},{24,16},{28,20},{1,9},{5... | collective-permute-start | bytes 233480 | tf_op jit(solution)/shard_map/ppermute | solution.py:233
  11.2 1.7 %collective-permute-start.1 = (bf16[16,2688]{1,0:T(8,128)(2,1)S(1)}, bf16[16,2688]{1,0:T(8,128)(2,1)S(1)}, u32[]{:S(2)}, u32[]{:S(2)}) collective-permute-start(bf16[16,2688]{1,0:T(8,128)(2,1)S(1)} %get-tuple-element.47), channel_id=1, source_target_pairs={{0,32},{32,64},{64,96},{96,128},{128,160},{160,192},{192,224},{224... | collective-permute-start | bytes 258056 | tf_op jit(solution)/shard_map/ppermute | solution.py:229
  12.9 4.0 %collective-permute-start.2 = (bf16[16,2688]{1,0:T(8,128)(2,1)S(1)}, bf16[16,2688]{1,0:T(8,128)(2,1)S(1)}, u32[]{:S(2)}, u32[]{:S(2)}) collective-permute-start(bf16[16,2688]{1,0:T(8,128)(2,1)S(1)} %get-tuple-element.47), channel_id=1, source_target_pairs={{0,224},{32,0},{64,32},{96,64},{128,96},{160,128},{192,160},{224,1... | collective-permute-start | bytes 258056 | tf_op jit(solution)/shard_map/ppermute | solution.py:229
  16.9 0.0 collective-permute-done.5
  16.9 0.0 collective-permute-done.6
  16.9 0.0 collective-permute-done.7
  17.0 0.0 copy-start.6
  17.0 0.1 collective-permute-start.8
  17.1 3.6 %collective-permute-start.9 = (bf16[64,2432]{1,0:T(8,128)(2,1)S(1)}, bf16[64,2432]{1,0:T(8,128)(2,1)S(1)}, u32[]{:S(2)}, u32[]{:S(2)}) collective-permute-start(bf16[64,2432]{1,0:T(8,128)(2,1)S(1)} %pad_maximum_fusion.refs_0_), channel_id=1, source_target_pairs={{0,224},{32,0},{64,32},{96,64},{128,96},{160,128},{192,160},{224,1... | collective-permute-start | bytes 933896 | tf_op jit(solution)/shard_map/ppermute | solution.py:229
  20.7 0.0 collective-permute-done.1
  20.7 0.0 collective-permute-start.3
  20.7 0.0 collective-permute-done.2
  20.7 2.7 %collective-permute-start.4 = (bf16[16,2688]{1,0:T(8,128)(2,1)S(1)}, bf16[16,2688]{1,0:T(8,128)(2,1)S(1)}, u32[]{:S(2)}, u32[]{:S(2)}) collective-permute-start(bf16[16,2688]{1,0:T(8,128)(2,1)S(1)} %collective-permute-done.2), channel_id=1, source_target_pairs={{0,224},{32,0},{64,32},{96,64},{128,96},{160,128},{192,160},{224,1... | collective-permute-start | bytes 258056 | tf_op jit(solution)/shard_map/ppermute | solution.py:229
  23.4 3.7 %collective-permute-done.3 = bf16[16,2688]{1,0:T(8,128)(2,1)S(1)} collective-permute-done((bf16[16,2688]{1,0:T(8,128)(2,1)S(1)}, bf16[16,2688]{1,0:T(8,128)(2,1)S(1)}, u32[]{:S(2)}, u32[]{:S(2)}) %collective-permute-start.3) | collective-permute-done | bytes 86048 | tf_op jit(solution)/shard_map/ppermute | solution.py:229
  27.1 0.0 collective-permute-done.8.refs_1_
  27.1 0.0 collective-permute-done.9.refs_2_
  27.2 0.1 collective-permute-start.10
  27.2 0.0 collective-permute-done.4
  27.3 0.5 collective-permute-start.13
  27.8 2.5 %collective-permute-start.14 = (bf16[64,2432]{1,0:T(8,128)(2,1)S(1)}, bf16[64,2432]{1,0:T(8,128)(2,1)S(1)}, u32[]{:S(2)}, u32[]{:S(2)}) collective-permute-start(bf16[64,2432]{1,0:T(8,128)(2,1)S(1)} %collective-permute-done.9.refs_2_), channel_id=1, source_target_pairs={{0,224},{32,0},{64,32},{96,64},{128,96},{160,128},{192,160},{224,1... | collective-permute-start | bytes 933896 | tf_op jit(solution)/shard_map/ppermute | solution.py:229
  30.3 1.4 %collective-permute-start.11 = (bf16[16,2688]{1,0:T(8,128)(2,1)S(1)}, bf16[16,2688]{1,0:T(8,128)(2,1)S(1)}, u32[]{:S(2)}, u32[]{:S(2)}) collective-permute-start(bf16[16,2688]{1,0:T(8,128)(2,1)S(1)} %collective-permute-done.4), channel_id=1, source_target_pairs={{0,224},{32,0},{64,32},{96,64},{128,96},{160,128},{192,160},{224,1... | collective-permute-start | bytes 258056 | tf_op jit(solution)/shard_map/ppermute | solution.py:229
  31.7 0.1 collective-permute-done.10
  31.8 0.0 collective-permute-start.12
  31.8 4.5 %collective-permute-done.11 = bf16[16,2688]{1,0:T(8,128)(2,1)S(1)} collective-permute-done((bf16[16,2688]{1,0:T(8,128)(2,1)S(1)}, bf16[16,2688]{1,0:T(8,128)(2,1)S(1)}, u32[]{:S(2)}, u32[]{:S(2)}) %collective-permute-start.11) | collective-permute-done | bytes 86048 | tf_op jit(solution)/shard_map/ppermute | solution.py:229
  36.3 1.3 %collective-permute-done.12 = bf16[16,2688]{1,0:T(8,128)(2,1)S(1)} collective-permute-done((bf16[16,2688]{1,0:T(8,128)(2,1)S(1)}, bf16[16,2688]{1,0:T(8,128)(2,1)S(1)}, u32[]{:S(2)}, u32[]{:S(2)}) %collective-permute-start.12) | collective-permute-done | bytes 86048 | tf_op jit(solution)/shard_map/ppermute | solution.py:229
  37.6 0.0 collective-permute-done.13.refs_3_
  37.6 0.0 collective-permute-done.14.refs_4_
  37.6 0.6 collective-permute-start.16
  38.2 1.0 collective-permute-start.15
  39.1 0.6 collective-permute-start.17
  39.7 2.1 %collective-permute-start.18 = (bf16[64,2432]{1,0:T(8,128)(2,1)S(1)}, bf16[64,2432]{1,0:T(8,128)(2,1)S(1)}, u32[]{:S(2)}, u32[]{:S(2)}) collective-permute-start(bf16[64,2432]{1,0:T(8,128)(2,1)S(1)} %collective-permute-done.14.refs_4_), channel_id=1, source_target_pairs={{0,224},{32,0},{64,32},{96,64},{128,96},{160,128},{192,160},{224,1... | collective-permute-start | bytes 933896 | tf_op jit(solution)/shard_map/ppermute | solution.py:229
  41.8 4.3 %collective-permute-done.17.refs_5_ = bf16[64,2432]{1,0:T(8,128)(2,1)S(1)} collective-permute-done((bf16[64,2432]{1,0:T(8,128)(2,1)S(1)}, bf16[64,2432]{1,0:T(8,128)(2,1)S(1)}, u32[]{:S(2)}, u32[]{:S(2)}) %collective-permute-start.17) | collective-permute-done | bytes 311328 | tf_op jit(solution)/shard_map/ppermute | solution.py:229
  46.1 0.0 collective-permute-start.21
  46.1 3.0 %collective-permute-done.16.refs_2_ = bf16[128,2688]{1,0:T(8,128)(2,1)S(1)} collective-permute-done((bf16[128,2688]{1,0:T(8,128)(2,1)S(1)}, bf16[128,2688]{1,0:T(8,128)(2,1)S(1)}, u32[]{:S(2)}, u32[]{:S(2)}) %collective-permute-start.16) | collective-permute-done | bytes 688160 | tf_op jit(solution)/shard_map/ppermute | solution.py:233
  49.1 0.0 collective-permute-done.18.refs_6_
  49.2 1.3 %collective-permute-start.20 = (bf16[64,2688]{1,0:T(8,128)(2,1)S(1)}, bf16[64,2688]{1,0:T(8,128)(2,1)S(1)}, u32[]{:S(2)}, u32[]{:S(2)}) collective-permute-start(bf16[64,2688]{1,0:T(8,128)(2,1)S(1)} %slice.19), channel_id=1, source_target_pairs={{0,12},{4,0},{8,4},{12,8},{16,28},{20,16},{24,20},{28,24},{1,13},{... | collective-permute-start | bytes 1032200 | tf_op jit(solution)/shard_map/ppermute | solution.py:233
  50.5 0.0 collective-permute-done.15.refs_1_
  50.5 0.3 collective-permute-start.19
  50.8 5.4 %collective-permute-done.21.refs_7_ = bf16[64,2432]{1,0:T(8,128)(2,1)} collective-permute-done((bf16[64,2432]{1,0:T(8,128)(2,1)S(1)}, bf16[64,2432]{1,0:T(8,128)(2,1)}, u32[]{:S(2)}, u32[]{:S(2)}) %collective-permute-start.21) | collective-permute-done | bytes 311328 | tf_op jit(solution)/shard_map/ppermute | solution.py:229
  56.3 8.4 %first_grams.1 = (f32[2,5,128,128]{3,2,1,0:T(8,128)}, f32[4,512,256]{2,1,0:T(8,128)}) custom-call(bf16[64,2432]{1,0:T(8,128)(2,1)} %copy-done.6, bf16[64,2432]{1,0:T(8,128)(2,1)} %copy-done.7, bf16[64,2432]{1,0:T(8,128)(2,1)} %copy-done.8, bf16[64,2432]{1,0:T(8,128)(2,1)} %copy-done.9, bf16[64,2432]{1,0:T(8,128)(2,1)} %copy-done.10, ...), custom_call_target="tpu_custom_call" | custom-call | flops 5000000000 | bytes 12582912 | tf_op jit(solution)/shard_map/first_grams/pallas_call | solution.py:451
  64.7 0.0 collective-permute-done.20.refs_4_
  64.7 0.0 collective-permute-done.19.refs_3_
  64.7 0.0 copy-start.5
  64.7 0.7 copy-done.4
  65.4 0.1 copy-done.5
  65.5 4.0 %panel_gram.1 = (f32[5,128,128]{2,1,0:T(8,128)}, f32[5,128,128]{2,1,0:T(8,128)}) custom-call(bf16[128,2688]{1,0:T(8,128)(2,1)} %copy-done.3, bf16[128,2688]{1,0:T(8,128)(2,1)} %copy-done.2, bf16[128,2688]{1,0:T(8,128)(2,1)} %copy-done.1, bf16[64,2688]{1,0:T(8,128)(2,1)} %copy-done.5, bf16[64,2688]{1,0:T(8,128)(2,1)} %copy-done.4, ...), custom_call_target="tpu_custom_call" | custom-call | flops 1500000000 | bytes 4194304 | tf_op jit(solution)/shard_map/panel_gram/pallas_call | solution.py:473
  69.6 8.3 %collective-permute-start.22 = (f32[5,128,128]{2,1,0:T(8,128)}, f32[5,128,128]{2,1,0:T(8,128)S(1)}, u32[]{:S(2)}, u32[]{:S(2)}) collective-permute-start(f32[5,128,128]{2,1,0:T(8,128)} %get-tuple-element.33), channel_id=1, source_target_pairs={{0,1},{1,0},{2,3},{3,2},{4,5},{5,4},{6,7},{7,6},{8,9},{9,8},{10,11... | collective-permute-start | bytes 983048 | tf_op jit(solution)/shard_map/ppermute | solution.py:515
  77.9 1.5 %collective-permute-done.22 = f32[5,128,128]{2,1,0:T(8,128)S(1)} collective-permute-done((f32[5,128,128]{2,1,0:T(8,128)}, f32[5,128,128]{2,1,0:T(8,128)S(1)}, u32[]{:S(2)}, u32[]{:S(2)}) %collective-permute-start.22) | collective-permute-done | bytes 327712 | tf_op jit(solution)/shard_map/ppermute | solution.py:515
  79.4 1.0 add.21
  80.4 1.4 %collective-permute-start.23 = (f32[5,128,128]{2,1,0:T(8,128)S(1)}, f32[5,128,128]{2,1,0:T(8,128)S(1)}, u32[]{:S(2)}, u32[]{:S(2)}) collective-permute-start(f32[5,128,128]{2,1,0:T(8,128)S(1)} %add.21), channel_id=1, source_target_pairs={{0,2},{2,0},{1,3},{3,1},{4,6},{6,4},{5,7},{7,5},{8,10},{10,8},{9,1... | collective-permute-start | bytes 983048 | tf_op jit(solution)/shard_map/ppermute | solution.py:519
  81.8 6.8 %row_gram.1 = (f32[2,512,256]{2,1,0:T(8,128)}, f32[2,512,256]{2,1,0:T(8,128)}) custom-call(bf16[128,2688]{1,0:T(8,128)(2,1)} %copy-done.3, bf16[128,2688]{1,0:T(8,128)(2,1)} %copy-done.2, bf16[128,2688]{1,0:T(8,128)(2,1)} %copy-done.1, bf16[64,2688]{1,0:T(8,128)(2,1)} %copy-done.5, bf16[64,2688]{1,0:T(8,128)(2,1)} %copy-done.4, bf16[5000,1024]{1,0:T(8,128)(2,1)} %refs_5_.1, ...), custom_call_target="tpu_custom_call" | custom-call | flops 4000000000 | bytes 12582912 | tf_op jit(solution)/shard_map/row_gram/pallas_call | solution.py:494
  88.6 0.8 collective-permute-done.23
  89.4 1.5 %collective-permute-start.25 = (f32[2,512,256]{2,1,0:T(8,128)}, f32[2,512,256]{2,1,0:T(8,128)S(1)}, u32[]{:S(2)}, u32[]{:S(2)}) collective-permute-start(f32[2,512,256]{2,1,0:T(8,128)} %get-tuple-element.46), channel_id=1, source_target_pairs={{0,1},{1,0},{2,3},{3,2},{4,5},{5,4},{6,7},{7,6},{8,9},{9,8},{10,11... | collective-permute-start | bytes 3145736 | tf_op jit(solution)/shard_map/ppermute | solution.py:515
  90.9 0.1 collective-permute-start.24
  91.0 2.9 %collective-permute-done.25.arrived_ref = f32[2,512,256]{2,1,0:T(8,128)S(1)} collective-permute-done((f32[2,512,256]{2,1,0:T(8,128)}, f32[2,512,256]{2,1,0:T(8,128)S(1)}, u32[]{:S(2)}, u32[]{:S(2)}) %collective-permute-start.25) | collective-permute-done | bytes 1048608 | tf_op jit(solution)/shard_map/ppermute | solution.py:515
  93.9 1.1 add_bitcast_fusion
  95.0 1.4 %collective-permute-start.26 = (f32[512,256]{1,0:T(8,128)S(1)}, f32[512,256]{1,0:T(8,128)S(1)}, u32[]{:S(2)}, u32[]{:S(2)}) collective-permute-start(f32[512,256]{1,0:T(8,128)S(1)} %add_bitcast_fusion), channel_id=1, source_target_pairs={{0,2},{2,0},{1,3},{3,1},{4,6},{6,4},{5,7},{7,5},{8,10},{10,8},{9,1... | collective-permute-start | bytes 1572872 | tf_op jit(solution)/shard_map/ppermute | solution.py:519
  96.4 13.6 %factor.1 = (f32[4,128,128]{2,1,0:T(8,128)S(1)}, f32[3,128,512]{2,1,0:T(8,128)S(1)}) custom-call(f32[5,128,128]{2,1,0:T(8,128)S(1)} %add.22.mine_ref, f32[5,128,128]{2,1,0:T(8,128)S(1)} %collective-permute-done.24.other_ref), custom_call_target="tpu_custom_call" | custom-call | flops 30000001024 | bytes 3145728 | tf_op jit(solution)/shard_map/factor/pallas_call | solution.py:199
  110.0 3.2 %solve.1 = f32[512,256]{1,0:T(8,128)} custom-call(f32[4,128,128]{2,1,0:T(8,128)S(1)} %get-tuple-element.43.inv_ref, f32[3,128,512]{2,1,0:T(8,128)S(1)} %get-tuple-element.44.upper_ref, f32[2,512,256]{2,1,0:T(8,128)S(1)} %copy-done, f32[2,512,256]{2,1,0:T(8,128)S(1)} %collective-permute-done.25.arrived_ref, f32[512,256]{1,0:T(8,128)S(1)} %collective-permute-done.26.other_ref), custom_call_target="tpu_custom_call" | custom-call | tf_op jit(solution)/shard_map/solve/pallas_call | solution.py:214
  (38 shorter events, 0.3 us)
Async XLA Ops:
  0.0 5.8 %collective-permute-start = (bf16[8,5000]{1,0:T(8,128)(2,1)}, bf16[8,5000]{1,0:T(8,128)(2,1)S(1)}, u32[]{:S(2)}, u32[]{:S(2)}) collective-permute-start(bf16[8,5000]{1,0:T(8,128)(2,1)} %bitcast.3), channel_id=1, source_target_pairs={{0,16},{4,20},{8,24},{12,28},{16,0},{20,4},{24,8},{28,12},{1,17},{... | collective-permute-start | bytes 240008 | tf_op jit(solution)/shard_map/ppermute | solution.py:242
  6.8 10.1 %collective-permute-start.5 = (bf16[16,2432]{1,0:T(8,128)(2,1)S(1)}, bf16[16,2432]{1,0:T(8,128)(2,1)S(1)}, u32[]{:S(2)}, u32[]{:S(2)}) collective-permute-start(bf16[16,2432]{1,0:T(8,128)(2,1)S(1)} %slice.17), channel_id=1, source_target_pairs={{0,4},{4,8},{8,12},{12,0},{16,20},{20,24},{24,28},{28,16},{1,5},{5... | collective-permute-start | bytes 233480 | tf_op jit(solution)/shard_map/ppermute | solution.py:233
  8.1 8.8 %collective-permute-start.6 = (bf16[16,2432]{1,0:T(8,128)(2,1)S(1)}, bf16[16,2432]{1,0:T(8,128)(2,1)S(1)}, u32[]{:S(2)}, u32[]{:S(2)}) collective-permute-start(bf16[16,2432]{1,0:T(8,128)(2,1)S(1)} %slice.17), channel_id=1, source_target_pairs={{0,12},{4,0},{8,4},{12,8},{16,28},{20,16},{24,20},{28,24},{1,13},{... | collective-permute-start | bytes 233480 | tf_op jit(solution)/shard_map/ppermute | solution.py:233
  9.6 7.4 %collective-permute-start.7 = (bf16[16,2432]{1,0:T(8,128)(2,1)S(1)}, bf16[16,2432]{1,0:T(8,128)(2,1)S(1)}, u32[]{:S(2)}, u32[]{:S(2)}) collective-permute-start(bf16[16,2432]{1,0:T(8,128)(2,1)S(1)} %slice.17), channel_id=1, source_target_pairs={{0,8},{4,12},{8,0},{12,4},{16,24},{20,28},{24,16},{28,20},{1,9},{5... | collective-permute-start | bytes 233480 | tf_op jit(solution)/shard_map/ppermute | solution.py:233
  11.2 9.5 %collective-permute-start.1 = (bf16[16,2688]{1,0:T(8,128)(2,1)S(1)}, bf16[16,2688]{1,0:T(8,128)(2,1)S(1)}, u32[]{:S(2)}, u32[]{:S(2)}) collective-permute-start(bf16[16,2688]{1,0:T(8,128)(2,1)S(1)} %get-tuple-element.47), channel_id=1, source_target_pairs={{0,32},{32,64},{64,96},{96,128},{128,160},{160,192},{192,224},{224... | collective-permute-start | bytes 258056 | tf_op jit(solution)/shard_map/ppermute | solution.py:229
  12.9 7.8 %collective-permute-start.2 = (bf16[16,2688]{1,0:T(8,128)(2,1)S(1)}, bf16[16,2688]{1,0:T(8,128)(2,1)S(1)}, u32[]{:S(2)}, u32[]{:S(2)}) collective-permute-start(bf16[16,2688]{1,0:T(8,128)(2,1)S(1)} %get-tuple-element.47), channel_id=1, source_target_pairs={{0,224},{32,0},{64,32},{96,64},{128,96},{160,128},{192,160},{224,1... | collective-permute-start | bytes 258056 | tf_op jit(solution)/shard_map/ppermute | solution.py:229
  17.0 39.3 %copy-start.6 = (bf16[64,2432]{1,0:T(8,128)(2,1)}, bf16[64,2432]{1,0:T(8,128)(2,1)S(1)}, u32[]{:S(2)}) copy-start(bf16[64,2432]{1,0:T(8,128)(2,1)S(1)} %pad_maximum_fusion.refs_0_) | copy-start | bytes 933892
  17.0 10.1 %collective-permute-start.8 = (bf16[64,2432]{1,0:T(8,128)(2,1)S(1)}, bf16[64,2432]{1,0:T(8,128)(2,1)S(1)}, u32[]{:S(2)}, u32[]{:S(2)}) collective-permute-start(bf16[64,2432]{1,0:T(8,128)(2,1)S(1)} %pad_maximum_fusion.refs_0_), channel_id=1, source_target_pairs={{0,32},{32,64},{64,96},{96,128},{128,160},{160,192},{192,224},{224... | collective-permute-start | bytes 933896 | tf_op jit(solution)/shard_map/ppermute | solution.py:229
  17.1 10.1 %collective-permute-start.9 = (bf16[64,2432]{1,0:T(8,128)(2,1)S(1)}, bf16[64,2432]{1,0:T(8,128)(2,1)S(1)}, u32[]{:S(2)}, u32[]{:S(2)}) collective-permute-start(bf16[64,2432]{1,0:T(8,128)(2,1)S(1)} %pad_maximum_fusion.refs_0_), channel_id=1, source_target_pairs={{0,224},{32,0},{64,32},{96,64},{128,96},{160,128},{192,160},{224,1... | collective-permute-start | bytes 933896 | tf_op jit(solution)/shard_map/ppermute | solution.py:229
  20.7 6.4 %collective-permute-start.3 = (bf16[16,2688]{1,0:T(8,128)(2,1)S(1)}, bf16[16,2688]{1,0:T(8,128)(2,1)S(1)}, u32[]{:S(2)}, u32[]{:S(2)}) collective-permute-start(bf16[16,2688]{1,0:T(8,128)(2,1)S(1)} %collective-permute-done.1), channel_id=1, source_target_pairs={{0,32},{32,64},{64,96},{96,128},{128,160},{160,192},{192,224},{224... | collective-permute-start | bytes 258056 | tf_op jit(solution)/shard_map/ppermute | solution.py:229
  20.7 6.6 %collective-permute-start.4 = (bf16[16,2688]{1,0:T(8,128)(2,1)S(1)}, bf16[16,2688]{1,0:T(8,128)(2,1)S(1)}, u32[]{:S(2)}, u32[]{:S(2)}) collective-permute-start(bf16[16,2688]{1,0:T(8,128)(2,1)S(1)} %collective-permute-done.2), channel_id=1, source_target_pairs={{0,224},{32,0},{64,32},{96,64},{128,96},{160,128},{192,160},{224,1... | collective-permute-start | bytes 258056 | tf_op jit(solution)/shard_map/ppermute | solution.py:229
  27.1 29.2 %copy-start.7 = (bf16[64,2432]{1,0:T(8,128)(2,1)}, bf16[64,2432]{1,0:T(8,128)(2,1)S(1)}, u32[]{:S(2)}) copy-start(bf16[64,2432]{1,0:T(8,128)(2,1)S(1)} %collective-permute-done.8.refs_1_) | copy-start | bytes 933892
  27.1 22.0 %copy-start.8 = (bf16[64,2432]{1,0:T(8,128)(2,1)}, bf16[64,2432]{1,0:T(8,128)(2,1)S(1)}, u32[]{:S(2)}) copy-start(bf16[64,2432]{1,0:T(8,128)(2,1)S(1)} %collective-permute-done.9.refs_2_) | copy-start | bytes 933892
  27.2 4.6 %collective-permute-start.10 = (bf16[16,2688]{1,0:T(8,128)(2,1)S(1)}, bf16[16,2688]{1,0:T(8,128)(2,1)S(1)}, u32[]{:S(2)}, u32[]{:S(2)}) collective-permute-start(bf16[16,2688]{1,0:T(8,128)(2,1)S(1)} %collective-permute-done.3), channel_id=1, source_target_pairs={{0,32},{32,64},{64,96},{96,128},{128,160},{160,192},{192,224},{224... | collective-permute-start | bytes 258056 | tf_op jit(solution)/shard_map/ppermute | solution.py:229
  27.3 10.3 %collective-permute-start.13 = (bf16[64,2432]{1,0:T(8,128)(2,1)S(1)}, bf16[64,2432]{1,0:T(8,128)(2,1)S(1)}, u32[]{:S(2)}, u32[]{:S(2)}) collective-permute-start(bf16[64,2432]{1,0:T(8,128)(2,1)S(1)} %collective-permute-done.8.refs_1_), channel_id=1, source_target_pairs={{0,32},{32,64},{64,96},{96,128},{128,160},{160,192},{192,224},{224... | collective-permute-start | bytes 933896 | tf_op jit(solution)/shard_map/ppermute | solution.py:229
  27.8 9.8 %collective-permute-start.14 = (bf16[64,2432]{1,0:T(8,128)(2,1)S(1)}, bf16[64,2432]{1,0:T(8,128)(2,1)S(1)}, u32[]{:S(2)}, u32[]{:S(2)}) collective-permute-start(bf16[64,2432]{1,0:T(8,128)(2,1)S(1)} %collective-permute-done.9.refs_2_), channel_id=1, source_target_pairs={{0,224},{32,0},{64,32},{96,64},{128,96},{160,128},{192,160},{224,1... | collective-permute-start | bytes 933896 | tf_op jit(solution)/shard_map/ppermute | solution.py:229
  30.3 6.0 %collective-permute-start.11 = (bf16[16,2688]{1,0:T(8,128)(2,1)S(1)}, bf16[16,2688]{1,0:T(8,128)(2,1)S(1)}, u32[]{:S(2)}, u32[]{:S(2)}) collective-permute-start(bf16[16,2688]{1,0:T(8,128)(2,1)S(1)} %collective-permute-done.4), channel_id=1, source_target_pairs={{0,224},{32,0},{64,32},{96,64},{128,96},{160,128},{192,160},{224,1... | collective-permute-start | bytes 258056 | tf_op jit(solution)/shard_map/ppermute | solution.py:229
  31.8 5.8 %collective-permute-start.12 = (bf16[16,2688]{1,0:T(8,128)(2,1)S(1)}, bf16[16,2688]{1,0:T(8,128)(2,1)S(1)}, u32[]{:S(2)}, u32[]{:S(2)}) collective-permute-start(bf16[16,2688]{1,0:T(8,128)(2,1)S(1)} %collective-permute-done.10), channel_id=1, source_target_pairs={{0,32},{32,64},{64,96},{96,128},{128,160},{160,192},{192,224},{224... | collective-permute-start | bytes 258056 | tf_op jit(solution)/shard_map/ppermute | solution.py:229
  37.5 27.2 %copy-start.3 = (bf16[128,2688]{1,0:T(8,128)(2,1)}, bf16[128,2688]{1,0:T(8,128)(2,1)S(1)}, u32[]{:S(2)}) copy-start(bf16[128,2688]{1,0:T(8,128)(2,1)S(1)} %constant_dynamic-update-slice_fusion.refs_0_) | copy-start | bytes 2064388
  37.6 11.6 %copy-start.9 = (bf16[64,2432]{1,0:T(8,128)(2,1)}, bf16[64,2432]{1,0:T(8,128)(2,1)S(1)}, u32[]{:S(2)}) copy-start(bf16[64,2432]{1,0:T(8,128)(2,1)S(1)} %collective-permute-done.13.refs_3_) | copy-start | bytes 933892
  37.6 12.9 %copy-start.10 = (bf16[64,2432]{1,0:T(8,128)(2,1)}, bf16[64,2432]{1,0:T(8,128)(2,1)S(1)}, u32[]{:S(2)}) copy-start(bf16[64,2432]{1,0:T(8,128)(2,1)S(1)} %collective-permute-done.14.refs_4_) | copy-start | bytes 933892
  37.6 11.5 %collective-permute-start.16 = (bf16[128,2688]{1,0:T(8,128)(2,1)S(1)}, bf16[128,2688]{1,0:T(8,128)(2,1)S(1)}, u32[]{:S(2)}, u32[]{:S(2)}) collective-permute-start(bf16[128,2688]{1,0:T(8,128)(2,1)S(1)} %constant_dynamic-update-slice_fusion.refs_0_), channel_id=1, source_target_pairs={{0,12},{4,0},{8,4},{12,8},{16,28},{20,16},{24,20},{28,24},{1,13},{... | collective-permute-start | bytes 2064392 | tf_op jit(solution)/shard_map/ppermute | solution.py:233
  38.2 12.3 %collective-permute-start.15 = (bf16[128,2688]{1,0:T(8,128)(2,1)S(1)}, bf16[128,2688]{1,0:T(8,128)(2,1)S(1)}, u32[]{:S(2)}, u32[]{:S(2)}) collective-permute-start(bf16[128,2688]{1,0:T(8,128)(2,1)S(1)} %constant_dynamic-update-slice_fusion.refs_0_), channel_id=1, source_target_pairs={{0,4},{4,8},{8,12},{12,0},{16,20},{20,24},{24,28},{28,16},{1,5},{5... | collective-permute-start | bytes 2064392 | tf_op jit(solution)/shard_map/ppermute | solution.py:233
  39.1 7.0 %collective-permute-start.17 = (bf16[64,2432]{1,0:T(8,128)(2,1)S(1)}, bf16[64,2432]{1,0:T(8,128)(2,1)S(1)}, u32[]{:S(2)}, u32[]{:S(2)}) collective-permute-start(bf16[64,2432]{1,0:T(8,128)(2,1)S(1)} %collective-permute-done.13.refs_3_), channel_id=1, source_target_pairs={{0,32},{32,64},{64,96},{96,128},{128,160},{160,192},{192,224},{224... | collective-permute-start | bytes 933896 | tf_op jit(solution)/shard_map/ppermute | solution.py:229
  39.7 9.4 %collective-permute-start.18 = (bf16[64,2432]{1,0:T(8,128)(2,1)S(1)}, bf16[64,2432]{1,0:T(8,128)(2,1)S(1)}, u32[]{:S(2)}, u32[]{:S(2)}) collective-permute-start(bf16[64,2432]{1,0:T(8,128)(2,1)S(1)} %collective-permute-done.14.refs_4_), channel_id=1, source_target_pairs={{0,224},{32,0},{64,32},{96,64},{128,96},{160,128},{192,160},{224,1... | collective-permute-start | bytes 933896 | tf_op jit(solution)/shard_map/ppermute | solution.py:229
  46.1 4.7 %copy-start.11 = (bf16[64,2432]{1,0:T(8,128)(2,1)}, bf16[64,2432]{1,0:T(8,128)(2,1)S(1)}, u32[]{:S(2)}) copy-start(bf16[64,2432]{1,0:T(8,128)(2,1)S(1)} %collective-permute-done.17.refs_5_) | copy-start | bytes 933892
  46.1 10.2 %collective-permute-start.21 = (bf16[64,2432]{1,0:T(8,128)(2,1)S(1)}, bf16[64,2432]{1,0:T(8,128)(2,1)}, u32[]{:S(2)}, u32[]{:S(2)}) collective-permute-start(bf16[64,2432]{1,0:T(8,128)(2,1)S(1)} %collective-permute-done.17.refs_5_), channel_id=1, source_target_pairs={{0,32},{32,64},{64,96},{96,128},{128,160},{160,192},{192,224},{224... | collective-permute-start | bytes 933896 | tf_op jit(solution)/shard_map/ppermute | solution.py:229
  49.1 15.6 %copy-start.1 = (bf16[128,2688]{1,0:T(8,128)(2,1)}, bf16[128,2688]{1,0:T(8,128)(2,1)S(1)}, u32[]{:S(2)}) copy-start(bf16[128,2688]{1,0:T(8,128)(2,1)S(1)} %collective-permute-done.16.refs_2_) | copy-start | bytes 2064388
  49.1 1.7 %copy-start.12 = (bf16[64,2432]{1,0:T(8,128)(2,1)}, bf16[64,2432]{1,0:T(8,128)(2,1)S(1)}, u32[]{:S(2)}) copy-start(bf16[64,2432]{1,0:T(8,128)(2,1)S(1)} %collective-permute-done.18.refs_6_) | copy-start | bytes 933892
  49.2 15.5 %collective-permute-start.20 = (bf16[64,2688]{1,0:T(8,128)(2,1)S(1)}, bf16[64,2688]{1,0:T(8,128)(2,1)S(1)}, u32[]{:S(2)}, u32[]{:S(2)}) collective-permute-start(bf16[64,2688]{1,0:T(8,128)(2,1)S(1)} %slice.19), channel_id=1, source_target_pairs={{0,12},{4,0},{8,4},{12,8},{16,28},{20,16},{24,20},{28,24},{1,13},{... | collective-permute-start | bytes 1032200 | tf_op jit(solution)/shard_map/ppermute | solution.py:233
  50.5 14.2 %copy-start.2 = (bf16[128,2688]{1,0:T(8,128)(2,1)}, bf16[128,2688]{1,0:T(8,128)(2,1)S(1)}, u32[]{:S(2)}) copy-start(bf16[128,2688]{1,0:T(8,128)(2,1)S(1)} %collective-permute-done.15.refs_1_) | copy-start | bytes 2064388
  50.5 14.2 %collective-permute-start.19 = (bf16[64,2688]{1,0:T(8,128)(2,1)S(1)}, bf16[64,2688]{1,0:T(8,128)(2,1)S(1)}, u32[]{:S(2)}, u32[]{:S(2)}) collective-permute-start(bf16[64,2688]{1,0:T(8,128)(2,1)S(1)} %slice.18), channel_id=1, source_target_pairs={{0,4},{4,8},{8,12},{12,0},{16,20},{20,24},{24,28},{28,16},{1,5},{5... | collective-permute-start | bytes 1032200 | tf_op jit(solution)/shard_map/ppermute | solution.py:233
  64.7 0.7 copy-start.4
  64.7 0.8 copy-start.5
  69.6 9.8 %collective-permute-start.22 = (f32[5,128,128]{2,1,0:T(8,128)}, f32[5,128,128]{2,1,0:T(8,128)S(1)}, u32[]{:S(2)}, u32[]{:S(2)}) collective-permute-start(f32[5,128,128]{2,1,0:T(8,128)} %get-tuple-element.33), channel_id=1, source_target_pairs={{0,1},{1,0},{2,3},{3,2},{4,5},{5,4},{6,7},{7,6},{8,9},{9,8},{10,11... | collective-permute-start | bytes 983048 | tf_op jit(solution)/shard_map/ppermute | solution.py:515
  80.4 9.0 %collective-permute-start.23 = (f32[5,128,128]{2,1,0:T(8,128)S(1)}, f32[5,128,128]{2,1,0:T(8,128)S(1)}, u32[]{:S(2)}, u32[]{:S(2)}) collective-permute-start(f32[5,128,128]{2,1,0:T(8,128)S(1)} %add.21), channel_id=1, source_target_pairs={{0,2},{2,0},{1,3},{3,1},{4,6},{6,4},{5,7},{7,5},{8,10},{10,8},{9,1... | collective-permute-start | bytes 983048 | tf_op jit(solution)/shard_map/ppermute | solution.py:519
  89.4 4.5 %collective-permute-start.25 = (f32[2,512,256]{2,1,0:T(8,128)}, f32[2,512,256]{2,1,0:T(8,128)S(1)}, u32[]{:S(2)}, u32[]{:S(2)}) collective-permute-start(f32[2,512,256]{2,1,0:T(8,128)} %get-tuple-element.46), channel_id=1, source_target_pairs={{0,1},{1,0},{2,3},{3,2},{4,5},{5,4},{6,7},{7,6},{8,9},{9,8},{10,11... | collective-permute-start | bytes 3145736 | tf_op jit(solution)/shard_map/ppermute | solution.py:515
  90.9 5.5 %collective-permute-start.24 = (f32[5,128,128]{2,1,0:T(8,128)S(1)}, f32[5,128,128]{2,1,0:T(8,128)S(1)}, u32[]{:S(2)}, u32[]{:S(2)}) collective-permute-start(f32[5,128,128]{2,1,0:T(8,128)S(1)} %add.22.mine_ref), channel_id=1, source_target_pairs={{0,1},{1,0},{2,3},{3,2},{4,5},{5,4},{6,7},{7,6},{8,9},{9,8},{10,11... | collective-permute-start | bytes 983048 | tf_op jit(solution)/shard_map/ppermute | solution.py:515
  95.0 15.0 %copy-start = (f32[2,512,256]{2,1,0:T(8,128)S(1)}, f32[2,512,256]{2,1,0:T(8,128)}, u32[]{:S(2)}) copy-start(f32[2,512,256]{2,1,0:T(8,128)} %get-tuple-element.45.keep_ref) | copy-start | bytes 3145732
  95.0 15.0 %collective-permute-start.26 = (f32[512,256]{1,0:T(8,128)S(1)}, f32[512,256]{1,0:T(8,128)S(1)}, u32[]{:S(2)}, u32[]{:S(2)}) collective-permute-start(f32[512,256]{1,0:T(8,128)S(1)} %add_bitcast_fusion), channel_id=1, source_target_pairs={{0,2},{2,0},{1,3},{3,1},{4,6},{6,4},{5,7},{7,5},{8,10},{10,8},{9,1... | collective-permute-start | bytes 1572872 | tf_op jit(solution)/shard_map/ppermute | solution.py:519

commit v4 on v3

--- a/solution.py
+++ b/solution.py
@@ -10,8 +10,8 @@
 ROW0 = (((0,), (0,)), ((), ()))
 NB = 128
 PANEL = 512
-FIRST_K = 2432
-SECOND_K = 2688
+FIRST_K = 2304
+SECOND_K = 2816
 CHUNK_K = 1024
 HALVES = (((0, 0), (0, 1), (0, 2), (0, 3), (3, 3)), ((1, 1), (1, 2), (1, 3), (2, 2), (2, 3)))
 
@@ -170,20 +170,11 @@
     lax.fori_loop(0, PANEL // NB, step, 0)
 
 
-def solve_kernel(inv_ref, upper_ref, keep_ref, arrived_ref, other_ref, out_ref, gram_ref, sems):
-    chip = lax.axis_index("orb") // 2
-    copies = [
-        pltpu.make_async_copy(ref.at[chip], gram_ref.at[k], sems.at[k])
-        for k, ref in enumerate((keep_ref, arrived_ref))
-    ]
-    for copy in copies:
-        copy.start()
-    for copy in copies:
-        copy.wait()
+def solve_kernel(inv_ref, upper_ref, keep_ref, arrived_ref, other_ref, out_ref):
     solved = []
     for j in range(PANEL // NB):
         cut = slice(j * NB, (j + 1) * NB)
-        gram = gram_ref[0, cut, :] + gram_ref[1, cut, :] + other_ref[cut, :]
+        gram = keep_ref[cut, :] + arrived_ref[cut, :] + other_ref[cut, :]
         rest = gram * gram
         for i in range(j):
             rest -= lax.dot_general(
@@ -210,12 +201,9 @@
 
 
 def solve(inv, upper, keep, arrived, other):
-    vmem, hbm = pl.BlockSpec(memory_space=pltpu.VMEM), pl.BlockSpec(memory_space=pl.ANY)
     return pl.pallas_call(
         solve_kernel,
-        in_specs=[vmem, vmem, hbm, hbm, vmem],
         out_shape=jax.ShapeDtypeStruct(other.shape, F32),
-        scratch_shapes=[pltpu.VMEM((2,) + other.shape, F32), pltpu.SemaphoreType.DMA((2,))],
         compiler_params=pltpu.CompilerParams(vmem_limit_bytes=40 << 20),
         name="solve",
     )(inv, upper, keep, arrived, other)
@@ -406,9 +394,10 @@
 
 
 def rows_kernel(places, pieces, *refs):
-    orbitals_ref, before_ref, give_ref, keep_ref = refs[pieces : pieces + 4]
-    panel_ref, window_ref, total_ref, start_ref, sems, window_sems, out_sems = refs[pieces + 4 :]
+    orbitals_ref, before_ref, *out_refs = refs[pieces : pieces + 6]
+    panel_ref, window_ref, total_ref, start_ref, sems, window_sems, out_sems = refs[pieces + 6 :]
     core = lax.axis_index("orb") % 2
+    chip = lax.axis_index("orb") // 2
     quarter = total_ref.shape[2]
     rows = orbitals_ref.shape[0] - FIRST_K
     window_ref[rows:, :] = jnp.zeros((SECOND_K - rows, orbitals_ref.shape[1]), jnp.bfloat16)
@@ -420,22 +409,16 @@
         if part.stop < SECOND_K:
             add_rows(panel_ref, window_ref, part, total_ref, c > 0)
     before.wait()
-    for n in range(4):
+    sends = []
+    for n, ref in enumerate(out_refs):
+        which = 2 * (1 - chip if n < 2 else chip) + (core if n % 2 else 1 - core)
+        columns = pl.ds(pl.multiple_of(which * quarter, quarter), quarter)
         gram = jnp.dot(
-            panel_ref[:, part],
-            window_ref[part, n * quarter : (n + 1) * quarter],
-            preferred_element_type=F32,
+            panel_ref[:, part], window_ref[part, columns], preferred_element_type=F32
         )
-        total_ref[n] = total_ref[n] + (start_ref[n] + gram)
-        if n % 2:
-            sends = sends if n > 1 else []
-            for ref, which in ((give_ref, 1 - core), (keep_ref, core)):
-                sends.append(
-                    pltpu.make_async_copy(
-                        total_ref.at[n - 1 + which], ref.at[n // 2], out_sems.at[len(sends)]
-                    )
-                )
-                sends[-1].start()
+        total_ref[which] = total_ref[which] + (start_ref[which] + gram)
+        sends.append(pltpu.make_async_copy(total_ref.at[which], ref, out_sems.at[n]))
+        sends[-1].start()
     for send in sends:
         send.wait()
 
@@ -490,12 +473,12 @@
 
 def row_gram(pieces, places, orbitals, before):
     columns, count = orbitals.shape[1], len(chunks(SECOND_K))
-    out = jax.ShapeDtypeStruct((2, PANEL, columns // 4), F32)
+    out = jax.ShapeDtypeStruct((PANEL, columns // 4), F32)
     return pl.pallas_call(
         lambda *refs: rows_kernel(places, len(pieces), *refs),
         in_specs=[HBM] * (len(pieces) + 2),
-        out_specs=[HBM] * 2,
-        out_shape=(out, out),
+        out_specs=[HBM] * 4,
+        out_shape=(out,) * 4,
         scratch_shapes=[
             pltpu.VMEM((PANEL, SECOND_K), jnp.bfloat16),
             pltpu.VMEM((SECOND_K, columns), jnp.bfloat16),
@@ -519,24 +502,19 @@
     return lax.ppermute(v, "orb", CHIP_SWAP)
 
 
-def pick(v, which):
-    return lax.dynamic_index_in_dim(v, which, 0, keepdims=False)
-
-
 def on_device(panel_orbitals, orbitals):
-    chip = lax.axis_index("orb") // 2
     (first, first_places), (second, second_places) = gather_panel(panel_orbitals)
     panel, rows = first_grams(first, first_places, orbitals)
     give, keep = panel_gram(second, second_places, panel)
     half = keep + swap_cores(give)
     half, second = lax.optimization_barrier((half, second))
-    half = half + swap_chips(half)
-    give, keep = row_gram(second, second_places, orbitals, rows)
-    half, give = lax.optimization_barrier((half, give))
-    arrived = swap_cores(give)
-    other = swap_chips(pick(keep, 1 - chip) + pick(arrived, 1 - chip))
+    sent = swap_chips(half)
+    give, keep, our_give, our_keep = row_gram(second, second_places, orbitals, rows)
+    half = after(half, our_keep) + sent
+    other = swap_chips(keep + swap_cores(give))
+    arrived = swap_cores(our_give)
     inv, upper = factorise(half, swap_cores(half))
-    return solve(inv, upper, keep, arrived, other)
+    return solve(inv, upper, our_keep, arrived, other)
 
 
 def solution(mesh):

time: 114 us -> 110 us (0.965)
  waiting for transfers between devices: 29.4 us -> 25.7 us
    ppermute x3 -> x4, waiting for transfers between devices: 4.33 us -> 1.89 us  [swap_cores(): return lax.ppermute(v, 'orb', CORE_SWAP)]
    ppermute x14, waiting for transfers between devices: 19.3 us -> 17.7 us  [along_z(): return lax.ppermute(v, 'prow', z_shift(k))]
    ppermute x3 -> x4, starting transfers between devices: 9.96 us -> 10.2 us  [swap_cores(): return lax.ppermute(v, 'orb', CORE_SWAP)]
  transfers between devices with their start and end apart: 27 -> 28, of which waited for: 11 -> 10; matrix products, arithmetic and copies ran while one was open for 1% -> 1% of each run, Pallas kernels for 25% -> 26%
where the time goes in v4:
time: 110 us; the launch traced here: 109 us
  starting transfers between devices  43.2 us (39%)
  Pallas kernels  35.7 us (32%)
  waiting for transfers between devices  25.7 us (23%)
  other arithmetic  3.19 us (3%)
    ppermute x14, starting transfers between devices, along_z(): return lax.ppermute(v, 'prow', z_shift(k))  19.2 us
    ppermute x14, waiting for transfers between devices, along_z(): return lax.ppermute(v, 'prow', z_shift(k))  17.7 us
    pallas_call x1, Pallas kernels, factorise(): pl.pallas_call(factor_kernel, out_shape=(jax.ShapeDtypeStruct((blocks, NB...  13.6 us
    ppermute x4, starting transfers between devices, swap_cores(): return lax.ppermute(v, 'orb', CORE_SWAP)  10.2 us
    pallas_call x1, Pallas kernels, first_grams(): pl.pallas_call(lambda *refs: first_kernel(places, len(pieces), *refs), in...  8.07 us
    ppermute x7, starting transfers between devices, along_x(): return lax.ppermute(v, 'pcol', x_shift(k))  7.5 us
    pallas_call x1, Pallas kernels, row_gram(): pl.pallas_call(lambda *refs: rows_kernel(places, len(pieces), *refs), in_...  6.97 us
    ppermute x7, waiting for transfers between devices, along_x(): return lax.ppermute(v, 'pcol', x_shift(k))  4.06 us
  transfers between devices with their start and end apart: 28, of which 10 were waited for; matrix products, arithmetic and copies ran while one was open for 1% of the time, Pallas kernels for 26%

profile of v4, /device:TPU:1, one launch (start us, length us, event | category | flops | bytes accessed | tf_op | source)
XLA Modules:
  0.0 109.2 jit_solution(2486986867299822359)
XLA Ops:
  0.0 3.7 %collective-permute-start = (bf16[8,5000]{1,0:T(8,128)(2,1)}, bf16[8,5000]{1,0:T(8,128)(2,1)S(1)}, u32[]{:S(2)}, u32[]{:S(2)}) collective-permute-start(bf16[8,5000]{1,0:T(8,128)(2,1)} %bitcast.1), channel_id=1, source_target_pairs={{0,16},{4,20},{8,24},{12,28},{16,0},{20,4},{24,8},{28,12},{1,17},{... | collective-permute-start | bytes 240008 | tf_op jit(solution)/shard_map/ppermute | solution.py:230
  3.7 2.0 %collective-permute-done = bf16[8,5000]{1,0:T(8,128)(2,1)S(1)} collective-permute-done((bf16[8,5000]{1,0:T(8,128)(2,1)}, bf16[8,5000]{1,0:T(8,128)(2,1)S(1)}, u32[]{:S(2)}, u32[]{:S(2)}) %collective-permute-start) | collective-permute-done | bytes 80032 | tf_op jit(solution)/shard_map/ppermute | solution.py:230
  5.8 1.0 maximum_select_fusion
  6.8 1.3 %collective-permute-start.5 = (bf16[16,2304]{1,0:T(8,128)(2,1)S(1)}, bf16[16,2304]{1,0:T(8,128)(2,1)S(1)}, u32[]{:S(2)}, u32[]{:S(2)}) collective-permute-start(bf16[16,2304]{1,0:T(8,128)(2,1)S(1)} %slice.17), channel_id=1, source_target_pairs={{0,4},{4,8},{8,12},{12,0},{16,20},{20,24},{24,28},{28,16},{1,5},{5... | collective-permute-start | bytes 221192 | tf_op jit(solution)/shard_map/ppermute | solution.py:221
  8.1 1.4 %collective-permute-start.6 = (bf16[16,2304]{1,0:T(8,128)(2,1)S(1)}, bf16[16,2304]{1,0:T(8,128)(2,1)S(1)}, u32[]{:S(2)}, u32[]{:S(2)}) collective-permute-start(bf16[16,2304]{1,0:T(8,128)(2,1)S(1)} %slice.17), channel_id=1, source_target_pairs={{0,12},{4,0},{8,4},{12,8},{16,28},{20,16},{24,20},{28,24},{1,13},{... | collective-permute-start | bytes 221192 | tf_op jit(solution)/shard_map/ppermute | solution.py:221
  9.6 1.6 %collective-permute-start.7 = (bf16[16,2304]{1,0:T(8,128)(2,1)S(1)}, bf16[16,2304]{1,0:T(8,128)(2,1)S(1)}, u32[]{:S(2)}, u32[]{:S(2)}) collective-permute-start(bf16[16,2304]{1,0:T(8,128)(2,1)S(1)} %slice.17), channel_id=1, source_target_pairs={{0,8},{4,12},{8,0},{12,4},{16,24},{20,28},{24,16},{28,20},{1,9},{5... | collective-permute-start | bytes 221192 | tf_op jit(solution)/shard_map/ppermute | solution.py:221
  11.2 1.7 %collective-permute-start.1 = (bf16[16,2816]{1,0:T(8,128)(2,1)S(1)}, bf16[16,2816]{1,0:T(8,128)(2,1)S(1)}, u32[]{:S(2)}, u32[]{:S(2)}) collective-permute-start(bf16[16,2816]{1,0:T(8,128)(2,1)S(1)} %get-tuple-element.49), channel_id=1, source_target_pairs={{0,32},{32,64},{64,96},{96,128},{128,160},{160,192},{192,224},{224... | collective-permute-start | bytes 270344 | tf_op jit(solution)/shard_map/ppermute | solution.py:217
  12.9 4.0 %collective-permute-start.2 = (bf16[16,2816]{1,0:T(8,128)(2,1)S(1)}, bf16[16,2816]{1,0:T(8,128)(2,1)S(1)}, u32[]{:S(2)}, u32[]{:S(2)}) collective-permute-start(bf16[16,2816]{1,0:T(8,128)(2,1)S(1)} %get-tuple-element.49), channel_id=1, source_target_pairs={{0,224},{32,0},{64,32},{96,64},{128,96},{160,128},{192,160},{224,1... | collective-permute-start | bytes 270344 | tf_op jit(solution)/shard_map/ppermute | solution.py:217
  16.9 0.0 collective-permute-done.5
  16.9 0.0 collective-permute-done.6
  16.9 0.0 collective-permute-done.7
  16.9 0.0 copy-start.6
  17.0 0.1 collective-permute-start.8
  17.1 3.5 %collective-permute-start.9 = (bf16[64,2304]{1,0:T(8,128)(2,1)S(1)}, bf16[64,2304]{1,0:T(8,128)(2,1)S(1)}, u32[]{:S(2)}, u32[]{:S(2)}) collective-permute-start(bf16[64,2304]{1,0:T(8,128)(2,1)S(1)} %pad_maximum_fusion.refs_0_), channel_id=1, source_target_pairs={{0,224},{32,0},{64,32},{96,64},{128,96},{160,128},{192,160},{224,1... | collective-permute-start | bytes 884744 | tf_op jit(solution)/shard_map/ppermute | solution.py:217
  20.6 0.0 collective-permute-done.1
  20.6 0.0 collective-permute-start.3
  20.6 0.0 collective-permute-done.2
  20.6 2.7 %collective-permute-start.4 = (bf16[16,2816]{1,0:T(8,128)(2,1)S(1)}, bf16[16,2816]{1,0:T(8,128)(2,1)S(1)}, u32[]{:S(2)}, u32[]{:S(2)}) collective-permute-start(bf16[16,2816]{1,0:T(8,128)(2,1)S(1)} %collective-permute-done.2), channel_id=1, source_target_pairs={{0,224},{32,0},{64,32},{96,64},{128,96},{160,128},{192,160},{224,1... | collective-permute-start | bytes 270344 | tf_op jit(solution)/shard_map/ppermute | solution.py:217
  23.3 3.7 %collective-permute-done.3 = bf16[16,2816]{1,0:T(8,128)(2,1)S(1)} collective-permute-done((bf16[16,2816]{1,0:T(8,128)(2,1)S(1)}, bf16[16,2816]{1,0:T(8,128)(2,1)S(1)}, u32[]{:S(2)}, u32[]{:S(2)}) %collective-permute-start.3) | collective-permute-done | bytes 90144 | tf_op jit(solution)/shard_map/ppermute | solution.py:217
  27.0 0.0 collective-permute-done.8.refs_1_
  27.0 0.0 collective-permute-done.9.refs_2_
  27.0 0.1 collective-permute-start.10
  27.1 0.0 collective-permute-done.4
  27.1 0.5 collective-permute-start.13
  27.6 2.6 %collective-permute-start.14 = (bf16[64,2304]{1,0:T(8,128)(2,1)S(1)}, bf16[64,2304]{1,0:T(8,128)(2,1)S(1)}, u32[]{:S(2)}, u32[]{:S(2)}) collective-permute-start(bf16[64,2304]{1,0:T(8,128)(2,1)S(1)} %collective-permute-done.9.refs_2_), channel_id=1, source_target_pairs={{0,224},{32,0},{64,32},{96,64},{128,96},{160,128},{192,160},{224,1... | collective-permute-start | bytes 884744 | tf_op jit(solution)/shard_map/ppermute | solution.py:217
  30.2 1.4 %collective-permute-start.11 = (bf16[16,2816]{1,0:T(8,128)(2,1)S(1)}, bf16[16,2816]{1,0:T(8,128)(2,1)S(1)}, u32[]{:S(2)}, u32[]{:S(2)}) collective-permute-start(bf16[16,2816]{1,0:T(8,128)(2,1)S(1)} %collective-permute-done.4), channel_id=1, source_target_pairs={{0,224},{32,0},{64,32},{96,64},{128,96},{160,128},{192,160},{224,1... | collective-permute-start | bytes 270344 | tf_op jit(solution)/shard_map/ppermute | solution.py:217
  31.6 0.1 collective-permute-done.10
  31.7 0.0 collective-permute-start.12
  31.7 3.9 %collective-permute-done.11 = bf16[16,2816]{1,0:T(8,128)(2,1)S(1)} collective-permute-done((bf16[16,2816]{1,0:T(8,128)(2,1)S(1)}, bf16[16,2816]{1,0:T(8,128)(2,1)S(1)}, u32[]{:S(2)}, u32[]{:S(2)}) %collective-permute-start.11) | collective-permute-done | bytes 90144 | tf_op jit(solution)/shard_map/ppermute | solution.py:217
  35.6 1.8 %collective-permute-done.12 = bf16[16,2816]{1,0:T(8,128)(2,1)S(1)} collective-permute-done((bf16[16,2816]{1,0:T(8,128)(2,1)S(1)}, bf16[16,2816]{1,0:T(8,128)(2,1)S(1)}, u32[]{:S(2)}, u32[]{:S(2)}) %collective-permute-start.12) | collective-permute-done | bytes 90144 | tf_op jit(solution)/shard_map/ppermute | solution.py:217
  37.5 0.0 collective-permute-done.13.refs_3_
  37.5 0.0 collective-permute-done.14.refs_4_
  37.5 0.6 collective-permute-start.16
  38.1 1.0 collective-permute-start.15
  39.1 0.4 collective-permute-start.17
  39.5 2.3 %collective-permute-start.18 = (bf16[64,2304]{1,0:T(8,128)(2,1)S(1)}, bf16[64,2304]{1,0:T(8,128)(2,1)S(1)}, u32[]{:S(2)}, u32[]{:S(2)}) collective-permute-start(bf16[64,2304]{1,0:T(8,128)(2,1)S(1)} %collective-permute-done.14.refs_4_), channel_id=1, source_target_pairs={{0,224},{32,0},{64,32},{96,64},{128,96},{160,128},{192,160},{224,1... | collective-permute-start | bytes 884744 | tf_op jit(solution)/shard_map/ppermute | solution.py:217
  41.7 4.1 %collective-permute-done.17.refs_5_ = bf16[64,2304]{1,0:T(8,128)(2,1)S(1)} collective-permute-done((bf16[64,2304]{1,0:T(8,128)(2,1)S(1)}, bf16[64,2304]{1,0:T(8,128)(2,1)S(1)}, u32[]{:S(2)}, u32[]{:S(2)}) %collective-permute-start.17) | collective-permute-done | bytes 294944 | tf_op jit(solution)/shard_map/ppermute | solution.py:217
  45.9 0.0 collective-permute-start.21
  45.9 4.0 %collective-permute-done.16.refs_2_ = bf16[128,2816]{1,0:T(8,128)(2,1)S(1)} collective-permute-done((bf16[128,2816]{1,0:T(8,128)(2,1)S(1)}, bf16[128,2816]{1,0:T(8,128)(2,1)S(1)}, u32[]{:S(2)}, u32[]{:S(2)}) %collective-permute-start.16) | collective-permute-done | bytes 720928 | tf_op jit(solution)/shard_map/ppermute | solution.py:221
  49.9 0.0 collective-permute-done.18.refs_6_
  50.0 1.3 %collective-permute-start.20 = (bf16[64,2816]{1,0:T(8,128)(2,1)S(1)}, bf16[64,2816]{1,0:T(8,128)(2,1)S(1)}, u32[]{:S(2)}, u32[]{:S(2)}) collective-permute-start(bf16[64,2816]{1,0:T(8,128)(2,1)S(1)} %slice.19), channel_id=1, source_target_pairs={{0,12},{4,0},{8,4},{12,8},{16,28},{20,16},{24,20},{28,24},{1,13},{... | collective-permute-start | bytes 1081352 | tf_op jit(solution)/shard_map/ppermute | solution.py:221
  51.3 0.0 collective-permute-done.15.refs_1_
  51.3 0.3 collective-permute-start.19
  51.6 4.0 %collective-permute-done.21.refs_7_ = bf16[64,2304]{1,0:T(8,128)(2,1)} collective-permute-done((bf16[64,2304]{1,0:T(8,128)(2,1)S(1)}, bf16[64,2304]{1,0:T(8,128)(2,1)}, u32[]{:S(2)}, u32[]{:S(2)}) %collective-permute-start.21) | collective-permute-done | bytes 294944 | tf_op jit(solution)/shard_map/ppermute | solution.py:217
  55.7 8.1 %first_grams.1 = (f32[2,5,128,128]{3,2,1,0:T(8,128)}, f32[4,512,256]{2,1,0:T(8,128)}) custom-call(bf16[64,2304]{1,0:T(8,128)(2,1)} %copy-done.6, bf16[64,2304]{1,0:T(8,128)(2,1)} %copy-done.7, bf16[64,2304]{1,0:T(8,128)(2,1)} %copy-done.8, bf16[64,2304]{1,0:T(8,128)(2,1)} %copy-done.9, bf16[64,2304]{1,0:T(8,128)(2,1)} %copy-done.10, ...), custom_call_target="tpu_custom_call" | custom-call | flops 5000000000 | bytes 12582912 | tf_op jit(solution)/shard_map/first_grams/pallas_call | solution.py:434
  63.8 0.7 copy-done.4
  64.5 0.2 copy-done.5
  64.6 4.0 %panel_gram.1 = (f32[5,128,128]{2,1,0:T(8,128)}, f32[5,128,128]{2,1,0:T(8,128)}) custom-call(bf16[128,2816]{1,0:T(8,128)(2,1)} %copy-done.3, bf16[128,2816]{1,0:T(8,128)(2,1)} %copy-done.2, bf16[128,2816]{1,0:T(8,128)(2,1)} %copy-done.1, bf16[64,2816]{1,0:T(8,128)(2,1)} %copy-done.5, bf16[64,2816]{1,0:T(8,128)(2,1)} %copy-done.4, ...), custom_call_target="tpu_custom_call" | custom-call | flops 1500000000 | bytes 4194304 | tf_op jit(solution)/shard_map/panel_gram/pallas_call | solution.py:456
  68.7 8.2 %collective-permute-start.22 = (f32[5,128,128]{2,1,0:T(8,128)}, f32[5,128,128]{2,1,0:T(8,128)S(1)}, u32[]{:S(2)}, u32[]{:S(2)}) collective-permute-start(f32[5,128,128]{2,1,0:T(8,128)} %get-tuple-element.34), channel_id=1, source_target_pairs={{0,1},{1,0},{2,3},{3,2},{4,5},{5,4},{6,7},{7,6},{8,9},{9,8},{10,11... | collective-permute-start | bytes 983048 | tf_op jit(solution)/shard_map/ppermute | solution.py:498
  76.8 1.5 %collective-permute-done.22 = f32[5,128,128]{2,1,0:T(8,128)S(1)} collective-permute-done((f32[5,128,128]{2,1,0:T(8,128)}, f32[5,128,128]{2,1,0:T(8,128)S(1)}, u32[]{:S(2)}, u32[]{:S(2)}) %collective-permute-start.22) | collective-permute-done | bytes 327712 | tf_op jit(solution)/shard_map/ppermute | solution.py:498
  78.3 1.0 add.11
  79.3 1.6 %collective-permute-start.23 = (f32[5,128,128]{2,1,0:T(8,128)S(1)}, f32[5,128,128]{2,1,0:T(8,128)S(1)}, u32[]{:S(2)}, u32[]{:S(2)}) collective-permute-start(f32[5,128,128]{2,1,0:T(8,128)S(1)} %add.11), channel_id=1, source_target_pairs={{0,2},{2,0},{1,3},{3,1},{4,6},{6,4},{5,7},{7,5},{8,10},{10,8},{9,1... | collective-permute-start | bytes 983048 | tf_op jit(solution)/shard_map/ppermute | solution.py:502
  80.9 7.0 %row_gram.1 = (f32[512,256]{1,0:T(8,128)}, f32[512,256]{1,0:T(8,128)}, f32[512,256]{1,0:T(8,128)}, f32[512,256]{1,0:T(8,128)}) custom-call(bf16[128,2816]{1,0:T(8,128)(2,1)} %copy-done.3, bf16[128,2816]{1,0:T(8,128)(2,1)} %copy-done.2, bf16[128,2816]{1,0:T(8,128)(2,1)} %copy-done.1, bf16[64,2816]{1,0:T(8,128)(2,1)} %copy-done.5, bf16[64,2816]{1,0:T(8,128)(2,1)} %copy-done.4, ...), custom_call_target="tpu_custom_call" | custom-call | flops 4000000000 | bytes 12582912 | tf_op jit(solution)/shard_map/row_gram/pallas_call | solution.py:477
  87.9 0.7 collective-permute-start.26
  88.7 0.0 collective-permute-done.23
  88.7 1.2 %collective-permute-start.24 = (f32[5,128,128]{2,1,0:T(8,128)S(1)}, f32[5,128,128]{2,1,0:T(8,128)S(1)}, u32[]{:S(2)}, u32[]{:S(2)}) collective-permute-start(f32[5,128,128]{2,1,0:T(8,128)S(1)} %add.12.mine_ref), channel_id=1, source_target_pairs={{0,1},{1,0},{2,3},{3,2},{4,5},{5,4},{6,7},{7,6},{8,9},{9,8},{10,11... | collective-permute-start | bytes 983048 | tf_op jit(solution)/shard_map/ppermute | solution.py:498
  89.9 0.1 collective-permute-start.25
  90.0 0.4 collective-permute-done.26
  90.4 1.1 %add.13 = f32[512,256]{1,0:T(8,128)S(1)} add(f32[512,256]{1,0:T(8,128)} %get-tuple-element.47, f32[512,256]{1,0:T(8,128)S(1)} %collective-permute-done.26) | non-fusion elementwise | flops 131072 | bytes 1572864 | tf_op jit(solution)/shard_map/add | solution.py:514
  91.5 1.0 collective-permute-start.27
  92.5 0.0 collective-permute-done.24.other_ref
  92.5 13.6 %factor.1 = (f32[4,128,128]{2,1,0:T(8,128)S(1)}, f32[3,128,512]{2,1,0:T(8,128)S(1)}) custom-call(f32[5,128,128]{2,1,0:T(8,128)S(1)} %add.12.mine_ref, f32[5,128,128]{2,1,0:T(8,128)S(1)} %collective-permute-done.24.other_ref), custom_call_target="tpu_custom_call" | custom-call | flops 30000001024 | bytes 3145728 | tf_op jit(solution)/shard_map/factor/pallas_call | solution.py:190
  106.1 0.0 collective-permute-done.27.other_ref
  106.1 3.1 %solve.1 = f32[512,256]{1,0:T(8,128)} custom-call(f32[4,128,128]{2,1,0:T(8,128)S(1)} %get-tuple-element.44.inv_ref, f32[3,128,512]{2,1,0:T(8,128)S(1)} %get-tuple-element.45.upper_ref, f32[512,256]{1,0:T(8,128)S(1)} %copy-done, f32[512,256]{1,0:T(8,128)S(1)} %collective-permute-done.25.arrived_ref, f32[512,256]{1,0:T(8,128)S(1)} %collective-permute-done.27.other_ref), custom_call_target="tpu_custom_call" | custom-call | tf_op jit(solution)/shard_map/solve/pallas_call | solution.py:204
  (40 shorter events, 0.2 us)
Async XLA Ops:
  0.0 5.8 %collective-permute-start = (bf16[8,5000]{1,0:T(8,128)(2,1)}, bf16[8,5000]{1,0:T(8,128)(2,1)S(1)}, u32[]{:S(2)}, u32[]{:S(2)}) collective-permute-start(bf16[8,5000]{1,0:T(8,128)(2,1)} %bitcast.1), channel_id=1, source_target_pairs={{0,16},{4,20},{8,24},{12,28},{16,0},{20,4},{24,8},{28,12},{1,17},{... | collective-permute-start | bytes 240008 | tf_op jit(solution)/shard_map/ppermute | solution.py:230
  6.8 10.1 %collective-permute-start.5 = (bf16[16,2304]{1,0:T(8,128)(2,1)S(1)}, bf16[16,2304]{1,0:T(8,128)(2,1)S(1)}, u32[]{:S(2)}, u32[]{:S(2)}) collective-permute-start(bf16[16,2304]{1,0:T(8,128)(2,1)S(1)} %slice.17), channel_id=1, source_target_pairs={{0,4},{4,8},{8,12},{12,0},{16,20},{20,24},{24,28},{28,16},{1,5},{5... | collective-permute-start | bytes 221192 | tf_op jit(solution)/shard_map/ppermute | solution.py:221
  8.1 8.8 %collective-permute-start.6 = (bf16[16,2304]{1,0:T(8,128)(2,1)S(1)}, bf16[16,2304]{1,0:T(8,128)(2,1)S(1)}, u32[]{:S(2)}, u32[]{:S(2)}) collective-permute-start(bf16[16,2304]{1,0:T(8,128)(2,1)S(1)} %slice.17), channel_id=1, source_target_pairs={{0,12},{4,0},{8,4},{12,8},{16,28},{20,16},{24,20},{28,24},{1,13},{... | collective-permute-start | bytes 221192 | tf_op jit(solution)/shard_map/ppermute | solution.py:221
  9.6 7.4 %collective-permute-start.7 = (bf16[16,2304]{1,0:T(8,128)(2,1)S(1)}, bf16[16,2304]{1,0:T(8,128)(2,1)S(1)}, u32[]{:S(2)}, u32[]{:S(2)}) collective-permute-start(bf16[16,2304]{1,0:T(8,128)(2,1)S(1)} %slice.17), channel_id=1, source_target_pairs={{0,8},{4,12},{8,0},{12,4},{16,24},{20,28},{24,16},{28,20},{1,9},{5... | collective-permute-start | bytes 221192 | tf_op jit(solution)/shard_map/ppermute | solution.py:221
  11.2 9.4 %collective-permute-start.1 = (bf16[16,2816]{1,0:T(8,128)(2,1)S(1)}, bf16[16,2816]{1,0:T(8,128)(2,1)S(1)}, u32[]{:S(2)}, u32[]{:S(2)}) collective-permute-start(bf16[16,2816]{1,0:T(8,128)(2,1)S(1)} %get-tuple-element.49), channel_id=1, source_target_pairs={{0,32},{32,64},{64,96},{96,128},{128,160},{160,192},{192,224},{224... | collective-permute-start | bytes 270344 | tf_op jit(solution)/shard_map/ppermute | solution.py:217
  12.9 7.7 %collective-permute-start.2 = (bf16[16,2816]{1,0:T(8,128)(2,1)S(1)}, bf16[16,2816]{1,0:T(8,128)(2,1)S(1)}, u32[]{:S(2)}, u32[]{:S(2)}) collective-permute-start(bf16[16,2816]{1,0:T(8,128)(2,1)S(1)} %get-tuple-element.49), channel_id=1, source_target_pairs={{0,224},{32,0},{64,32},{96,64},{128,96},{160,128},{192,160},{224,1... | collective-permute-start | bytes 270344 | tf_op jit(solution)/shard_map/ppermute | solution.py:217
  16.9 38.7 %copy-start.6 = (bf16[64,2304]{1,0:T(8,128)(2,1)}, bf16[64,2304]{1,0:T(8,128)(2,1)S(1)}, u32[]{:S(2)}) copy-start(bf16[64,2304]{1,0:T(8,128)(2,1)S(1)} %pad_maximum_fusion.refs_0_) | copy-start | bytes 884740
  17.0 10.0 %collective-permute-start.8 = (bf16[64,2304]{1,0:T(8,128)(2,1)S(1)}, bf16[64,2304]{1,0:T(8,128)(2,1)S(1)}, u32[]{:S(2)}, u32[]{:S(2)}) collective-permute-start(bf16[64,2304]{1,0:T(8,128)(2,1)S(1)} %pad_maximum_fusion.refs_0_), channel_id=1, source_target_pairs={{0,32},{32,64},{64,96},{96,128},{128,160},{160,192},{192,224},{224... | collective-permute-start | bytes 884744 | tf_op jit(solution)/shard_map/ppermute | solution.py:217
  17.1 9.9 %collective-permute-start.9 = (bf16[64,2304]{1,0:T(8,128)(2,1)S(1)}, bf16[64,2304]{1,0:T(8,128)(2,1)S(1)}, u32[]{:S(2)}, u32[]{:S(2)}) collective-permute-start(bf16[64,2304]{1,0:T(8,128)(2,1)S(1)} %pad_maximum_fusion.refs_0_), channel_id=1, source_target_pairs={{0,224},{32,0},{64,32},{96,64},{128,96},{160,128},{192,160},{224,1... | collective-permute-start | bytes 884744 | tf_op jit(solution)/shard_map/ppermute | solution.py:217
  20.6 6.4 %collective-permute-start.3 = (bf16[16,2816]{1,0:T(8,128)(2,1)S(1)}, bf16[16,2816]{1,0:T(8,128)(2,1)S(1)}, u32[]{:S(2)}, u32[]{:S(2)}) collective-permute-start(bf16[16,2816]{1,0:T(8,128)(2,1)S(1)} %collective-permute-done.1), channel_id=1, source_target_pairs={{0,32},{32,64},{64,96},{96,128},{128,160},{160,192},{192,224},{224... | collective-permute-start | bytes 270344 | tf_op jit(solution)/shard_map/ppermute | solution.py:217
  20.6 6.5 %collective-permute-start.4 = (bf16[16,2816]{1,0:T(8,128)(2,1)S(1)}, bf16[16,2816]{1,0:T(8,128)(2,1)S(1)}, u32[]{:S(2)}, u32[]{:S(2)}) collective-permute-start(bf16[16,2816]{1,0:T(8,128)(2,1)S(1)} %collective-permute-done.2), channel_id=1, source_target_pairs={{0,224},{32,0},{64,32},{96,64},{128,96},{160,128},{192,160},{224,1... | collective-permute-start | bytes 270344 | tf_op jit(solution)/shard_map/ppermute | solution.py:217
  27.0 24.3 %copy-start.7 = (bf16[64,2304]{1,0:T(8,128)(2,1)}, bf16[64,2304]{1,0:T(8,128)(2,1)S(1)}, u32[]{:S(2)}) copy-start(bf16[64,2304]{1,0:T(8,128)(2,1)S(1)} %collective-permute-done.8.refs_1_) | copy-start | bytes 884740
  27.0 22.9 %copy-start.8 = (bf16[64,2304]{1,0:T(8,128)(2,1)}, bf16[64,2304]{1,0:T(8,128)(2,1)S(1)}, u32[]{:S(2)}) copy-start(bf16[64,2304]{1,0:T(8,128)(2,1)S(1)} %collective-permute-done.9.refs_2_) | copy-start | bytes 884740
  27.0 4.7 %collective-permute-start.10 = (bf16[16,2816]{1,0:T(8,128)(2,1)S(1)}, bf16[16,2816]{1,0:T(8,128)(2,1)S(1)}, u32[]{:S(2)}, u32[]{:S(2)}) collective-permute-start(bf16[16,2816]{1,0:T(8,128)(2,1)S(1)} %collective-permute-done.3), channel_id=1, source_target_pairs={{0,32},{32,64},{64,96},{96,128},{128,160},{160,192},{192,224},{224... | collective-permute-start | bytes 270344 | tf_op jit(solution)/shard_map/ppermute | solution.py:217
  27.1 10.4 %collective-permute-start.13 = (bf16[64,2304]{1,0:T(8,128)(2,1)S(1)}, bf16[64,2304]{1,0:T(8,128)(2,1)S(1)}, u32[]{:S(2)}, u32[]{:S(2)}) collective-permute-start(bf16[64,2304]{1,0:T(8,128)(2,1)S(1)} %collective-permute-done.8.refs_1_), channel_id=1, source_target_pairs={{0,32},{32,64},{64,96},{96,128},{128,160},{160,192},{192,224},{224... | collective-permute-start | bytes 884744 | tf_op jit(solution)/shard_map/ppermute | solution.py:217
  27.6 9.9 %collective-permute-start.14 = (bf16[64,2304]{1,0:T(8,128)(2,1)S(1)}, bf16[64,2304]{1,0:T(8,128)(2,1)S(1)}, u32[]{:S(2)}, u32[]{:S(2)}) collective-permute-start(bf16[64,2304]{1,0:T(8,128)(2,1)S(1)} %collective-permute-done.9.refs_2_), channel_id=1, source_target_pairs={{0,224},{32,0},{64,32},{96,64},{128,96},{160,128},{192,160},{224,1... | collective-permute-start | bytes 884744 | tf_op jit(solution)/shard_map/ppermute | solution.py:217
  30.2 5.4 %collective-permute-start.11 = (bf16[16,2816]{1,0:T(8,128)(2,1)S(1)}, bf16[16,2816]{1,0:T(8,128)(2,1)S(1)}, u32[]{:S(2)}, u32[]{:S(2)}) collective-permute-start(bf16[16,2816]{1,0:T(8,128)(2,1)S(1)} %collective-permute-done.4), channel_id=1, source_target_pairs={{0,224},{32,0},{64,32},{96,64},{128,96},{160,128},{192,160},{224,1... | collective-permute-start | bytes 270344 | tf_op jit(solution)/shard_map/ppermute | solution.py:217
  31.7 5.8 %collective-permute-start.12 = (bf16[16,2816]{1,0:T(8,128)(2,1)S(1)}, bf16[16,2816]{1,0:T(8,128)(2,1)S(1)}, u32[]{:S(2)}, u32[]{:S(2)}) collective-permute-start(bf16[16,2816]{1,0:T(8,128)(2,1)S(1)} %collective-permute-done.10), channel_id=1, source_target_pairs={{0,32},{32,64},{64,96},{96,128},{128,160},{160,192},{192,224},{224... | collective-permute-start | bytes 270344 | tf_op jit(solution)/shard_map/ppermute | solution.py:217
  37.5 26.3 %copy-start.3 = (bf16[128,2816]{1,0:T(8,128)(2,1)}, bf16[128,2816]{1,0:T(8,128)(2,1)S(1)}, u32[]{:S(2)}) copy-start(bf16[128,2816]{1,0:T(8,128)(2,1)S(1)} %constant_dynamic-update-slice_fusion.refs_0_) | copy-start | bytes 2162692
  37.5 12.4 %copy-start.9 = (bf16[64,2304]{1,0:T(8,128)(2,1)}, bf16[64,2304]{1,0:T(8,128)(2,1)S(1)}, u32[]{:S(2)}) copy-start(bf16[64,2304]{1,0:T(8,128)(2,1)S(1)} %collective-permute-done.13.refs_3_) | copy-start | bytes 884740
  37.5 14.1 %copy-start.10 = (bf16[64,2304]{1,0:T(8,128)(2,1)}, bf16[64,2304]{1,0:T(8,128)(2,1)S(1)}, u32[]{:S(2)}) copy-start(bf16[64,2304]{1,0:T(8,128)(2,1)S(1)} %collective-permute-done.14.refs_4_) | copy-start | bytes 884740
  37.5 12.4 %collective-permute-start.16 = (bf16[128,2816]{1,0:T(8,128)(2,1)S(1)}, bf16[128,2816]{1,0:T(8,128)(2,1)S(1)}, u32[]{:S(2)}, u32[]{:S(2)}) collective-permute-start(bf16[128,2816]{1,0:T(8,128)(2,1)S(1)} %constant_dynamic-update-slice_fusion.refs_0_), channel_id=1, source_target_pairs={{0,12},{4,0},{8,4},{12,8},{16,28},{20,16},{24,20},{28,24},{1,13},{... | collective-permute-start | bytes 2162696 | tf_op jit(solution)/shard_map/ppermute | solution.py:221
  38.1 13.2 %collective-permute-start.15 = (bf16[128,2816]{1,0:T(8,128)(2,1)S(1)}, bf16[128,2816]{1,0:T(8,128)(2,1)S(1)}, u32[]{:S(2)}, u32[]{:S(2)}) collective-permute-start(bf16[128,2816]{1,0:T(8,128)(2,1)S(1)} %constant_dynamic-update-slice_fusion.refs_0_), channel_id=1, source_target_pairs={{0,4},{4,8},{8,12},{12,0},{16,20},{20,24},{24,28},{28,16},{1,5},{5... | collective-permute-start | bytes 2162696 | tf_op jit(solution)/shard_map/ppermute | solution.py:221
  39.1 6.8 %collective-permute-start.17 = (bf16[64,2304]{1,0:T(8,128)(2,1)S(1)}, bf16[64,2304]{1,0:T(8,128)(2,1)S(1)}, u32[]{:S(2)}, u32[]{:S(2)}) collective-permute-start(bf16[64,2304]{1,0:T(8,128)(2,1)S(1)} %collective-permute-done.13.refs_3_), channel_id=1, source_target_pairs={{0,32},{32,64},{64,96},{96,128},{128,160},{160,192},{192,224},{224... | collective-permute-start | bytes 884744 | tf_op jit(solution)/shard_map/ppermute | solution.py:217
  39.5 10.5 %collective-permute-start.18 = (bf16[64,2304]{1,0:T(8,128)(2,1)S(1)}, bf16[64,2304]{1,0:T(8,128)(2,1)S(1)}, u32[]{:S(2)}, u32[]{:S(2)}) collective-permute-start(bf16[64,2304]{1,0:T(8,128)(2,1)S(1)} %collective-permute-done.14.refs_4_), channel_id=1, source_target_pairs={{0,224},{32,0},{64,32},{96,64},{128,96},{160,128},{192,160},{224,1... | collective-permute-start | bytes 884744 | tf_op jit(solution)/shard_map/ppermute | solution.py:217
  45.8 5.8 %copy-start.11 = (bf16[64,2304]{1,0:T(8,128)(2,1)}, bf16[64,2304]{1,0:T(8,128)(2,1)S(1)}, u32[]{:S(2)}) copy-start(bf16[64,2304]{1,0:T(8,128)(2,1)S(1)} %collective-permute-done.17.refs_5_) | copy-start | bytes 884740
  45.9 9.8 %collective-permute-start.21 = (bf16[64,2304]{1,0:T(8,128)(2,1)S(1)}, bf16[64,2304]{1,0:T(8,128)(2,1)}, u32[]{:S(2)}, u32[]{:S(2)}) collective-permute-start(bf16[64,2304]{1,0:T(8,128)(2,1)S(1)} %collective-permute-done.17.refs_5_), channel_id=1, source_target_pairs={{0,32},{32,64},{64,96},{96,128},{128,160},{160,192},{192,224},{224... | collective-permute-start | bytes 884744 | tf_op jit(solution)/shard_map/ppermute | solution.py:217
  49.9 13.9 %copy-start.1 = (bf16[128,2816]{1,0:T(8,128)(2,1)}, bf16[128,2816]{1,0:T(8,128)(2,1)S(1)}, u32[]{:S(2)}) copy-start(bf16[128,2816]{1,0:T(8,128)(2,1)S(1)} %collective-permute-done.16.refs_2_) | copy-start | bytes 2162692
  50.0 1.7 %copy-start.12 = (bf16[64,2304]{1,0:T(8,128)(2,1)}, bf16[64,2304]{1,0:T(8,128)(2,1)S(1)}, u32[]{:S(2)}) copy-start(bf16[64,2304]{1,0:T(8,128)(2,1)S(1)} %collective-permute-done.18.refs_6_) | copy-start | bytes 884740
  50.0 13.8 %collective-permute-start.20 = (bf16[64,2816]{1,0:T(8,128)(2,1)S(1)}, bf16[64,2816]{1,0:T(8,128)(2,1)S(1)}, u32[]{:S(2)}, u32[]{:S(2)}) collective-permute-start(bf16[64,2816]{1,0:T(8,128)(2,1)S(1)} %slice.19), channel_id=1, source_target_pairs={{0,12},{4,0},{8,4},{12,8},{16,28},{20,16},{24,20},{28,24},{1,13},{... | collective-permute-start | bytes 1081352 | tf_op jit(solution)/shard_map/ppermute | solution.py:221
  51.3 12.5 %copy-start.2 = (bf16[128,2816]{1,0:T(8,128)(2,1)}, bf16[128,2816]{1,0:T(8,128)(2,1)S(1)}, u32[]{:S(2)}) copy-start(bf16[128,2816]{1,0:T(8,128)(2,1)S(1)} %collective-permute-done.15.refs_1_) | copy-start | bytes 2162692
  51.3 12.4 %collective-permute-start.19 = (bf16[64,2816]{1,0:T(8,128)(2,1)S(1)}, bf16[64,2816]{1,0:T(8,128)(2,1)S(1)}, u32[]{:S(2)}, u32[]{:S(2)}) collective-permute-start(bf16[64,2816]{1,0:T(8,128)(2,1)S(1)} %slice.18), channel_id=1, source_target_pairs={{0,4},{4,8},{8,12},{12,0},{16,20},{20,24},{24,28},{28,16},{1,5},{5... | collective-permute-start | bytes 1081352 | tf_op jit(solution)/shard_map/ppermute | solution.py:221
  63.7 0.7 copy-start.4
  63.8 0.9 copy-start.5
  68.7 9.6 %collective-permute-start.22 = (f32[5,128,128]{2,1,0:T(8,128)}, f32[5,128,128]{2,1,0:T(8,128)S(1)}, u32[]{:S(2)}, u32[]{:S(2)}) collective-permute-start(f32[5,128,128]{2,1,0:T(8,128)} %get-tuple-element.34), channel_id=1, source_target_pairs={{0,1},{1,0},{2,3},{3,2},{4,5},{5,4},{6,7},{7,6},{8,9},{9,8},{10,11... | collective-permute-start | bytes 983048 | tf_op jit(solution)/shard_map/ppermute | solution.py:498
  79.3 9.3 %collective-permute-start.23 = (f32[5,128,128]{2,1,0:T(8,128)S(1)}, f32[5,128,128]{2,1,0:T(8,128)S(1)}, u32[]{:S(2)}, u32[]{:S(2)}) collective-permute-start(f32[5,128,128]{2,1,0:T(8,128)S(1)} %add.11), channel_id=1, source_target_pairs={{0,2},{2,0},{1,3},{3,1},{4,6},{6,4},{5,7},{7,5},{8,10},{10,8},{9,1... | collective-permute-start | bytes 983048 | tf_op jit(solution)/shard_map/ppermute | solution.py:502
  87.9 2.5 %collective-permute-start.26 = (f32[512,256]{1,0:T(8,128)}, f32[512,256]{1,0:T(8,128)S(1)}, u32[]{:S(2)}, u32[]{:S(2)}) collective-permute-start(f32[512,256]{1,0:T(8,128)} %get-tuple-element.48), channel_id=1, source_target_pairs={{0,1},{1,0},{2,3},{3,2},{4,5},{5,4},{6,7},{7,6},{8,9},{9,8},{10,11... | collective-permute-start | bytes 1572872 | tf_op jit(solution)/shard_map/ppermute | solution.py:498
  88.7 3.8 %collective-permute-start.24 = (f32[5,128,128]{2,1,0:T(8,128)S(1)}, f32[5,128,128]{2,1,0:T(8,128)S(1)}, u32[]{:S(2)}, u32[]{:S(2)}) collective-permute-start(f32[5,128,128]{2,1,0:T(8,128)S(1)} %add.12.mine_ref), channel_id=1, source_target_pairs={{0,1},{1,0},{2,3},{3,2},{4,5},{5,4},{6,7},{7,6},{8,9},{9,8},{10,11... | collective-permute-start | bytes 983048 | tf_op jit(solution)/shard_map/ppermute | solution.py:498
  89.9 16.2 %collective-permute-start.25 = (f32[512,256]{1,0:T(8,128)}, f32[512,256]{1,0:T(8,128)S(1)}, u32[]{:S(2)}, u32[]{:S(2)}) collective-permute-start(f32[512,256]{1,0:T(8,128)} %get-tuple-element.46), channel_id=1, source_target_pairs={{0,1},{1,0},{2,3},{3,2},{4,5},{5,4},{6,7},{7,6},{8,9},{9,8},{10,11... | collective-permute-start | bytes 1572872 | tf_op jit(solution)/shard_map/ppermute | solution.py:498
  91.5 14.6 %copy-start = (f32[512,256]{1,0:T(8,128)S(1)}, f32[512,256]{1,0:T(8,128)}, u32[]{:S(2)}) copy-start(f32[512,256]{1,0:T(8,128)} %get-tuple-element.42.keep_ref) | copy-start | bytes 1572868
  91.5 14.6 %collective-permute-start.27 = (f32[512,256]{1,0:T(8,128)S(1)}, f32[512,256]{1,0:T(8,128)S(1)}, u32[]{:S(2)}, u32[]{:S(2)}) collective-permute-start(f32[512,256]{1,0:T(8,128)S(1)} %add.13), channel_id=1, source_target_pairs={{0,2},{2,0},{1,3},{3,1},{4,6},{6,4},{5,7},{7,5},{8,10},{10,8},{9,1... | collective-permute-start | bytes 1572872 | tf_op jit(solution)/shard_map/ppermute | solution.py:502

commit v5 on v4

--- a/solution.py
+++ b/solution.py
@@ -10,8 +10,8 @@
 ROW0 = (((0,), (0,)), ((), ()))
 NB = 128
 PANEL = 512
-FIRST_K = 2304
-SECOND_K = 2816
+FIRST_K = 1920
+SECOND_K = 3200
 CHUNK_K = 1024
 HALVES = (((0, 0), (0, 1), (0, 2), (0, 3), (3, 3)), ((1, 1), (1, 2), (1, 3), (2, 2), (2, 3)))
 
@@ -246,19 +246,21 @@
     turn(column, column_z, 1)
     turn(planes, plane_z, 1)
     turn(column, column_z, 2)
+    batches = [jnp.concatenate(column, 0)]
+    x_up, x_down = [along_x(1, batches[0])], [along_x(-1, batches[0])]
     turn(column, column_z, 3, *planes[1:3])
     column_z.append(4)
     column.append(along_z(1, column[-2]))
     turn(planes, plane_z, 2)
-    column = jnp.concatenate(column, 0)
-    half = column.shape[0] // 2
-    column = after(column, *planes[3:5])
-    x_up, x_down = along_x(1, column), along_x(-1, column)
+    batches.append(after(jnp.concatenate(column[5:], 0), *planes[3:5]))
+    x_up.append(along_x(1, batches[1]))
+    x_down.append(along_x(-1, batches[1]))
+    x_far = [along_x(1, x_up[0][:48]), along_x(-1, x_down[0][48:])]
     turn(planes, plane_z, 3)
-    x_far = (
-        along_x(1, after(x_up[:half], *planes[5:7])),
-        along_x(-1, after(x_down[half:], *planes[5:7])),
-    )
+    x_far += [
+        along_x(1, after(x_up[1][:16], *planes[5:7])),
+        along_x(-1, after(x_down[1][16:], *planes[5:7])),
+    ]
     planes.append(along_z(1, planes[-2]))
     plane_z.append(4)
 
@@ -267,11 +269,16 @@
     ]
     columns, column_places = [], []
     for piece, dx, units in (
-        (column, 0, range(8)),
-        (x_up, -1, range(8)),
-        (x_down, 1, range(8)),
-        (x_far[0], 2, range(4)),
-        (x_far[1], 2, range(4, 8)),
+        (batches[0], 0, range(5)),
+        (batches[1], 0, range(5, 8)),
+        (x_up[0], -1, range(5)),
+        (x_up[1], -1, range(5, 8)),
+        (x_down[0], 1, range(5)),
+        (x_down[1], 1, range(5, 8)),
+        (x_far[0], 2, range(3)),
+        (x_far[1], 2, range(3, 5)),
+        (x_far[2], 2, range(5, 6)),
+        (x_far[3], 2, range(6, 8)),
     ):
         column_places += [(len(columns), 16 * k, column_z[m], dx) for k, m in enumerate(units)]
         columns.append(piece)

time: 110 us -> 106 us (0.964)
  waiting for transfers between devices: 25.7 us -> 17.2 us
  starting transfers between devices: 43.2 us -> 46.8 us
    ppermute x14, waiting for transfers between devices: 17.7 us -> 8.47 us  [along_z(): return lax.ppermute(v, 'prow', z_shift(k))]
    ppermute x7 -> x11, starting transfers between devices: 7.5 us -> 12.3 us  [along_x(): return lax.ppermute(v, 'pcol', x_shift(k))]
    ppermute x4, starting transfers between devices: 10.2 us -> 8.37 us  [swap_cores(): return lax.ppermute(v, 'orb', CORE_SWAP)]
    ppermute x14, starting transfers between devices: 19.2 us -> 20.7 us  [along_z(): return lax.ppermute(v, 'prow', z_shift(k))]
    ppermute x7 -> x11, waiting for transfers between devices: 4.06 us -> 4.13 us  [along_x(): return lax.ppermute(v, 'pcol', x_shift(k))]
  transfers between devices with their start and end apart: 28 -> 32, of which waited for: 10 -> 8; matrix products, arithmetic and copies ran while one was open for 1% -> 2% of each run, Pallas kernels for 26% -> 27%
where the time goes in v5:
time: 106 us; the launch traced here: 105 us
  starting transfers between devices  46.8 us (44%)
  Pallas kernels  35.9 us (34%)
  waiting for transfers between devices  17.2 us (16%)
  other arithmetic  3.21 us (3%)
  local copies, waits for them, and re-layouts  1.65 us (2%)
    ppermute x14, starting transfers between devices, along_z(): return lax.ppermute(v, 'prow', z_shift(k))  20.7 us
    pallas_call x1, Pallas kernels, factorise(): pl.pallas_call(factor_kernel, out_shape=(jax.ShapeDtypeStruct((blocks, NB...  13.6 us
    ppermute x11, starting transfers between devices, along_x(): return lax.ppermute(v, 'pcol', x_shift(k))  12.3 us
    ppermute x14, waiting for transfers between devices, along_z(): return lax.ppermute(v, 'prow', z_shift(k))  8.47 us
    ppermute x4, starting transfers between devices, swap_cores(): return lax.ppermute(v, 'orb', CORE_SWAP)  8.37 us
    pallas_call x1, Pallas kernels, row_gram(): pl.pallas_call(lambda *refs: rows_kernel(places, len(pieces), *refs), in_...  7.66 us
    pallas_call x1, Pallas kernels, first_grams(): pl.pallas_call(lambda *refs: first_kernel(places, len(pieces), *refs), in...  7.06 us
    pallas_call x1, Pallas kernels, panel_gram(): pl.pallas_call(lambda *refs: panel_kernel(places, len(pieces), *refs), in...  4.5 us
  transfers between devices with their start and end apart: 32, of which 8 were waited for; matrix products, arithmetic and copies ran while one was open for 2% of the time, Pallas kernels for 27%

profile of v5, /device:TPU:1, one launch (start us, length us, event | category | flops | bytes accessed | tf_op | source)
XLA Modules:
  0.0 105.1 jit_solution(6546237588456402757)
XLA Ops:
  0.0 3.7 %collective-permute-start = (bf16[8,5000]{1,0:T(8,128)(2,1)}, bf16[8,5000]{1,0:T(8,128)(2,1)S(1)}, u32[]{:S(2)}, u32[]{:S(2)}) collective-permute-start(bf16[8,5000]{1,0:T(8,128)(2,1)} %bitcast.1), channel_id=1, source_target_pairs={{0,16},{4,20},{8,24},{12,28},{16,0},{20,4},{24,8},{28,12},{1,17},{... | collective-permute-start | bytes 240008 | tf_op jit(solution)/shard_map/ppermute | solution.py:230
  3.7 2.0 %collective-permute-done = bf16[8,5000]{1,0:T(8,128)(2,1)S(1)} collective-permute-done((bf16[8,5000]{1,0:T(8,128)(2,1)}, bf16[8,5000]{1,0:T(8,128)(2,1)S(1)}, u32[]{:S(2)}, u32[]{:S(2)}) %collective-permute-start) | collective-permute-done | bytes 80032 | tf_op jit(solution)/shard_map/ppermute | solution.py:230
  5.8 1.0 maximum_select_fusion
  6.8 1.3 %collective-permute-start.5 = (bf16[16,1920]{1,0:T(8,128)(2,1)S(1)}, bf16[16,1920]{1,0:T(8,128)(2,1)S(1)}, u32[]{:S(2)}, u32[]{:S(2)}) collective-permute-start(bf16[16,1920]{1,0:T(8,128)(2,1)S(1)} %slice.25), channel_id=1, source_target_pairs={{0,4},{4,8},{8,12},{12,0},{16,20},{20,24},{24,28},{28,16},{1,5},{5... | collective-permute-start | bytes 184328 | tf_op jit(solution)/shard_map/ppermute | solution.py:221
  8.1 1.4 %collective-permute-start.6 = (bf16[16,1920]{1,0:T(8,128)(2,1)S(1)}, bf16[16,1920]{1,0:T(8,128)(2,1)S(1)}, u32[]{:S(2)}, u32[]{:S(2)}) collective-permute-start(bf16[16,1920]{1,0:T(8,128)(2,1)S(1)} %slice.25), channel_id=1, source_target_pairs={{0,12},{4,0},{8,4},{12,8},{16,28},{20,16},{24,20},{28,24},{1,13},{... | collective-permute-start | bytes 184328 | tf_op jit(solution)/shard_map/ppermute | solution.py:221
  9.6 1.6 %collective-permute-start.7 = (bf16[16,1920]{1,0:T(8,128)(2,1)S(1)}, bf16[16,1920]{1,0:T(8,128)(2,1)S(1)}, u32[]{:S(2)}, u32[]{:S(2)}) collective-permute-start(bf16[16,1920]{1,0:T(8,128)(2,1)S(1)} %slice.25), channel_id=1, source_target_pairs={{0,8},{4,12},{8,0},{12,4},{16,24},{20,28},{24,16},{28,20},{1,9},{5... | collective-permute-start | bytes 184328 | tf_op jit(solution)/shard_map/ppermute | solution.py:221
  11.2 1.7 %collective-permute-start.1 = (bf16[16,3200]{1,0:T(8,128)(2,1)S(1)}, bf16[16,3200]{1,0:T(8,128)(2,1)S(1)}, u32[]{:S(2)}, u32[]{:S(2)}) collective-permute-start(bf16[16,3200]{1,0:T(8,128)(2,1)S(1)} %get-tuple-element.59), channel_id=1, source_target_pairs={{0,32},{32,64},{64,96},{96,128},{128,160},{160,192},{192,224},{224... | collective-permute-start | bytes 307208 | tf_op jit(solution)/shard_map/ppermute | solution.py:217
  12.9 4.0 %collective-permute-start.2 = (bf16[16,3200]{1,0:T(8,128)(2,1)S(1)}, bf16[16,3200]{1,0:T(8,128)(2,1)S(1)}, u32[]{:S(2)}, u32[]{:S(2)}) collective-permute-start(bf16[16,3200]{1,0:T(8,128)(2,1)S(1)} %get-tuple-element.59), channel_id=1, source_target_pairs={{0,224},{32,0},{64,32},{96,64},{128,96},{160,128},{192,160},{224,1... | collective-permute-start | bytes 307208 | tf_op jit(solution)/shard_map/ppermute | solution.py:217
  16.9 0.0 collective-permute-done.5
  17.0 0.0 copy-start.8
  17.0 0.1 collective-permute-start.8
  17.1 3.3 %collective-permute-start.9 = (bf16[64,1920]{1,0:T(8,128)(2,1)S(1)}, bf16[64,1920]{1,0:T(8,128)(2,1)S(1)}, u32[]{:S(2)}, u32[]{:S(2)}) collective-permute-start(bf16[64,1920]{1,0:T(8,128)(2,1)S(1)} %pad_maximum_fusion.1.refs_0_), channel_id=1, source_target_pairs={{0,224},{32,0},{64,32},{96,64},{128,96},{160,128},{192,160},{224,1... | collective-permute-start | bytes 737288 | tf_op jit(solution)/shard_map/ppermute | solution.py:217
  20.3 0.0 collective-permute-done.1
  20.3 2.7 %collective-permute-start.4 = (bf16[16,3200]{1,0:T(8,128)(2,1)S(1)}, bf16[16,3200]{1,0:T(8,128)(2,1)S(1)}, u32[]{:S(2)}, u32[]{:S(2)}) collective-permute-start(bf16[16,3200]{1,0:T(8,128)(2,1)S(1)} %collective-permute-done.2), channel_id=1, source_target_pairs={{0,224},{32,0},{64,32},{96,64},{128,96},{160,128},{192,160},{224,1... | collective-permute-start | bytes 307208 | tf_op jit(solution)/shard_map/ppermute | solution.py:217
  23.0 3.6 %collective-permute-done.3 = bf16[16,3200]{1,0:T(8,128)(2,1)S(1)} collective-permute-done((bf16[16,3200]{1,0:T(8,128)(2,1)S(1)}, bf16[16,3200]{1,0:T(8,128)(2,1)S(1)}, u32[]{:S(2)}, u32[]{:S(2)}) %collective-permute-start.3) | collective-permute-done | bytes 102432 | tf_op jit(solution)/shard_map/ppermute | solution.py:217
  26.6 0.0 collective-permute-done.9.refs_2_
  26.6 0.1 collective-permute-start.10
  26.7 0.5 collective-permute-start.13
  27.2 2.4 %collective-permute-start.11 = (bf16[16,3200]{1,0:T(8,128)(2,1)S(1)}, bf16[16,3200]{1,0:T(8,128)(2,1)S(1)}, u32[]{:S(2)}, u32[]{:S(2)}) collective-permute-start(bf16[16,3200]{1,0:T(8,128)(2,1)S(1)} %collective-permute-done.4), channel_id=1, source_target_pairs={{0,224},{32,0},{64,32},{96,64},{128,96},{160,128},{192,160},{224,1... | collective-permute-start | bytes 307208 | tf_op jit(solution)/shard_map/ppermute | solution.py:217
  29.6 1.8 %collective-permute-done.10 = bf16[16,3200]{1,0:T(8,128)(2,1)S(1)} collective-permute-done((bf16[16,3200]{1,0:T(8,128)(2,1)S(1)}, bf16[16,3200]{1,0:T(8,128)(2,1)S(1)}, u32[]{:S(2)}, u32[]{:S(2)}) %collective-permute-start.10) | collective-permute-done | bytes 102432 | tf_op jit(solution)/shard_map/ppermute | solution.py:217
  31.4 0.0 collective-permute-start.12
  31.4 0.7 collective-permute-start.15
  32.1 2.1 %collective-permute-start.17 = (bf16[80,3200]{1,0:T(8,128)(2,1)S(1)}, bf16[80,3200]{1,0:T(8,128)(2,1)S(1)}, u32[]{:S(2)}, u32[]{:S(2)}) collective-permute-start(bf16[80,3200]{1,0:T(8,128)(2,1)S(1)} %constant_dynamic-update-slice_fusion.refs_0_), channel_id=1, source_target_pairs={{0,12},{4,0},{8,4},{12,8},{16,28},{20,16},{24,20},{28,24},{1,13},{... | collective-permute-start | bytes 1536008 | tf_op jit(solution)/shard_map/ppermute | solution.py:221
  34.2 0.0 collective-permute-done.13.refs_3_
  34.2 2.7 %collective-permute-start.14 = (bf16[64,1920]{1,0:T(8,128)(2,1)S(1)}, bf16[64,1920]{1,0:T(8,128)(2,1)S(1)}, u32[]{:S(2)}, u32[]{:S(2)}) collective-permute-start(bf16[64,1920]{1,0:T(8,128)(2,1)S(1)} %collective-permute-done.9.refs_2_), channel_id=1, source_target_pairs={{0,224},{32,0},{64,32},{96,64},{128,96},{160,128},{192,160},{224,1... | collective-permute-start | bytes 737288 | tf_op jit(solution)/shard_map/ppermute | solution.py:217
  36.9 0.0 collective-permute-done.11
  36.9 0.0 collective-permute-start.21
  36.9 0.6 collective-permute-done.12
  37.6 2.5 %collective-permute-done.14.refs_4_ = bf16[64,1920]{1,0:T(8,128)(2,1)S(1)} collective-permute-done((bf16[64,1920]{1,0:T(8,128)(2,1)S(1)}, bf16[64,1920]{1,0:T(8,128)(2,1)S(1)}, u32[]{:S(2)}, u32[]{:S(2)}) %collective-permute-start.14) | collective-permute-done | bytes 245792 | tf_op jit(solution)/shard_map/ppermute | solution.py:217
  40.0 0.6 collective-permute-start.18
  40.7 0.8 collective-permute-start.16
  41.5 3.2 %collective-permute-start.22 = (bf16[64,1920]{1,0:T(8,128)(2,1)S(1)}, bf16[64,1920]{1,0:T(8,128)(2,1)S(1)}, u32[]{:S(2)}, u32[]{:S(2)}) collective-permute-start(bf16[64,1920]{1,0:T(8,128)(2,1)S(1)} %collective-permute-done.14.refs_4_), channel_id=1, source_target_pairs={{0,224},{32,0},{64,32},{96,64},{128,96},{160,128},{192,160},{224,1... | collective-permute-start | bytes 737288 | tf_op jit(solution)/shard_map/ppermute | solution.py:217
  44.7 0.1 collective-permute-start.25
  44.8 0.2 collective-permute-start.19
  45.0 4.1 %collective-permute-done.18.refs_5_ = bf16[48,3200]{1,0:T(8,128)(2,1)S(1)} collective-permute-done((bf16[48,3200]{1,0:T(8,128)(2,1)S(1)}, bf16[48,3200]{1,0:T(8,128)(2,1)S(1)}, u32[]{:S(2)}, u32[]{:S(2)}) %collective-permute-start.18) | collective-permute-done | bytes 307232 | tf_op jit(solution)/shard_map/ppermute | solution.py:221
  49.1 2.1 %collective-permute-start.20 = (bf16[32,3200]{1,0:T(8,128)(2,1)S(1)}, bf16[32,3200]{1,0:T(8,128)(2,1)S(1)}, u32[]{:S(2)}, u32[]{:S(2)}) collective-permute-start(bf16[32,3200]{1,0:T(8,128)(2,1)S(1)} %slice.27), channel_id=1, source_target_pairs={{0,12},{4,0},{8,4},{12,8},{16,28},{20,16},{24,20},{28,24},{1,13},{... | collective-permute-start | bytes 614408 | tf_op jit(solution)/shard_map/ppermute | solution.py:221
  51.2 0.1 collective-permute-start.24
  51.3 0.0 collective-permute-done.16.refs_3_
  51.3 0.7 slice.28
  52.1 1.4 %collective-permute-start.23 = (bf16[16,3200]{1,0:T(8,128)(2,1)}, bf16[16,3200]{1,0:T(8,128)(2,1)S(1)}, u32[]{:S(2)}, u32[]{:S(2)}) collective-permute-start(bf16[16,3200]{1,0:T(8,128)(2,1)} %slice.28), channel_id=1, source_target_pairs={{0,4},{4,8},{8,12},{12,0},{16,20},{20,24},{24,28},{28,16},{1,5},{5... | collective-permute-start | bytes 307208 | tf_op jit(solution)/shard_map/ppermute | solution.py:221
  53.5 0.0 collective-permute-done.25.refs_7_
  53.5 7.1 %first_grams.1 = (f32[2,5,128,128]{3,2,1,0:T(8,128)}, f32[4,512,256]{2,1,0:T(8,128)}) custom-call(bf16[64,1920]{1,0:T(8,128)(2,1)} %copy-done.8, bf16[64,1920]{1,0:T(8,128)(2,1)} %copy-done.11, bf16[64,1920]{1,0:T(8,128)(2,1)} %copy-done.12, bf16[64,1920]{1,0:T(8,128)(2,1)} %copy-done.13, bf16[64,1920]{1,0:T(8,128)(2,1)} %copy-done.14, ...), custom_call_target="tpu_custom_call" | custom-call | flops 5000000000 | bytes 12582912 | tf_op jit(solution)/shard_map/first_grams/pallas_call | solution.py:441
  60.6 0.0 collective-permute-done.20.refs_7_
  60.6 0.0 collective-permute-done.24.refs_9_
  60.7 0.6 copy-done.9
  61.3 0.0 copy-done.10
  61.3 0.1 copy-done.7
  61.4 4.5 %panel_gram.1 = (f32[5,128,128]{2,1,0:T(8,128)}, f32[5,128,128]{2,1,0:T(8,128)}) custom-call(bf16[80,3200]{1,0:T(8,128)(2,1)} %copy-done.5, bf16[48,3200]{1,0:T(8,128)(2,1)} %copy-done.2, bf16[80,3200]{1,0:T(8,128)(2,1)} %copy-done.1, bf16[48,3200]{1,0:T(8,128)(2,1)} %copy-done.6, bf16[80,3200]{1,0:T(8,128)(2,1)} %copy-done.3, bf16[48,3200]{1,0:T(8,128)(2,1)} %copy-done.4, ...), custom_call_target="tpu_custom_call" | custom-call | flops 1500000000 | bytes 4194304 | tf_op jit(solution)/shard_map/panel_gram/pallas_call | solution.py:463
  65.9 7.0 %collective-permute-start.26 = (f32[5,128,128]{2,1,0:T(8,128)}, f32[5,128,128]{2,1,0:T(8,128)S(1)}, u32[]{:S(2)}, u32[]{:S(2)}) collective-permute-start(f32[5,128,128]{2,1,0:T(8,128)} %get-tuple-element.39), channel_id=1, source_target_pairs={{0,1},{1,0},{2,3},{3,2},{4,5},{5,4},{6,7},{7,6},{8,9},{9,8},{10,11... | collective-permute-start | bytes 983048 | tf_op jit(solution)/shard_map/ppermute | solution.py:505
  73.0 1.5 %collective-permute-done.26 = f32[5,128,128]{2,1,0:T(8,128)S(1)} collective-permute-done((f32[5,128,128]{2,1,0:T(8,128)}, f32[5,128,128]{2,1,0:T(8,128)S(1)}, u32[]{:S(2)}, u32[]{:S(2)}) %collective-permute-start.26) | collective-permute-done | bytes 327712 | tf_op jit(solution)/shard_map/ppermute | solution.py:505
  74.4 1.0 add.11
  75.4 1.4 %collective-permute-start.27 = (f32[5,128,128]{2,1,0:T(8,128)S(1)}, f32[5,128,128]{2,1,0:T(8,128)S(1)}, u32[]{:S(2)}, u32[]{:S(2)}) collective-permute-start(f32[5,128,128]{2,1,0:T(8,128)S(1)} %add.11), channel_id=1, source_target_pairs={{0,2},{2,0},{1,3},{3,1},{4,6},{6,4},{5,7},{7,5},{8,10},{10,8},{9,1... | collective-permute-start | bytes 983048 | tf_op jit(solution)/shard_map/ppermute | solution.py:509
  76.8 7.7 %row_gram.1 = (f32[512,256]{1,0:T(8,128)}, f32[512,256]{1,0:T(8,128)}, f32[512,256]{1,0:T(8,128)}, f32[512,256]{1,0:T(8,128)}) custom-call(bf16[80,3200]{1,0:T(8,128)(2,1)} %copy-done.5, bf16[48,3200]{1,0:T(8,128)(2,1)} %copy-done.2, bf16[80,3200]{1,0:T(8,128)(2,1)} %copy-done.1, bf16[48,3200]{1,0:T(8,128)(2,1)} %copy-done.6, bf16[80,3200]{1,0:T(8,128)(2,1)} %copy-done.3, ...), custom_call_target="tpu_custom_call" | custom-call | flops 4000000000 | bytes 12582912 | tf_op jit(solution)/shard_map/row_gram/pallas_call | solution.py:484
  84.5 0.7 collective-permute-start.30
  85.2 0.0 collective-permute-done.27
  85.3 0.5 collective-permute-start.28
  85.8 0.1 collective-permute-start.29
  85.9 1.1 %collective-permute-done.30 = f32[512,256]{1,0:T(8,128)S(1)} collective-permute-done((f32[512,256]{1,0:T(8,128)}, f32[512,256]{1,0:T(8,128)S(1)}, u32[]{:S(2)}, u32[]{:S(2)}) %collective-permute-start.30) | collective-permute-done | bytes 524320 | tf_op jit(solution)/shard_map/ppermute | solution.py:505
  87.0 1.1 %add.13 = f32[512,256]{1,0:T(8,128)S(1)} add(f32[512,256]{1,0:T(8,128)} %get-tuple-element.57, f32[512,256]{1,0:T(8,128)S(1)} %collective-permute-done.30) | non-fusion elementwise | flops 131072 | bytes 1572864 | tf_op jit(solution)/shard_map/add | solution.py:521
  88.1 0.3 collective-permute-start.31
  88.4 0.0 collective-permute-done.28.other_ref
  88.4 13.6 %factor.1 = (f32[4,128,128]{2,1,0:T(8,128)S(1)}, f32[3,128,512]{2,1,0:T(8,128)S(1)}) custom-call(f32[5,128,128]{2,1,0:T(8,128)S(1)} %add.12.mine_ref, f32[5,128,128]{2,1,0:T(8,128)S(1)} %collective-permute-done.28.other_ref), custom_call_target="tpu_custom_call" | custom-call | flops 30000001024 | bytes 3145728 | tf_op jit(solution)/shard_map/factor/pallas_call | solution.py:190
  102.0 0.0 collective-permute-done.31.other_ref
  102.0 3.1 %solve.1 = f32[512,256]{1,0:T(8,128)} custom-call(f32[4,128,128]{2,1,0:T(8,128)S(1)} %get-tuple-element.54.inv_ref, f32[3,128,512]{2,1,0:T(8,128)S(1)} %get-tuple-element.55.upper_ref, f32[512,256]{1,0:T(8,128)S(1)} %copy-done, f32[512,256]{1,0:T(8,128)S(1)} %collective-permute-done.29.arrived_ref, f32[512,256]{1,0:T(8,128)S(1)} %collective-permute-done.31.other_ref), custom_call_target="tpu_custom_call" | custom-call | tf_op jit(solution)/shard_map/solve/pallas_call | solution.py:204
  (56 shorter events, 0.3 us)
Async XLA Ops:
  0.0 5.8 %collective-permute-start = (bf16[8,5000]{1,0:T(8,128)(2,1)}, bf16[8,5000]{1,0:T(8,128)(2,1)S(1)}, u32[]{:S(2)}, u32[]{:S(2)}) collective-permute-start(bf16[8,5000]{1,0:T(8,128)(2,1)} %bitcast.1), channel_id=1, source_target_pairs={{0,16},{4,20},{8,24},{12,28},{16,0},{20,4},{24,8},{28,12},{1,17},{... | collective-permute-start | bytes 240008 | tf_op jit(solution)/shard_map/ppermute | solution.py:230
  6.8 10.1 %collective-permute-start.5 = (bf16[16,1920]{1,0:T(8,128)(2,1)S(1)}, bf16[16,1920]{1,0:T(8,128)(2,1)S(1)}, u32[]{:S(2)}, u32[]{:S(2)}) collective-permute-start(bf16[16,1920]{1,0:T(8,128)(2,1)S(1)} %slice.25), channel_id=1, source_target_pairs={{0,4},{4,8},{8,12},{12,0},{16,20},{20,24},{24,28},{28,16},{1,5},{5... | collective-permute-start | bytes 184328 | tf_op jit(solution)/shard_map/ppermute | solution.py:221
  8.1 8.8 %collective-permute-start.6 = (bf16[16,1920]{1,0:T(8,128)(2,1)S(1)}, bf16[16,1920]{1,0:T(8,128)(2,1)S(1)}, u32[]{:S(2)}, u32[]{:S(2)}) collective-permute-start(bf16[16,1920]{1,0:T(8,128)(2,1)S(1)} %slice.25), channel_id=1, source_target_pairs={{0,12},{4,0},{8,4},{12,8},{16,28},{20,16},{24,20},{28,24},{1,13},{... | collective-permute-start | bytes 184328 | tf_op jit(solution)/shard_map/ppermute | solution.py:221
  9.6 7.4 %collective-permute-start.7 = (bf16[16,1920]{1,0:T(8,128)(2,1)S(1)}, bf16[16,1920]{1,0:T(8,128)(2,1)S(1)}, u32[]{:S(2)}, u32[]{:S(2)}) collective-permute-start(bf16[16,1920]{1,0:T(8,128)(2,1)S(1)} %slice.25), channel_id=1, source_target_pairs={{0,8},{4,12},{8,0},{12,4},{16,24},{20,28},{24,16},{28,20},{1,9},{5... | collective-permute-start | bytes 184328 | tf_op jit(solution)/shard_map/ppermute | solution.py:221
  11.2 9.1 %collective-permute-start.1 = (bf16[16,3200]{1,0:T(8,128)(2,1)S(1)}, bf16[16,3200]{1,0:T(8,128)(2,1)S(1)}, u32[]{:S(2)}, u32[]{:S(2)}) collective-permute-start(bf16[16,3200]{1,0:T(8,128)(2,1)S(1)} %get-tuple-element.59), channel_id=1, source_target_pairs={{0,32},{32,64},{64,96},{96,128},{128,160},{160,192},{192,224},{224... | collective-permute-start | bytes 307208 | tf_op jit(solution)/shard_map/ppermute | solution.py:217
  12.9 7.4 %collective-permute-start.2 = (bf16[16,3200]{1,0:T(8,128)(2,1)S(1)}, bf16[16,3200]{1,0:T(8,128)(2,1)S(1)}, u32[]{:S(2)}, u32[]{:S(2)}) collective-permute-start(bf16[16,3200]{1,0:T(8,128)(2,1)S(1)} %get-tuple-element.59), channel_id=1, source_target_pairs={{0,224},{32,0},{64,32},{96,64},{128,96},{160,128},{192,160},{224,1... | collective-permute-start | bytes 307208 | tf_op jit(solution)/shard_map/ppermute | solution.py:217
  17.0 36.5 %copy-start.8 = (bf16[64,1920]{1,0:T(8,128)(2,1)}, bf16[64,1920]{1,0:T(8,128)(2,1)S(1)}, u32[]{:S(2)}) copy-start(bf16[64,1920]{1,0:T(8,128)(2,1)S(1)} %pad_maximum_fusion.1.refs_0_) | copy-start | bytes 737284
  17.0 9.6 %collective-permute-start.8 = (bf16[64,1920]{1,0:T(8,128)(2,1)S(1)}, bf16[64,1920]{1,0:T(8,128)(2,1)S(1)}, u32[]{:S(2)}, u32[]{:S(2)}) collective-permute-start(bf16[64,1920]{1,0:T(8,128)(2,1)S(1)} %pad_maximum_fusion.1.refs_0_), channel_id=1, source_target_pairs={{0,32},{32,64},{64,96},{96,128},{128,160},{160,192},{192,224},{224... | collective-permute-start | bytes 737288 | tf_op jit(solution)/shard_map/ppermute | solution.py:217
  17.1 9.5 %collective-permute-start.9 = (bf16[64,1920]{1,0:T(8,128)(2,1)S(1)}, bf16[64,1920]{1,0:T(8,128)(2,1)S(1)}, u32[]{:S(2)}, u32[]{:S(2)}) collective-permute-start(bf16[64,1920]{1,0:T(8,128)(2,1)S(1)} %pad_maximum_fusion.1.refs_0_), channel_id=1, source_target_pairs={{0,224},{32,0},{64,32},{96,64},{128,96},{160,128},{192,160},{224,1... | collective-permute-start | bytes 737288 | tf_op jit(solution)/shard_map/ppermute | solution.py:217
  20.3 6.3 %collective-permute-start.3 = (bf16[16,3200]{1,0:T(8,128)(2,1)S(1)}, bf16[16,3200]{1,0:T(8,128)(2,1)S(1)}, u32[]{:S(2)}, u32[]{:S(2)}) collective-permute-start(bf16[16,3200]{1,0:T(8,128)(2,1)S(1)} %collective-permute-done.1), channel_id=1, source_target_pairs={{0,32},{32,64},{64,96},{96,128},{128,160},{160,192},{192,224},{224... | collective-permute-start | bytes 307208 | tf_op jit(solution)/shard_map/ppermute | solution.py:217
  20.3 6.9 %collective-permute-start.4 = (bf16[16,3200]{1,0:T(8,128)(2,1)S(1)}, bf16[16,3200]{1,0:T(8,128)(2,1)S(1)}, u32[]{:S(2)}, u32[]{:S(2)}) collective-permute-start(bf16[16,3200]{1,0:T(8,128)(2,1)S(1)} %collective-permute-done.2), channel_id=1, source_target_pairs={{0,224},{32,0},{64,32},{96,64},{128,96},{160,128},{192,160},{224,1... | collective-permute-start | bytes 307208 | tf_op jit(solution)/shard_map/ppermute | solution.py:217
  26.6 13.4 %copy-start.11 = (bf16[64,1920]{1,0:T(8,128)(2,1)}, bf16[64,1920]{1,0:T(8,128)(2,1)S(1)}, u32[]{:S(2)}) copy-start(bf16[64,1920]{1,0:T(8,128)(2,1)S(1)} %collective-permute-done.8.refs_1_) | copy-start | bytes 737284
  26.6 13.4 %copy-start.12 = (bf16[64,1920]{1,0:T(8,128)(2,1)}, bf16[64,1920]{1,0:T(8,128)(2,1)S(1)}, u32[]{:S(2)}) copy-start(bf16[64,1920]{1,0:T(8,128)(2,1)S(1)} %collective-permute-done.9.refs_2_) | copy-start | bytes 737284
  26.6 4.8 %collective-permute-start.10 = (bf16[16,3200]{1,0:T(8,128)(2,1)S(1)}, bf16[16,3200]{1,0:T(8,128)(2,1)S(1)}, u32[]{:S(2)}, u32[]{:S(2)}) collective-permute-start(bf16[16,3200]{1,0:T(8,128)(2,1)S(1)} %collective-permute-done.3), channel_id=1, source_target_pairs={{0,32},{32,64},{64,96},{96,128},{128,160},{160,192},{192,224},{224... | collective-permute-start | bytes 307208 | tf_op jit(solution)/shard_map/ppermute | solution.py:217
  26.7 7.5 %collective-permute-start.13 = (bf16[64,1920]{1,0:T(8,128)(2,1)S(1)}, bf16[64,1920]{1,0:T(8,128)(2,1)S(1)}, u32[]{:S(2)}, u32[]{:S(2)}) collective-permute-start(bf16[64,1920]{1,0:T(8,128)(2,1)S(1)} %collective-permute-done.8.refs_1_), channel_id=1, source_target_pairs={{0,32},{32,64},{64,96},{96,128},{128,160},{160,192},{192,224},{224... | collective-permute-start | bytes 737288 | tf_op jit(solution)/shard_map/ppermute | solution.py:217
  27.2 9.7 %collective-permute-start.11 = (bf16[16,3200]{1,0:T(8,128)(2,1)S(1)}, bf16[16,3200]{1,0:T(8,128)(2,1)S(1)}, u32[]{:S(2)}, u32[]{:S(2)}) collective-permute-start(bf16[16,3200]{1,0:T(8,128)(2,1)S(1)} %collective-permute-done.4), channel_id=1, source_target_pairs={{0,224},{32,0},{64,32},{96,64},{128,96},{160,128},{192,160},{224,1... | collective-permute-start | bytes 307208 | tf_op jit(solution)/shard_map/ppermute | solution.py:217
  31.4 6.1 %collective-permute-start.12 = (bf16[16,3200]{1,0:T(8,128)(2,1)S(1)}, bf16[16,3200]{1,0:T(8,128)(2,1)S(1)}, u32[]{:S(2)}, u32[]{:S(2)}) collective-permute-start(bf16[16,3200]{1,0:T(8,128)(2,1)S(1)} %collective-permute-done.10), channel_id=1, source_target_pairs={{0,32},{32,64},{64,96},{96,128},{128,160},{160,192},{192,224},{224... | collective-permute-start | bytes 307208 | tf_op jit(solution)/shard_map/ppermute | solution.py:217
  31.4 29.1 %copy-start.5 = (bf16[80,3200]{1,0:T(8,128)(2,1)}, bf16[80,3200]{1,0:T(8,128)(2,1)S(1)}, u32[]{:S(2)}) copy-start(bf16[80,3200]{1,0:T(8,128)(2,1)S(1)} %constant_dynamic-update-slice_fusion.refs_0_) | copy-start | bytes 1536004
  31.4 10.1 %collective-permute-start.15 = (bf16[80,3200]{1,0:T(8,128)(2,1)S(1)}, bf16[80,3200]{1,0:T(8,128)(2,1)S(1)}, u32[]{:S(2)}, u32[]{:S(2)}) collective-permute-start(bf16[80,3200]{1,0:T(8,128)(2,1)S(1)} %constant_dynamic-update-slice_fusion.refs_0_), channel_id=1, source_target_pairs={{0,4},{4,8},{8,12},{12,0},{16,20},{20,24},{24,28},{28,16},{1,5},{5... | collective-permute-start | bytes 1536008 | tf_op jit(solution)/shard_map/ppermute | solution.py:221
  32.1 12.7 %collective-permute-start.17 = (bf16[80,3200]{1,0:T(8,128)(2,1)S(1)}, bf16[80,3200]{1,0:T(8,128)(2,1)S(1)}, u32[]{:S(2)}, u32[]{:S(2)}) collective-permute-start(bf16[80,3200]{1,0:T(8,128)(2,1)S(1)} %constant_dynamic-update-slice_fusion.refs_0_), channel_id=1, source_target_pairs={{0,12},{4,0},{8,4},{12,8},{16,28},{20,16},{24,20},{28,24},{1,13},{... | collective-permute-start | bytes 1536008 | tf_op jit(solution)/shard_map/ppermute | solution.py:221
  34.2 10.5 %copy-start.13 = (bf16[64,1920]{1,0:T(8,128)(2,1)}, bf16[64,1920]{1,0:T(8,128)(2,1)S(1)}, u32[]{:S(2)}) copy-start(bf16[64,1920]{1,0:T(8,128)(2,1)S(1)} %collective-permute-done.13.refs_3_) | copy-start | bytes 737284
  34.2 5.8 %collective-permute-start.14 = (bf16[64,1920]{1,0:T(8,128)(2,1)S(1)}, bf16[64,1920]{1,0:T(8,128)(2,1)S(1)}, u32[]{:S(2)}, u32[]{:S(2)}) collective-permute-start(bf16[64,1920]{1,0:T(8,128)(2,1)S(1)} %collective-permute-done.9.refs_2_), channel_id=1, source_target_pairs={{0,224},{32,0},{64,32},{96,64},{128,96},{160,128},{192,160},{224,1... | collective-permute-start | bytes 737288 | tf_op jit(solution)/shard_map/ppermute | solution.py:217
  36.9 7.8 %collective-permute-start.21 = (bf16[64,1920]{1,0:T(8,128)(2,1)S(1)}, bf16[64,1920]{1,0:T(8,128)(2,1)S(1)}, u32[]{:S(2)}, u32[]{:S(2)}) collective-permute-start(bf16[64,1920]{1,0:T(8,128)(2,1)S(1)} %collective-permute-done.13.refs_3_), channel_id=1, source_target_pairs={{0,32},{32,64},{64,96},{96,128},{128,160},{160,192},{192,224},{224... | collective-permute-start | bytes 737288 | tf_op jit(solution)/shard_map/ppermute | solution.py:217
  37.6 23.1 %copy-start.2 = (bf16[48,3200]{1,0:T(8,128)(2,1)}, bf16[48,3200]{1,0:T(8,128)(2,1)S(1)}, u32[]{:S(2)}) copy-start(bf16[48,3200]{1,0:T(8,128)(2,1)S(1)} %pad_maximum_fusion.refs_1_) | copy-start | bytes 921604
  40.0 11.3 %copy-start.14 = (bf16[64,1920]{1,0:T(8,128)(2,1)}, bf16[64,1920]{1,0:T(8,128)(2,1)S(1)}, u32[]{:S(2)}) copy-start(bf16[64,1920]{1,0:T(8,128)(2,1)S(1)} %collective-permute-done.14.refs_4_) | copy-start | bytes 737284
  40.0 9.1 %collective-permute-start.18 = (bf16[48,3200]{1,0:T(8,128)(2,1)S(1)}, bf16[48,3200]{1,0:T(8,128)(2,1)S(1)}, u32[]{:S(2)}, u32[]{:S(2)}) collective-permute-start(bf16[48,3200]{1,0:T(8,128)(2,1)S(1)} %pad_maximum_fusion.refs_1_), channel_id=1, source_target_pairs={{0,12},{4,0},{8,4},{12,8},{16,28},{20,16},{24,20},{28,24},{1,13},{... | collective-permute-start | bytes 921608 | tf_op jit(solution)/shard_map/ppermute | solution.py:221
  40.7 10.7 %collective-permute-start.16 = (bf16[48,3200]{1,0:T(8,128)(2,1)S(1)}, bf16[48,3200]{1,0:T(8,128)(2,1)S(1)}, u32[]{:S(2)}, u32[]{:S(2)}) collective-permute-start(bf16[48,3200]{1,0:T(8,128)(2,1)S(1)} %pad_maximum_fusion.refs_1_), channel_id=1, source_target_pairs={{0,4},{4,8},{8,12},{12,0},{16,20},{20,24},{24,28},{28,16},{1,5},{5... | collective-permute-start | bytes 921608 | tf_op jit(solution)/shard_map/ppermute | solution.py:221
  41.5 19.2 %copy-start.1 = (bf16[80,3200]{1,0:T(8,128)(2,1)}, bf16[80,3200]{1,0:T(8,128)(2,1)S(1)}, u32[]{:S(2)}) copy-start(bf16[80,3200]{1,0:T(8,128)(2,1)S(1)} %collective-permute-done.15.refs_2_) | copy-start | bytes 1536004
  41.5 9.7 %collective-permute-start.22 = (bf16[64,1920]{1,0:T(8,128)(2,1)S(1)}, bf16[64,1920]{1,0:T(8,128)(2,1)S(1)}, u32[]{:S(2)}, u32[]{:S(2)}) collective-permute-start(bf16[64,1920]{1,0:T(8,128)(2,1)S(1)} %collective-permute-done.14.refs_4_), channel_id=1, source_target_pairs={{0,224},{32,0},{64,32},{96,64},{128,96},{160,128},{192,160},{224,1... | collective-permute-start | bytes 737288 | tf_op jit(solution)/shard_map/ppermute | solution.py:217
  44.7 7.4 %copy-start.15 = (bf16[64,1920]{1,0:T(8,128)(2,1)}, bf16[64,1920]{1,0:T(8,128)(2,1)S(1)}, u32[]{:S(2)}) copy-start(bf16[64,1920]{1,0:T(8,128)(2,1)S(1)} %collective-permute-done.21.refs_5_) | copy-start | bytes 737284
  44.7 8.8 %collective-permute-start.25 = (bf16[64,1920]{1,0:T(8,128)(2,1)S(1)}, bf16[64,1920]{1,0:T(8,128)(2,1)}, u32[]{:S(2)}, u32[]{:S(2)}) collective-permute-start(bf16[64,1920]{1,0:T(8,128)(2,1)S(1)} %collective-permute-done.21.refs_5_), channel_id=1, source_target_pairs={{0,32},{32,64},{64,96},{96,128},{128,160},{160,192},{192,224},{224... | collective-permute-start | bytes 737288 | tf_op jit(solution)/shard_map/ppermute | solution.py:217
  44.8 15.8 %copy-start.3 = (bf16[80,3200]{1,0:T(8,128)(2,1)}, bf16[80,3200]{1,0:T(8,128)(2,1)S(1)}, u32[]{:S(2)}) copy-start(bf16[80,3200]{1,0:T(8,128)(2,1)S(1)} %collective-permute-done.17.refs_4_) | copy-start | bytes 1536004
  44.8 15.8 %collective-permute-start.19 = (bf16[48,3200]{1,0:T(8,128)(2,1)S(1)}, bf16[48,3200]{1,0:T(8,128)(2,1)S(1)}, u32[]{:S(2)}, u32[]{:S(2)}) collective-permute-start(bf16[48,3200]{1,0:T(8,128)(2,1)S(1)} %slice.26), channel_id=1, source_target_pairs={{0,4},{4,8},{8,12},{12,0},{16,20},{20,24},{24,28},{28,16},{1,5},{5... | collective-permute-start | bytes 921608 | tf_op jit(solution)/shard_map/ppermute | solution.py:221
  49.1 11.6 %copy-start.4 = (bf16[48,3200]{1,0:T(8,128)(2,1)}, bf16[48,3200]{1,0:T(8,128)(2,1)S(1)}, u32[]{:S(2)}) copy-start(bf16[48,3200]{1,0:T(8,128)(2,1)S(1)} %collective-permute-done.18.refs_5_) | copy-start | bytes 921604
  49.1 11.5 %collective-permute-start.20 = (bf16[32,3200]{1,0:T(8,128)(2,1)S(1)}, bf16[32,3200]{1,0:T(8,128)(2,1)S(1)}, u32[]{:S(2)}, u32[]{:S(2)}) collective-permute-start(bf16[32,3200]{1,0:T(8,128)(2,1)S(1)} %slice.27), channel_id=1, source_target_pairs={{0,12},{4,0},{8,4},{12,8},{16,28},{20,16},{24,20},{28,24},{1,13},{... | collective-permute-start | bytes 614408 | tf_op jit(solution)/shard_map/ppermute | solution.py:221
  51.2 2.3 %copy-start.16 = (bf16[64,1920]{1,0:T(8,128)(2,1)}, bf16[64,1920]{1,0:T(8,128)(2,1)S(1)}, u32[]{:S(2)}) copy-start(bf16[64,1920]{1,0:T(8,128)(2,1)S(1)} %collective-permute-done.22.refs_6_) | copy-start | bytes 737284
  51.2 9.4 %collective-permute-start.24 = (bf16[32,3200]{1,0:T(8,128)(2,1)S(1)}, bf16[32,3200]{1,0:T(8,128)(2,1)}, u32[]{:S(2)}, u32[]{:S(2)}) collective-permute-start(bf16[32,3200]{1,0:T(8,128)(2,1)S(1)} %slice.29), channel_id=1, source_target_pairs={{0,12},{4,0},{8,4},{12,8},{16,28},{20,16},{24,20},{28,24},{1,13},{... | collective-permute-start | bytes 614408 | tf_op jit(solution)/shard_map/ppermute | solution.py:221
  51.3 9.3 %copy-start.6 = (bf16[48,3200]{1,0:T(8,128)(2,1)}, bf16[48,3200]{1,0:T(8,128)(2,1)S(1)}, u32[]{:S(2)}) copy-start(bf16[48,3200]{1,0:T(8,128)(2,1)S(1)} %collective-permute-done.16.refs_3_) | copy-start | bytes 921604
  52.1 8.5 %collective-permute-start.23 = (bf16[16,3200]{1,0:T(8,128)(2,1)}, bf16[16,3200]{1,0:T(8,128)(2,1)S(1)}, u32[]{:S(2)}, u32[]{:S(2)}) collective-permute-start(bf16[16,3200]{1,0:T(8,128)(2,1)} %slice.28), channel_id=1, source_target_pairs={{0,4},{4,8},{8,12},{12,0},{16,20},{20,24},{24,28},{28,16},{1,5},{5... | collective-permute-start | bytes 307208 | tf_op jit(solution)/shard_map/ppermute | solution.py:221
  60.6 0.7 copy-start.9
  60.6 0.7 copy-start.10
  60.6 0.8 copy-start.7
  65.9 8.5 %collective-permute-start.26 = (f32[5,128,128]{2,1,0:T(8,128)}, f32[5,128,128]{2,1,0:T(8,128)S(1)}, u32[]{:S(2)}, u32[]{:S(2)}) collective-permute-start(f32[5,128,128]{2,1,0:T(8,128)} %get-tuple-element.39), channel_id=1, source_target_pairs={{0,1},{1,0},{2,3},{3,2},{4,5},{5,4},{6,7},{7,6},{8,9},{9,8},{10,11... | collective-permute-start | bytes 983048 | tf_op jit(solution)/shard_map/ppermute | solution.py:505
  75.4 9.8 %collective-permute-start.27 = (f32[5,128,128]{2,1,0:T(8,128)S(1)}, f32[5,128,128]{2,1,0:T(8,128)S(1)}, u32[]{:S(2)}, u32[]{:S(2)}) collective-permute-start(f32[5,128,128]{2,1,0:T(8,128)S(1)} %add.11), channel_id=1, source_target_pairs={{0,2},{2,0},{1,3},{3,1},{4,6},{6,4},{5,7},{7,5},{8,10},{10,8},{9,1... | collective-permute-start | bytes 983048 | tf_op jit(solution)/shard_map/ppermute | solution.py:509
  84.5 2.5 %collective-permute-start.30 = (f32[512,256]{1,0:T(8,128)}, f32[512,256]{1,0:T(8,128)S(1)}, u32[]{:S(2)}, u32[]{:S(2)}) collective-permute-start(f32[512,256]{1,0:T(8,128)} %get-tuple-element.58), channel_id=1, source_target_pairs={{0,1},{1,0},{2,3},{3,2},{4,5},{5,4},{6,7},{7,6},{8,9},{9,8},{10,11... | collective-permute-start | bytes 1572872 | tf_op jit(solution)/shard_map/ppermute | solution.py:505
  85.3 3.1 %collective-permute-start.28 = (f32[5,128,128]{2,1,0:T(8,128)S(1)}, f32[5,128,128]{2,1,0:T(8,128)S(1)}, u32[]{:S(2)}, u32[]{:S(2)}) collective-permute-start(f32[5,128,128]{2,1,0:T(8,128)S(1)} %add.12.mine_ref), channel_id=1, source_target_pairs={{0,1},{1,0},{2,3},{3,2},{4,5},{5,4},{6,7},{7,6},{8,9},{9,8},{10,11... | collective-permute-start | bytes 983048 | tf_op jit(solution)/shard_map/ppermute | solution.py:505
  85.8 16.2 %collective-permute-start.29 = (f32[512,256]{1,0:T(8,128)}, f32[512,256]{1,0:T(8,128)S(1)}, u32[]{:S(2)}, u32[]{:S(2)}) collective-permute-start(f32[512,256]{1,0:T(8,128)} %get-tuple-element.56), channel_id=1, source_target_pairs={{0,1},{1,0},{2,3},{3,2},{4,5},{5,4},{6,7},{7,6},{8,9},{9,8},{10,11... | collective-permute-start | bytes 1572872 | tf_op jit(solution)/shard_map/ppermute | solution.py:505
  88.1 13.9 %copy-start = (f32[512,256]{1,0:T(8,128)S(1)}, f32[512,256]{1,0:T(8,128)}, u32[]{:S(2)}) copy-start(f32[512,256]{1,0:T(8,128)} %get-tuple-element.52.keep_ref) | copy-start | bytes 1572868
  88.1 13.9 %collective-permute-start.31 = (f32[512,256]{1,0:T(8,128)S(1)}, f32[512,256]{1,0:T(8,128)S(1)}, u32[]{:S(2)}, u32[]{:S(2)}) collective-permute-start(f32[512,256]{1,0:T(8,128)S(1)} %add.13), channel_id=1, source_target_pairs={{0,2},{2,0},{1,3},{3,1},{4,6},{6,4},{5,7},{7,5},{8,10},{10,8},{9,1... | collective-permute-start | bytes 1572872 | tf_op jit(solution)/shard_map/ppermute | solution.py:509
